TPU v7x, 32 devices: a whole 2x2x4 slice. The times are simulated.
32 devices in a mesh: region: 8 (over z, y), rep: 4 (over x, core).
Axes of the slice: x: 2, y: 2, z: 4, core: 2. Of those that a mesh axis runs over, the one named last changes fastest.
Arguments:
- unit_cost: float32 [16, 131072], P(None, ('region', 'rep')), may hold values from -6 to 6
- start_primal: float32 [16, 131072], P(None, ('region', 'rep')), may hold values from 0 to 0.125
- start_dual: float32 [65536], P('region'), may hold values from 0 to 1
- quota_bound: float32 [65536], P('region'), may hold values from 2 to 6
- person_slot: int32 [131072], P(('region', 'rep')), may hold values from 0 to 1023
- cell_lists: int32 [8, 8, 128], P('region'), may hold values from 0 to 511
Outputs:
- primal: float32 [16, 131072], P(None, ('region', 'rep'))
- dual: float32 [65536], P('region')
Inputs may be any that keep to these rules, and one draw needn't show every extreme that they name: person_slot = d * 128 + j names slot j of the person's region's list toward owner block d.
All inputs are finite; a program needn't handle non-finite values.
Results may differ from a plain program's by a relative error of at most 0.0003.
Values sent between devices are 32-bit elements; how exact they have to be, the bound alone decides.
No kernel may reach another device: no remote copies, remote signals or barrier semaphores. Data moves between devices by JAX's collectives and lax.ppermute only.
A program may use at most 64 MiB of HBM per device.

v0:
```python
import jax
import jax.numpy as jnp
from jax import lax
from jax.sharding import PartitionSpec as P

ITERS = 2
BISECT = 30


PRIMAL_STEP = 0.5
DUAL_STEP = 0.25


def project_simplex(values):
    largest = jnp.max(values, axis=0)

    def bisect_once(repeat, bounds):
        low_end, high_end = bounds
        middle = 0.5 * (low_end + high_end)
        mass_sum = jnp.sum(jnp.maximum(values - middle, 0.0), axis=0)
        above = mass_sum > 1.0
        return (jnp.where(above, middle, low_end), jnp.where(above, high_end, middle))

    low_end, high_end = lax.fori_loop(0, BISECT, bisect_once, (largest - 1.0, largest))
    middle = 0.5 * (low_end + high_end)
    return jnp.maximum(values - middle, 0.0)


def local(unit_cost, start_primal, start_dual, quota_bound, person_slot, cell_lists):
    options = unit_cost.shape[0]
    regions = lax.axis_size("region")
    list_len = cell_lists.shape[2]
    groups = quota_bound.shape[0] // options
    slot_count = regions * list_len
    own_lists = cell_lists[0]
    primal = start_primal
    dual = start_dual
    for repeat in range(ITERS):
        dual_rows = dual.reshape(groups, options)
        picked = jnp.take(dual_rows, own_lists.reshape(-1), axis=0).reshape(
            regions, list_len * options
        )
        slot_arrived = lax.all_to_all(picked, "region", split_axis=0, concat_axis=0, tiled=True)
        prices = slot_arrived.reshape(slot_count, options)
        adjoint = jnp.take(prices, person_slot, axis=0).T
        fresh = project_simplex(primal - PRIMAL_STEP * (unit_cost + adjoint))
        partial_rows = jax.ops.segment_sum(
            (2.0 * fresh - primal).T, person_slot, num_segments=slot_count
        )
        partial_rows = partial_rows.reshape(regions, list_len * options)
        summed = lax.psum(partial_rows, "rep")
        arrived = lax.all_to_all(summed, "region", split_axis=0, concat_axis=0, tiled=True)
        block_sum = jax.ops.segment_sum(
            arrived.reshape(slot_count, options), own_lists.reshape(-1), num_segments=groups
        )
        applied = block_sum.reshape(-1)
        dual = jnp.maximum(dual + DUAL_STEP * (applied - quota_bound), 0.0)
        primal = fresh
    return (primal, dual)


def solution(mesh):
    placed = (
        P(None, ("region", "rep")),
        P(None, ("region", "rep")),
        P("region"),
        P("region"),
        P(("region", "rep")),
        P("region", None, None),
    )
    return jax.shard_map(
        local,
        mesh=mesh,
        in_specs=placed,
        out_specs=(P(None, ("region", "rep")), P("region")),
        check_vma=False,
    )
```

profile of v0, /device:TPU:0, one launch (start us, length us, event | category | flops | bytes accessed | tf_op | source)
XLA Modules:
  0.0 246.2 jit_solution(10379357901981070034)
XLA Ops:
  7.2 0.7 compare_and_fusion.1
  7.9 0.7 fusion.29
  8.6 0.9 reshape.64
  9.5 2.8 %gather_fusion = f32[1024,16]{1,0:T(8,128)S(1)} fusion(f32[512,16]{1,0:T(8,128)S(1)} %reshape.64, s32[1024]{0:T(1024)S(1)} %fusion.29), kind=kCustom, calls=%fused_computation.clone | custom fusion | bytes 135168 | tf_op jit(solution)/shard_map/jit(_take)/gather | solution.py:40
  12.3 0.2 broadcast_select_fusion.1
  12.5 0.9 all_to_all.32
  13.4 7.3 %all-to-all-start = ((f32[8,1,2048]{2,1,0:T(1,128)}), f32[8,1,2048]{2,1,0:T(1,128)S(1)}, u32[]{:S(2)}, u32[]{:S(2)}) async-start(f32[8,1,2048]{2,1,0:T(1,128)} %all_to_all.32), calls=%async_computation | async-start | bytes 131072 | tf_op jit(solution)/shard_map/all_to_all | solution.py:43
  20.7 2.0 copy.23
  22.7 1.9 copy.24
  24.6 2.9 %all-to-all-done = f32[8,1,2048]{2,1,0:T(1,128)S(1)} async-done(((f32[8,1,2048]{2,1,0:T(1,128)}), f32[8,1,2048]{2,1,0:T(1,128)S(1)}, u32[]{:S(2)}, u32[]{:S(2)}) %all-to-all-start) | async-done | bytes 65568 | tf_op jit(solution)/shard_map/all_to_all | solution.py:43
  27.5 0.2 reduce
  27.7 0.2 reshape.65
  27.9 14.1 %gather_fusion.1 = f32[4096,16]{1,0:T(8,128)} fusion(f32[1024,16]{1,0:T(8,128)S(1)} %reshape.65, s32[4096]{0:T(1024)S(1)} %fusion.28), kind=kCustom, calls=%fused_computation.1.clone | custom fusion | bytes 540672 | tf_op jit(solution)/shard_map/jit(_take)/gather | solution.py:45
  42.0 3.5 %fusion.32 = (f32[4096]{0:T(1024)S(1)}, f32[16,4096]{0,1:T(8,128)S(1)}) fusion(f32[16,4096]{0,1:T(8,128)} %copy.24, f32[16,4096]{0,1:T(8,128)} %copy.23, f32[4096,16]{1,0:T(8,128)} %gather_fusion.1, pred[4096]{0:T(1024)(128)(4,1)S(1)} %compare_and_fusion), kind=kLoop, calls=%fused_computation.61 | loop fusion | flops 323584 | bytes 1069056 | tf_op jit(solution)/shard_map/reduce_max | solution.py:15
  45.5 0.6 copy.25
  46.0 4.1 %while.24 = (s32[]{:T(128)}, f32[4096]{0:T(1024)S(1)}, f32[4096]{0:T(1024)S(1)}, f32[16,4096]{1,0:T(8,128)S(1)}, s32[]{:T(128)}) while((s32[]{:T(128)}, f32[4096]{0:T(1024)S(1)}, f32[4096]{0:T(1024)S(1)}, f32[16,4096]{1,0:T(8,128)S(1)}, s32[]{:T(128)}) %tuple.54), condition=%wide.region_3.6_spmd, body=%wide.region_1.0_spmd.sunk | while | flops 229378 | bytes 499773 | solution.py:24
  50.1 24.9 %scatter_custom_fusion = f32[1024,16]{1,0:T(8,128)S(1)} fusion(s32[4096]{0:T(1024)S(1)} %copy-done.4, f32[16,4096]{0,1:T(8,128)} %copy.24, f32[16,4096]{0,1:T(8,128)S(1)} %get-tuple-element.107, f32[]{:T(128)} %constant.48.clone.1, f32[]{:T(128)} %constant.47.clone.1, f32[4096]{0:T(1024)S(1)} %add_multiply_fusion.3), kind=kCustom, calls=%fused_computation.23 | custom fusion | flops 327680 | bytes 4277760 | tf_op jit(solution)/shard_map/scatter-add | solution.py:47
  75.1 0.9 all_to_all.26
  76.1 29.6 %all-reduce.3.cloned.1.call-done = f32[8,1,2048]{2,0,1:T(8,128)} async-done(((f32[8,1,2048]{2,0,1:T(8,128)}), f32[8,1,2048]{2,0,1:T(8,128)}) %all-reduce.3.cloned.1.call-update) | async-done | bytes 65552 | tf_op jit(solution)/shard_map/psum | solution.py:51
  105.7 0.9 copy.27
  106.6 12.2 %all_to_all.38 = f32[8,1,2048]{2,1,0:T(1,128)S(1)} all-to-all(f32[8,1,2048]{2,1,0:T(1,128)S(1)} %copy.27), channel_id=1, replica_groups=mesh['region'=8,'rep'=4] {'region'}, dimensions={0} | all-to-all | bytes 131072 | tf_op jit(solution)/shard_map/all_to_all | solution.py:52
  118.8 0.2 reduce.1
  119.0 0.2 reshape.120
  119.2 6.2 %scatter_custom_fusion.1 = f32[512,16]{1,0:T(8,128)S(1)} fusion(s32[1024]{0:T(1024)} %bitcast.23, f32[1024,16]{1,0:T(8,128)S(1)} %reshape.120, f32[]{:T(128)} %constant.47.clone.1), kind=kCustom, calls=%fused_computation.46 | custom fusion | flops 16384 | bytes 33280 | tf_op jit(solution)/shard_map/scatter-add | solution.py:53
  125.4 0.1 reshape.68
  125.7 2.8 %gather_fusion.2 = f32[1024,16]{1,0:T(8,128)S(1)} fusion(f32[512,16]{1,0:T(8,128)S(1)} %reshape.69, s32[1024]{0:T(1024)S(1)} %fusion.29), kind=kCustom, calls=%fused_computation.2.clone | custom fusion | bytes 135168 | tf_op jit(solution)/shard_map/jit(_take)/gather | solution.py:40
  128.5 0.2 broadcast_select_fusion
  128.7 0.2 all_to_all.33
  128.9 9.3 %all_to_all.39 = f32[8,1,2048]{2,1,0:T(1,128)S(1)} all-to-all(f32[8,1,2048]{2,1,0:T(1,128)S(1)} %all_to_all.33), channel_id=1, replica_groups=mesh['region'=8,'rep'=4] {'region'}, dimensions={0} | all-to-all | bytes 131072 | tf_op jit(solution)/shard_map/all_to_all | solution.py:43
  138.2 0.2 reduce.2
  138.4 0.2 reshape.70
  138.6 14.1 %gather_fusion.3 = f32[4096,16]{1,0:T(8,128)} fusion(f32[1024,16]{1,0:T(8,128)S(1)} %reshape.70, s32[4096]{0:T(1024)S(1)} %fusion.28), kind=kCustom, calls=%fused_computation.3.clone | custom fusion | bytes 540672 | tf_op jit(solution)/shard_map/jit(_take)/gather | solution.py:45
  152.7 4.9 %fusion.30 = (f32[4096]{0:T(1024)S(1)}, f32[16,4096]{0,1:T(8,128)}) fusion(f32[16,4096]{0,1:T(8,128)} %copy.23, f32[4096,16]{1,0:T(8,128)} %gather_fusion.3, pred[4096]{0:T(1024)(128)(4,1)S(1)} %compare_and_fusion, f32[16,4096]{0,1:T(8,128)S(1)} %get-tuple-element.107, f32[4096]{0:T(1024)S(1)} %add_multiply_fusion.3), kind=kLoop, calls=%fused_computation.60 | loop fusion | flops 454656 | bytes 1085440 | tf_op jit(solution)/shard_map/reduce_max | solution.py:15
  157.6 2.2 copy.30
  159.7 4.1 %while.25 = (s32[]{:T(128)}, f32[4096]{0:T(1024)S(1)}, f32[4096]{0:T(1024)S(1)}, f32[16,4096]{1,0:T(8,128)S(1)}, s32[]{:T(128)}) while((s32[]{:T(128)}, f32[4096]{0:T(1024)S(1)}, f32[4096]{0:T(1024)S(1)}, f32[16,4096]{1,0:T(8,128)S(1)}, s32[]{:T(128)}) %tuple.57), condition=%wide.region_10.13_spmd, body=%wide.region_8.12_spmd.sunk | while | flops 229378 | bytes 499773 | solution.py:24
  163.8 25.5 %scatter_custom_fusion.2 = f32[1024,16]{1,0:T(8,128)S(1)} fusion(s32[4096]{0:T(1024)S(1)} %copy-done.4, f32[16,4096]{0,1:T(8,128)S(1)} %get-tuple-element.107, f32[]{:T(128)} %constant.48.clone.1, f32[]{:T(128)} %constant.47.clone.1, f32[4096]{0:T(1024)S(1)} %add_multiply_fusion.3, f32[16,4096]{0,1:T(8,128)} %get-tuple-element.105, ...), kind=kCustom, calls=%fused_computation.18 | custom fusion | flops 458752 | bytes 4294144 | tf_op jit(solution)/shard_map/scatter-add | solution.py:47
  189.4 0.9 all_to_all.30
  190.3 27.8 %all-reduce.5.cloned.1.call-done = f32[8,1,2048]{2,0,1:T(8,128)} async-done(((f32[8,1,2048]{2,0,1:T(8,128)}), f32[8,1,2048]{2,0,1:T(8,128)}) %all-reduce.5.cloned.1.call-update) | async-done | bytes 65552 | tf_op jit(solution)/shard_map/psum | solution.py:51
  218.1 1.5 copy.31
  219.6 5.5 %all-to-all-start.3 = ((f32[8,1,2048]{2,1,0:T(1,128)}), f32[8,1,2048]{2,1,0:T(1,128)S(1)}, u32[]{:S(2)}, u32[]{:S(2)}) async-start(f32[8,1,2048]{2,1,0:T(1,128)} %copy.31), calls=%async_computation.3 | async-start | bytes 131072 | tf_op jit(solution)/shard_map/all_to_all | solution.py:52
  225.1 1.9 subtract_maximum_fusion
  227.0 1.3 copy.32
  228.3 3.7 %all-to-all-done.3 = f32[8,1,2048]{2,1,0:T(1,128)S(1)} async-done(((f32[8,1,2048]{2,1,0:T(1,128)}), f32[8,1,2048]{2,1,0:T(1,128)S(1)}, u32[]{:S(2)}, u32[]{:S(2)}) %all-to-all-start.3) | async-done | bytes 65568 | tf_op jit(solution)/shard_map/all_to_all | solution.py:52
  232.0 0.2 reduce.3
  232.2 0.2 reshape.136
  232.4 6.2 %scatter_custom_fusion.3 = f32[512,16]{1,0:T(8,128)S(1)} fusion(s32[1024]{0:T(1024)} %bitcast.24, f32[1024,16]{1,0:T(8,128)S(1)} %reshape.136, f32[]{:T(128)} %constant.47.clone.1), kind=kCustom, calls=%fused_computation.44 | custom fusion | flops 16384 | bytes 33280 | tf_op jit(solution)/shard_map/scatter-add | solution.py:53
  238.6 0.1 reshape.73
  238.7 0.6 add_maximum_fusion
  (322 shorter events, 5.4 us)
Async XLA Ops:
  9.4 11.3 %copy-start.4 = (s32[4096]{0:T(1024)S(1)}, s32[4096]{0:T(1024)}, u32[]{:S(2)}) copy-start(s32[4096]{0:T(1024)} %param.18) | copy-start | bytes 49156
  9.4 11.3 %copy-start = (f32[16,4096]{1,0:T(8,128)S(1)}, f32[16,4096]{1,0:T(8,128)}, u32[]{:S(2)}) copy-start(f32[16,4096]{1,0:T(8,128)} %param.14) | copy-start | bytes 786436
  12.3 10.4 %copy-start.1 = (f32[16,4096]{1,0:T(8,128)S(1)}, f32[16,4096]{1,0:T(8,128)}, u32[]{:S(2)}) copy-start(f32[16,4096]{1,0:T(8,128)} %param.15) | copy-start | bytes 786436
  13.4 14.2 %all-to-all-start = ((f32[8,1,2048]{2,1,0:T(1,128)}), f32[8,1,2048]{2,1,0:T(1,128)S(1)}, u32[]{:S(2)}, u32[]{:S(2)}) async-start(f32[8,1,2048]{2,1,0:T(1,128)} %all_to_all.32), calls=%async_computation | async-start | bytes 131072 | tf_op jit(solution)/shard_map/all_to_all | solution.py:43
  20.6 85.0 %all-reduce.3.cloned.1.call-start = ((), (), s32[]{:S(2)}) async-start(), calls=%async_computation.4 | async-start | bytes 131072 | tf_op jit(solution)/shard_map/psum | solution.py:51
  75.1 50.4 %copy-start.2 = (f32[8192]{0:T(1024)S(1)}, f32[8192]{0:T(1024)}, u32[]{:S(2)}) copy-start(f32[8192]{0:T(1024)} %param.16) | copy-start | bytes 98308
  75.1 50.4 %copy-start.3 = (f32[8192]{0:T(1024)S(1)}, f32[8192]{0:T(1024)}, u32[]{:S(2)}) copy-start(f32[8192]{0:T(1024)} %param.17) | copy-start | bytes 98308
  76.0 142.0 %all-reduce.5.cloned.1.call-start = ((), (), s32[]{:S(2)}) async-start(), calls=%async_computation.5 | async-start | bytes 131072 | tf_op jit(solution)/shard_map/psum | solution.py:51
  219.6 12.4 %all-to-all-start.3 = ((f32[8,1,2048]{2,1,0:T(1,128)}), f32[8,1,2048]{2,1,0:T(1,128)S(1)}, u32[]{:S(2)}, u32[]{:S(2)}) async-start(f32[8,1,2048]{2,1,0:T(1,128)} %copy.31), calls=%async_computation.3 | async-start | bytes 131072 | tf_op jit(solution)/shard_map/all_to_all | solution.py:52
Sparse Core Ops, SparseCore 0:
  76.2 29.4 all-reduce.2
  190.4 27.6 all-reduce.4
where the time goes:
time: 247 us; the launch traced here: 246 us
  other arithmetic  81.1 us (33%)
  waiting for transfers between devices  64 us (26%)
  local copies, waits for them, and re-layouts  49.3 us (20%)
  blocking collectives  21.5 us (9%)
  between operations  14.3 us (6%)
  starting transfers between devices  12.9 us (5%)
  loops' own time  3.07 us (1%)
    psum x2, waiting for transfers between devices, local(): summed = lax.psum(partial_rows, 'rep')  57.4 us
    scatter-add x2, other arithmetic, local(): jax.ops.segment_sum((2.0 * fresh - primal).T, person_slot, num_segments=s...  50.5 us
    gather x2, local copies, waits for them, and re-layouts, local(): adjoint = jnp.take(prices, person_slot, axis=0).T  28.2 us
    scatter-add x2, other arithmetic, local(): jax.ops.segment_sum(arrived.reshape(slot_count, options), own_lists.resha...  12.4 us
    all_to_all x1, blocking collectives, local(): lax.all_to_all(summed, 'region', split_axis=0, concat_axis=0, tiled=True)  12.2 us
    all_to_all x1, blocking collectives, local(): lax.all_to_all(picked, 'region', split_axis=0, concat_axis=0, tiled=True)  9.29 us
    reduce_max x2, other arithmetic, project_simplex(): largest = jnp.max(values, axis=0)  8.33 us
    all_to_all x1, starting transfers between devices, local(): lax.all_to_all(picked, 'region', split_axis=0, concat_axis=0, tiled=True)  7.28 us
  transfers between devices with their start and end apart: 4, of which 4 were waited for; matrix products, arithmetic and copies ran while one was open for 3% of the time, Pallas kernels for 0%

commit v1 on v0

v1 whole, which is shorter than its diff:
```python
import functools

import jax
import jax.numpy as jnp
from jax import lax
from jax.experimental import pallas as pl
from jax.experimental.pallas import tpu as pltpu
from jax.sharding import PartitionSpec as P

ITERS = 2
BISECT = 30
PRIMAL_STEP = 0.5
DUAL_STEP = 0.25
LANES = 128
SUBLANES = 8
CHUNK = 8


def sorting_network(count):
    pairs = []
    p = 1
    while p < count:
        k = p
        while k >= 1:
            for j in range(k % p, count - k, 2 * k):
                for i in range(min(k, count - j - k)):
                    if (i + j) // (2 * p) == (i + j + k) // (2 * p):
                        pairs.append((i + j, i + j + k))
            k //= 2
        p *= 2
    return pairs


def repeat_chunks(total, body, init):
    if total == 1:
        return body(0, init)
    return lax.fori_loop(0, total, body, init)


def simplex_theta(values):
    ranked = list(values)
    for a, b in sorting_network(len(values)):
        ranked[a], ranked[b] = jnp.maximum(ranked[a], ranked[b]), jnp.minimum(ranked[a], ranked[b])
    largest = ranked[0]
    total = jnp.zeros_like(largest)
    best = jnp.full_like(largest, -1.0)
    for k in range(1, len(values)):
        total = total + (ranked[k] - largest)
        best = jnp.maximum(best, (total - 1.0) * (1.0 / (k + 1)))
    cells = float(2**BISECT)
    step = jnp.maximum(jnp.ceil((best + 1.0) * cells), 1.0) - 0.5
    return (largest - 1.0) + step * (1.0 / cells)


def split_two(x):
    high = x.astype(jnp.bfloat16)
    low = (x - high.astype(jnp.float32)).astype(jnp.bfloat16)
    return high, low


def person_kernel(prices_ref, slot_ref, cost_ref, primal_ref, fresh_ref, sums_ref, x_ref, parts_ref, hot_ref):
    regions, options, _ = prices_ref.shape
    rep = sums_ref.shape[0] // regions
    rows = slot_ref.shape[0]
    halves = options // SUBLANES
    chunks = regions // CHUNK

    for g in range(rows // SUBLANES):
        slot = slot_ref[g * SUBLANES : (g + 1) * SUBLANES, :]
        owner = slot // LANES
        within = slot - owner * LANES

        def pick(chunk, found):
            found = list(found)
            for d in range(CHUNK):
                mine = owner == chunk * CHUNK + d
                for o in range(options):
                    table = jnp.broadcast_to(prices_ref[chunk * CHUNK + d, o : o + 1, :], (SUBLANES, LANES))
                    value = jnp.take_along_axis(table, within, axis=1)
                    found[o] = jnp.where(mine, value, found[o])
            return tuple(found)

        zero = jnp.zeros((SUBLANES, LANES), jnp.float32)
        adjoint = repeat_chunks(chunks, pick, (zero,) * options)
        places = []
        values = []
        for o in range(options):
            first = ((o // SUBLANES) * rows + g * SUBLANES) * SUBLANES + o % SUBLANES
            at = pl.ds(first, SUBLANES, stride=SUBLANES)
            places.append(at)
            values.append(primal_ref[at, :] - PRIMAL_STEP * (cost_ref[at, :] + adjoint[o]))
        theta = simplex_theta(values)
        for o in range(options):
            fresh = jnp.maximum(values[o] - theta, 0.0)
            fresh_ref[places[o], :] = fresh
            x_ref[places[o], :] = 2.0 * fresh - primal_ref[places[o], :]

    lane_rows = 2 * SUBLANES
    for c in range(rows):
        span = slice(c * LANES, (c + 1) * LANES)
        x = jnp.concatenate(
            [x_ref[(h * rows + c) * SUBLANES : (h * rows + c + 1) * SUBLANES, :] for h in range(halves)], axis=0
        )
        high, low = split_two(x)
        parts_ref[0:options, span] = high
        parts_ref[options : 2 * options, span] = low
        slot = jnp.broadcast_to(slot_ref[c : c + 1, :], (LANES, LANES))
        here = lax.broadcasted_iota(jnp.int32, (LANES, LANES), 0)
        hot_ref[:, span] = jnp.where((slot & (LANES - 1)) == here, 1.0, 0.0).astype(jnp.bfloat16)

    def add_up(chunk, carry):
        lines = []
        slot = jnp.concatenate([slot_ref[c : c + 1, :] for c in range(rows)], axis=1)
        owner = slot // LANES - chunk * CHUNK
        for part in range(2):
            x = parts_ref[part * options : (part + 1) * options, :]
            for d in range(CHUNK):
                mine = jnp.where(owner == d, 1.0, 0.0)
                mine = jnp.broadcast_to(mine, (options, rows * LANES)).astype(jnp.bfloat16)
                lines.append(x * mine)
        left = jnp.concatenate(lines, axis=0)
        total = lax.dot_general(
            left, hot_ref[...], (((1,), (1,)), ((), ())), preferred_element_type=jnp.float32
        )
        total = total[: CHUNK * options] + total[CHUNK * options :]
        for d in range(CHUNK):
            block = total[d * options : (d + 1) * options, :]
            for k in range(rep):
                sums_ref[(chunk * CHUNK + d) * rep + k] = block
        return carry

    repeat_chunks(chunks, add_up, 0)


def group_place(lists):
    return (lists & (SUBLANES - 1)), lists >> 3


def pick_rows(dual_blocks, lists_ref, picked_ref):
    regions = lists_ref.shape[0]
    options = picked_ref.shape[1]
    half = LANES // 2

    def one(r, carry):
        residue, column = group_place(lists_ref[pl.ds(r, 1), :])
        block = jnp.broadcast_to(residue >> 1, (options, LANES))
        lane = jnp.broadcast_to((residue & 1) * half + column, (options, LANES))
        found = jnp.zeros((options, LANES), jnp.float32)
        for b, table in enumerate(dual_blocks):
            found = jnp.where(block == b, jnp.take_along_axis(table, lane, axis=1), found)
        picked_ref[r] = found
        return carry

    if regions <= CHUNK:
        for r in range(regions):
            one(r, 0)
    else:
        lax.fori_loop(0, regions, one, 0)


def first_kernel(dual_ref, quota_ref, lists_ref, picked_ref, dual_rows_ref, quota_rows_ref):
    options = picked_ref.shape[1]
    half = LANES // 2
    both = jnp.concatenate([dual_ref[...], quota_ref[...]], axis=0).T
    left = lax.broadcasted_iota(jnp.int32, (options, LANES), 1) < half
    duals = []
    for b in range(SUBLANES // 2):
        even = both[2 * b * options : (2 * b + 1) * options, :]
        odd = both[(2 * b + 1) * options : (2 * b + 2) * options, :]
        dual = jnp.where(left, even, pltpu.roll(odd, half, 1))
        quota = jnp.where(left, pltpu.roll(even, half, 1), odd)
        dual_rows_ref[:, b * LANES : (b + 1) * LANES] = dual
        quota_rows_ref[:, b * LANES : (b + 1) * LANES] = quota
        duals.append(dual)
    pick_rows(duals, lists_ref, picked_ref)


def block_sums(arrived_ref, lists_ref, groups):
    regions = lists_ref.shape[0]
    rep = arrived_ref.shape[0] // regions
    options = arrived_ref.shape[1]
    half = groups // SUBLANES

    def add_up(chunk, total):
        highs, lows, hots = [], [], []
        here = lax.broadcasted_iota(jnp.int32, (groups, LANES), 0)
        for i in range(CHUNK):
            r = chunk * CHUNK + i
            x = arrived_ref[r * rep]
            for k in range(1, rep):
                x = x + arrived_ref[r * rep + k]
            high, low = split_two(x)
            highs.append(high)
            lows.append(low)
            residue, column = group_place(lists_ref[pl.ds(r, 1), :])
            place = jnp.broadcast_to(residue * half + column, (groups, LANES))
            hots.append(jnp.where(place == here, 1.0, 0.0).astype(jnp.bfloat16))
        left = jnp.concatenate([jnp.concatenate(highs, axis=1), jnp.concatenate(lows, axis=1)], axis=0)
        right = jnp.concatenate(hots, axis=1)
        product = lax.dot_general(left, right, (((1,), (1,)), ((), ())), preferred_element_type=jnp.float32)
        return total + product[:options] + product[options:]

    return repeat_chunks(regions // CHUNK, add_up, jnp.zeros((options, groups), jnp.float32))


def middle_kernel(arrived_ref, lists_ref, dual_rows_ref, quota_rows_ref, picked_ref, next_rows_ref):
    applied = block_sums(arrived_ref, lists_ref, dual_rows_ref.shape[1])
    dual = jnp.maximum(dual_rows_ref[...] + DUAL_STEP * (applied - quota_rows_ref[...]), 0.0)
    next_rows_ref[...] = dual
    pick_rows([dual[:, b * LANES : (b + 1) * LANES] for b in range(SUBLANES // 2)], lists_ref, picked_ref)


def last_kernel(arrived_ref, lists_ref, dual_rows_ref, quota_rows_ref, dual_ref):
    options = dual_rows_ref.shape[0]
    half = LANES // 2
    applied = block_sums(arrived_ref, lists_ref, dual_rows_ref.shape[1])
    dual = jnp.maximum(dual_rows_ref[...] + DUAL_STEP * (applied - quota_rows_ref[...]), 0.0)
    lines = []
    for b in range(SUBLANES // 2):
        block = dual[:, b * LANES : (b + 1) * LANES]
        lines.append(block)
        lines.append(pltpu.roll(block, half, 1))
    dual_ref[...] = jnp.concatenate(lines, axis=0).T[: dual_ref.shape[0], :]


def call(kernel, out_shape, scratch=()):
    return pl.pallas_call(
        kernel,
        out_shape=[jax.ShapeDtypeStruct(shape, jnp.float32) for shape in out_shape],
        scratch_shapes=list(scratch),
        compiler_params=pltpu.CompilerParams(vmem_limit_bytes=48 * 1024 * 1024),
    )


def local(unit_cost, start_primal, start_dual, quota_bound, person_slot, cell_lists):
    options, persons = unit_cost.shape
    regions = lax.axis_size("region")
    rep = lax.axis_size("rep")
    groups = quota_bound.shape[0] // options
    rows = persons // LANES
    halves = options // SUBLANES
    lists = cell_lists[0]
    slots = person_slot.reshape(rows, LANES)

    def to_tiles(x):
        x = x.reshape(halves, SUBLANES, rows, LANES).transpose(0, 2, 1, 3)
        return x.reshape(options * rows, LANES)

    def from_tiles(x):
        x = x.reshape(halves, rows, SUBLANES, LANES).transpose(0, 2, 1, 3)
        return x.reshape(options, persons)

    flat = (groups * options // LANES, LANES)
    row_shape = (options, groups)
    picked_shape = (regions, options, LANES)
    tile_shape = (options * rows, LANES)
    sums_shape = (regions * rep, options, LANES)
    scratch = (
        pltpu.VMEM(tile_shape, jnp.float32),
        pltpu.VMEM((2 * options, persons), jnp.bfloat16),
        pltpu.VMEM((LANES, persons), jnp.bfloat16),
    )
    persons_step = call(person_kernel, (tile_shape, sums_shape), scratch)

    picked, dual_rows, quota_rows = call(first_kernel, (picked_shape, row_shape, row_shape))(
        start_dual.reshape(flat), quota_bound.reshape(flat), lists
    )
    cost = to_tiles(unit_cost)
    primal = to_tiles(start_primal)
    for repeat in range(ITERS):
        prices = lax.all_to_all(picked, "region", split_axis=0, concat_axis=0, tiled=True)
        primal, sums = persons_step(prices, slots, cost, primal)
        arrived = lax.all_to_all(sums, ("region", "rep"), split_axis=0, concat_axis=0, tiled=True)
        if repeat + 1 < ITERS:
            picked, dual_rows = call(middle_kernel, (picked_shape, row_shape))(
                arrived, lists, dual_rows, quota_rows
            )
    (dual,) = call(last_kernel, (flat,))(arrived, lists, dual_rows, quota_rows)
    return (from_tiles(primal), dual.reshape(-1))


def solution(mesh):
    placed = (
        P(None, ("region", "rep")),
        P(None, ("region", "rep")),
        P("region"),
        P("region"),
        P(("region", "rep")),
        P("region", None, None),
    )
    return jax.shard_map(
        local,
        mesh=mesh,
        in_specs=placed,
        out_specs=(P(None, ("region", "rep")), P("region")),
        check_vma=False,
    )
```

time: 247 us -> 59.5 us (0.24)
  other arithmetic: 81.1 us -> 0 us
  waiting for transfers between devices: 64 us -> 0 us
  local copies, waits for them, and re-layouts: 49.3 us -> 4.1 us
  blocking collectives: 21.5 us -> 48.4 us
  between operations: 14.3 us -> 0.67 us
  starting transfers between devices: 12.9 us -> 0 us
  Pallas kernels: 0 us -> 5.79 us
  loops' own time: 3.07 us -> 0 us
    scatter-add x4 -> x0, other arithmetic: 62.9 us -> none  [the longest x2 50.5 us: local(): jax.ops.segment_sum((2.0 * fresh - primal).T, person_slot, num_segments=s...]
    psum x2 -> x0, waiting for transfers between devices: 57.4 us -> none  [local(): summed = lax.psum(partial_rows, 'rep')]
    gather x4 -> x0, local copies, waits for them, and re-layouts: 33.8 us -> none  [the longest x2 28.2 us: local(): adjoint = jnp.take(prices, person_slot, axis=0).T]
    all_to_all x1 -> x2, blocking collectives: 9.29 us -> 23.6 us  [local(): lax.all_to_all(picked, 'region', split_axis=0, concat_axis=0, tiled=True)]
    all_to_all x2 -> x0, starting transfers between devices: 12.8 us -> none  [the longest x1 7.28 us: local(): lax.all_to_all(picked, 'region', split_axis=0, concat_axis=0, tiled=True)]
    all_to_all x1 -> x2, blocking collectives: 12.2 us -> 24.8 us  [local(): lax.all_to_all(sums, ('region', 'rep'), split_axis=0, concat_axis=0, tile...]
    reduce_max x2 -> x0, other arithmetic: 8.33 us -> none  [project_simplex(): largest = jnp.max(values, axis=0)]
    all_to_all x2 -> x0, waiting for transfers between devices: 6.64 us -> none  [the longest x1 3.69 us: local(): lax.all_to_all(summed, 'region', split_axis=0, concat_axis=0, tiled=True)]
  transfers between devices with their start and end apart: 4 -> 0, of which waited for: 4 -> 0; matrix products, arithmetic and copies ran while one was open for 3% -> 0% of each run, Pallas kernels for 0% -> 0%
where the time goes in v1:
time: 59.5 us; the launch traced here: 59 us
  blocking collectives  48.4 us (81%)
  Pallas kernels  5.79 us (10%)
  local copies, waits for them, and re-layouts  4.1 us (7%)
  between operations  0.67 us (1%)
    all_to_all x2, blocking collectives, local(): lax.all_to_all(sums, ('region', 'rep'), split_axis=0, concat_axis=0, tile...  24.8 us
    all_to_all x2, blocking collectives, local(): lax.all_to_all(picked, 'region', split_axis=0, concat_axis=0, tiled=True)  23.6 us
    unnamed x14, local copies, waits for them, and re-layouts  4.1 us
    pallas_call x2, Pallas kernels, local(): primal, sums = persons_step(prices, slots, cost, primal)  3.63 us

profile of v1, /device:TPU:0, one launch (start us, length us, event | category | flops | bytes accessed | tf_op | source)
XLA Modules:
  0.0 59.0 jit_solution(483192292684887206)
XLA Ops:
  0.6 0.0 copy-start.4
  0.6 0.7 %copy-done.4 = s32[1,8,128]{2,1,0:T(8,128)S(1)} copy-done((s32[1,8,128]{2,1,0:T(8,128)S(1)}, s32[1,8,128]{2,1,0:T(8,128)}, u32[]{:S(2)}) %copy-start.4) | copy-done | bytes 4120
  1.3 0.0 copy-start.5
  1.3 0.8 %copy-done.5 = f32[8192]{0:T(1024)S(1)} copy-done((f32[8192]{0:T(1024)S(1)}, f32[8192]{0:T(1024)}, u32[]{:S(2)}) %copy-start.5) | copy-done | bytes 32792
  2.1 0.0 copy-start.6
  2.1 0.8 %copy-done.6 = f32[8192]{0:T(1024)S(1)} copy-done((f32[8192]{0:T(1024)S(1)}, f32[8192]{0:T(1024)}, u32[]{:S(2)}) %copy-start.6) | copy-done | bytes 32792
  2.8 0.4 shard_map.77
  3.2 0.0 copy-start.3
  3.2 14.1 %all_to_all.20.prices_ref = f32[8,16,128]{2,1,0:T(8,128)S(1)} all-to-all(f32[8,16,128]{2,1,0:T(8,128)S(1)} %get-tuple-element.11), channel_id=1, replica_groups=mesh['region'=8,'rep'=4] {'region'}, dimensions={0} | all-to-all | bytes 131072 | tf_op jit(solution)/shard_map/all_to_all | solution.py:271
  17.3 0.0 copy-done.3
  17.3 0.0 copy-start
  17.3 0.9 %copy-done = f32[16,4096]{1,0:T(8,128)S(1)} copy-done((f32[16,4096]{1,0:T(8,128)S(1)}, f32[16,4096]{1,0:T(8,128)}, u32[]{:S(2)}) %copy-start) | copy-done | bytes 262168
  18.3 0.0 copy-start.2
  18.3 0.9 %copy-done.2 = f32[16,4096]{1,0:T(8,128)S(1)} copy-done((f32[16,4096]{1,0:T(8,128)S(1)}, f32[16,4096]{1,0:T(8,128)}, u32[]{:S(2)}) %copy-start.2) | copy-done | bytes 262168
  19.2 1.6 %shard_map.78 = (f32[512,128]{1,0:T(8,128)S(1)}, f32[32,16,128]{2,1,0:T(8,128)S(1)}) custom-call(f32[8,16,128]{2,1,0:T(8,128)S(1)} %all_to_all.20.prices_ref, s32[32,128]{1,0:T(8,128)S(1)} %bitcast.23, f32[512,128]{1,0:T(8,128)S(1)} %bitcast.20, f32[512,128]{1,0:T(8,128)S(1)} %bitcast.22), custom_call_target="tpu_custom_call" | custom-call | tf_op jit(solution)/shard_map/pallas_call | solution.py:272
  20.8 12.5 %all_to_all.21.arrived_ref = f32[32,16,128]{2,1,0:T(8,128)S(1)} all-to-all(f32[32,16,128]{2,1,0:T(8,128)S(1)} %get-tuple-element.12), channel_id=1, replica_groups=mesh['region'=8,'rep'=4] {'region','rep'}, dimensions={0} | all-to-all | bytes 524288 | tf_op jit(solution)/shard_map/all_to_all | solution.py:273
  33.3 0.0 copy-start.1
  33.3 0.6 %shard_map.79 = (f32[8,16,128]{2,1,0:T(8,128)S(1)}, f32[16,512]{1,0:T(8,128)S(1)}) custom-call(f32[32,16,128]{2,1,0:T(8,128)S(1)} %all_to_all.21.arrived_ref, s32[8,128]{1,0:T(8,128)S(1)} %bitcast.26, f32[16,512]{1,0:T(8,128)S(1)} %get-tuple-element.13.dual_rows_ref, f32[16,512]{1,0:T(8,128)S(1)} %get-tuple-element.14.quota_rows_ref), custom_call_target="tpu_custom_call" | custom-call | tf_op jit(solution)/shard_map/pallas_call | solution.py:275
  33.9 9.5 %all_to_all.22.prices_ref = f32[8,16,128]{2,1,0:T(8,128)S(1)} all-to-all(f32[8,16,128]{2,1,0:T(8,128)S(1)} %get-tuple-element.15), channel_id=1, replica_groups=mesh['region'=8,'rep'=4] {'region'}, dimensions={0} | all-to-all | bytes 131072 | tf_op jit(solution)/shard_map/all_to_all | solution.py:271
  43.5 0.0 copy-done.1
  43.5 2.1 %shard_map.80 = (f32[512,128]{1,0:T(8,128)}, f32[32,16,128]{2,1,0:T(8,128)S(1)}) custom-call(f32[8,16,128]{2,1,0:T(8,128)S(1)} %all_to_all.22.prices_ref, s32[32,128]{1,0:T(8,128)S(1)} %bitcast.24, f32[512,128]{1,0:T(8,128)S(1)} %bitcast.21, f32[512,128]{1,0:T(8,128)S(1)} %get-tuple-element.16.primal_ref), custom_call_target="tpu_custom_call" | custom-call | tf_op jit(solution)/shard_map/pallas_call | solution.py:272
  45.5 12.3 %all_to_all.23.arrived_ref = f32[32,16,128]{2,1,0:T(8,128)S(1)} all-to-all(f32[32,16,128]{2,1,0:T(8,128)S(1)} %get-tuple-element.18), channel_id=1, replica_groups=mesh['region'=8,'rep'=4] {'region','rep'}, dimensions={0} | all-to-all | bytes 524288 | tf_op jit(solution)/shard_map/all_to_all | solution.py:273
  57.8 1.2 %shard_map.81 = f32[64,128]{1,0:T(8,128)} custom-call(f32[32,16,128]{2,1,0:T(8,128)S(1)} %all_to_all.23.arrived_ref, s32[8,128]{1,0:T(8,128)S(1)} %bitcast.27, f32[16,512]{1,0:T(8,128)S(1)} %get-tuple-element.19.dual_rows_ref, f32[16,512]{1,0:T(8,128)S(1)} %get-tuple-element.14.quota_rows_ref), custom_call_target="tpu_custom_call" | custom-call | tf_op jit(solution)/shard_map/pallas_call | solution.py:278
Async XLA Ops:
  0.6 0.7 %copy-start.4 = (s32[1,8,128]{2,1,0:T(8,128)S(1)}, s32[1,8,128]{2,1,0:T(8,128)}, u32[]{:S(2)}) copy-start(s32[1,8,128]{2,1,0:T(8,128)} %param.11) | copy-start | bytes 12292
  1.3 0.8 %copy-start.5 = (f32[8192]{0:T(1024)S(1)}, f32[8192]{0:T(1024)}, u32[]{:S(2)}) copy-start(f32[8192]{0:T(1024)} %param.8) | copy-start | bytes 98308
  2.1 0.8 %copy-start.6 = (f32[8192]{0:T(1024)S(1)}, f32[8192]{0:T(1024)}, u32[]{:S(2)}) copy-start(f32[8192]{0:T(1024)} %param.9) | copy-start | bytes 98308
  3.2 14.1 %copy-start.3 = (s32[4096]{0:T(1024)S(1)}, s32[4096]{0:T(1024)}, u32[]{:S(2)}) copy-start(s32[4096]{0:T(1024)} %param.10) | copy-start | bytes 49156
  17.3 1.0 %copy-start = (f32[16,4096]{1,0:T(8,128)S(1)}, f32[16,4096]{1,0:T(8,128)}, u32[]{:S(2)}) copy-start(f32[16,4096]{1,0:T(8,128)} %param.6) | copy-start | bytes 786436
  18.3 0.9 %copy-start.2 = (f32[16,4096]{1,0:T(8,128)S(1)}, f32[16,4096]{1,0:T(8,128)}, u32[]{:S(2)}) copy-start(f32[16,4096]{1,0:T(8,128)} %param.7) | copy-start | bytes 786436
  33.3 10.1 %copy-start.1 = (f32[16,4096]{1,0:T(8,128)S(1)}, f32[16,4096]{1,0:T(8,128)}, u32[]{:S(2)}) copy-start(f32[16,4096]{1,0:T(8,128)} %param.6) | copy-start | bytes 786436

commit v2 on v1

v2 whole, which is shorter than its diff:
```python
import functools

import jax
import jax.numpy as jnp
from jax import lax
from jax.experimental import pallas as pl
from jax.experimental.pallas import tpu as pltpu
from jax.sharding import PartitionSpec as P

ITERS = 2
BISECT = 30
PRIMAL_STEP = 0.5
DUAL_STEP = 0.25
LANES = 128
SUBLANES = 8
CHUNK = 8


def sorting_network(count):
    pairs = []
    p = 1
    while p < count:
        k = p
        while k >= 1:
            for j in range(k % p, count - k, 2 * k):
                for i in range(min(k, count - j - k)):
                    if (i + j) // (2 * p) == (i + j + k) // (2 * p):
                        pairs.append((i + j, i + j + k))
            k //= 2
        p *= 2
    return pairs


def repeat_chunks(total, body, init):
    if total == 1:
        return body(0, init)
    return lax.fori_loop(0, total, body, init)


def simplex_theta(values):
    ranked = list(values)
    for a, b in sorting_network(len(values)):
        ranked[a], ranked[b] = jnp.maximum(ranked[a], ranked[b]), jnp.minimum(ranked[a], ranked[b])
    largest = ranked[0]
    total = jnp.zeros_like(largest)
    best = jnp.full_like(largest, -1.0)
    for k in range(1, len(values)):
        total = total + (ranked[k] - largest)
        best = jnp.maximum(best, (total - 1.0) * (1.0 / (k + 1)))
    cells = float(2**BISECT)
    step = jnp.maximum(jnp.ceil((best + 1.0) * cells), 1.0) - 0.5
    return (largest - 1.0) + step * (1.0 / cells)


def split_two(x):
    high = x.astype(jnp.bfloat16)
    low = (x - high.astype(jnp.float32)).astype(jnp.bfloat16)
    return high, low


def person_kernel(options, rep, last, *refs):
    if last:
        prices_ref, share_ref, slot_ref, cost_ref, primal_ref, fresh_ref, sums_ref, x_ref, parts_ref, hot_ref = refs
        regions = share_ref.shape[0]
    else:
        prices_ref, slot_ref, cost_ref, primal_ref, fresh_ref, sums_ref, x_ref, parts_ref, hot_ref = refs
        regions = prices_ref.shape[0]
    quarter = options // rep
    rows = slot_ref.shape[0]
    halves = options // SUBLANES
    chunks = regions // CHUNK

    def price(d, o):
        if last:
            return prices_ref[d * rep + o // quarter, o % quarter : o % quarter + 1, :]
        return prices_ref[d, o : o + 1, :]

    for g in range(rows // SUBLANES):
        slot = slot_ref[g * SUBLANES : (g + 1) * SUBLANES, :]
        owner = slot // LANES
        within = slot - owner * LANES

        def pick(chunk, found):
            found = list(found)
            for d in range(CHUNK):
                mine = owner == chunk * CHUNK + d
                for o in range(options):
                    table = jnp.broadcast_to(price(chunk * CHUNK + d, o), (SUBLANES, LANES))
                    value = jnp.take_along_axis(table, within, axis=1)
                    found[o] = jnp.where(mine, value, found[o])
            return tuple(found)

        zero = jnp.zeros((SUBLANES, LANES), jnp.float32)
        adjoint = repeat_chunks(chunks, pick, (zero,) * options)
        places = []
        values = []
        for o in range(options):
            first = ((o // SUBLANES) * rows + g * SUBLANES) * SUBLANES + o % SUBLANES
            at = pl.ds(first, SUBLANES, stride=SUBLANES)
            places.append(at)
            values.append(primal_ref[at, :] - PRIMAL_STEP * (cost_ref[at, :] + adjoint[o]))
        theta = simplex_theta(values)
        for o in range(options):
            fresh = jnp.maximum(values[o] - theta, 0.0)
            fresh_ref[places[o], :] = fresh
            x_ref[places[o], :] = 2.0 * fresh - primal_ref[places[o], :]

    for c in range(rows):
        span = slice(c * LANES, (c + 1) * LANES)
        x = jnp.concatenate(
            [x_ref[(h * rows + c) * SUBLANES : (h * rows + c + 1) * SUBLANES, :] for h in range(halves)], axis=0
        )
        high, low = split_two(x)
        parts_ref[0:options, span] = high
        parts_ref[options : 2 * options, span] = low
        slot = jnp.broadcast_to(slot_ref[c : c + 1, :], (LANES, LANES))
        here = lax.broadcasted_iota(jnp.int32, (LANES, LANES), 0)
        hot_ref[:, span] = jnp.where((slot & (LANES - 1)) == here, 1.0, 0.0).astype(jnp.bfloat16)

    def add_up(chunk, carry):
        lines = []
        slot = jnp.concatenate([slot_ref[c : c + 1, :] for c in range(rows)], axis=1)
        owner = slot // LANES - chunk * CHUNK
        for part in range(2):
            x = parts_ref[part * options : (part + 1) * options, :]
            for d in range(CHUNK):
                mine = jnp.where(owner == d, 1.0, 0.0)
                mine = jnp.broadcast_to(mine, (options, rows * LANES)).astype(jnp.bfloat16)
                lines.append(x * mine)
        left = jnp.concatenate(lines, axis=0)
        total = lax.dot_general(
            left, hot_ref[...], (((1,), (1,)), ((), ())), preferred_element_type=jnp.float32
        )
        total = total[: CHUNK * options] + total[CHUNK * options :]
        for i in range(CHUNK):
            d = chunk * CHUNK + i
            block = total[i * options : (i + 1) * options, :]
            if last:
                share = jnp.where(lax.axis_index("rep") == 0, share_ref[d, options : options + SUBLANES, :], 0.0)
                held = jnp.concatenate([price(d, o) for o in range(options)], axis=0)
                block = DUAL_STEP * block + held * jnp.concatenate([share] * halves, axis=0)
            for k in range(rep):
                sums_ref[d * rep + k] = block if last else block[k * quarter : (k + 1) * quarter, :]
        return carry

    repeat_chunks(chunks, add_up, 0)


def group_place(lists):
    return (lists & (SUBLANES - 1)), lists >> 3


def each_region(regions, body):
    if regions <= CHUNK:
        for r in range(regions):
            body(r, 0)
    else:
        lax.fori_loop(0, regions, body, 0)


def pick_rows(blocks, lists_ref, r):
    lines = blocks[0].shape[0]
    residue, column = group_place(lists_ref[pl.ds(r, 1), :])
    block = jnp.broadcast_to(residue >> 1, (lines, LANES))
    lane = jnp.broadcast_to((residue & 1) * (LANES // 2) + column, (lines, LANES))
    found = jnp.zeros((lines, LANES), jnp.float32)
    for b, table in enumerate(blocks):
        found = jnp.where(block == b, jnp.take_along_axis(table, lane, axis=1), found)
    return found


def count_rows(lists_ref):
    here = lax.broadcasted_iota(jnp.int32, (SUBLANES, LANES), 0)
    there = lax.broadcasted_iota(jnp.int32, (LANES, LANES), 0)

    def add_up(chunk, total):
        lefts, rights = [], []
        for i in range(CHUNK):
            residue, column = group_place(lists_ref[pl.ds(chunk * CHUNK + i, 1), :])
            lefts.append(jnp.where(jnp.broadcast_to(residue, here.shape) == here, 1.0, 0.0).astype(jnp.bfloat16))
            rights.append(jnp.where(jnp.broadcast_to(column, there.shape) == there, 1.0, 0.0).astype(jnp.bfloat16))
        return total + lax.dot_general(
            jnp.concatenate(lefts, axis=1),
            jnp.concatenate(rights, axis=1),
            (((1,), (1,)), ((), ())),
            preferred_element_type=jnp.float32,
        )

    return repeat_chunks(lists_ref.shape[0] // CHUNK, add_up, jnp.zeros((SUBLANES, LANES), jnp.float32))


def first_kernel(options, *refs):
    sources, outs = refs[:6], refs[6:13]
    dual_ref, quota_ref, sems = refs[13:]
    picked_ref, shift_ref, base_ref, lists_ref, slot_ref, cost_ref, primal_ref = outs
    targets = (dual_ref, quota_ref, lists_ref, slot_ref, cost_ref, primal_ref)
    copies = [
        pltpu.make_async_copy(source, target, sems.at[i])
        for i, (source, target) in enumerate(zip(sources, targets))
    ]
    for copy in copies:
        copy.start()
    for copy in copies[:3]:
        copy.wait()
    half = LANES // 2
    quarter = shift_ref.shape[1]
    counts = count_rows(lists_ref)
    shares = 1.0 / jnp.maximum(counts, 1.0)
    both = jnp.concatenate([dual_ref[...], quota_ref[...]], axis=0).T
    left = lax.broadcasted_iota(jnp.int32, (options, LANES), 1) < half
    duals = []
    for b in range(SUBLANES // 2):
        span = slice(b * LANES, (b + 1) * LANES)
        even = both[2 * b * options : (2 * b + 1) * options, :]
        odd = both[(2 * b + 1) * options : (2 * b + 2) * options, :]
        dual = jnp.where(left, even, pltpu.roll(odd, half, 1))
        quota = jnp.where(left, pltpu.roll(even, half, 1), odd)
        count_even = jnp.broadcast_to(counts[2 * b : 2 * b + 1, :], (options, LANES))
        count_odd = jnp.broadcast_to(counts[2 * b + 1 : 2 * b + 2, :], (options, LANES))
        count = jnp.where(left, count_even, pltpu.roll(count_odd, half, 1))
        shift = dual - DUAL_STEP * quota
        for k in range(options // quarter):
            shift_ref[k, :, span] = shift[k * quarter : (k + 1) * quarter, :]
        alone = dual
        for _ in range(ITERS - 1):
            alone = jnp.maximum(alone - DUAL_STEP * quota, 0.0)
        base_ref[:, span] = jnp.where(count == 0.0, alone, 0.0) - DUAL_STEP * quota
        duals.append(dual)

    here = lax.broadcasted_iota(jnp.int32, (SUBLANES, LANES), 0)

    def one(r, carry):
        picked_ref[r, 0:options, :] = pick_rows(duals, lists_ref, r)
        residue, column = group_place(lists_ref[pl.ds(r, 1), :])
        share = jnp.take_along_axis(shares, jnp.broadcast_to(column, (SUBLANES, LANES)), axis=1)
        share = jnp.sum(jnp.where(residue == here, share, 0.0), axis=0, keepdims=True)
        picked_ref[r, options : options + SUBLANES, :] = jnp.broadcast_to(share, (SUBLANES, LANES))
        return carry

    each_region(lists_ref.shape[0], one)
    for copy in copies[3:]:
        copy.wait()


def block_sums(arrived_ref, lists_ref, groups):
    regions = lists_ref.shape[0]
    rep = arrived_ref.shape[0] // regions
    options = arrived_ref.shape[1]
    half = groups // SUBLANES

    def add_up(chunk, total):
        sums, hots = [], []
        here = lax.broadcasted_iota(jnp.int32, (groups, LANES), 0)
        for i in range(CHUNK):
            r = chunk * CHUNK + i
            x = arrived_ref[r * rep]
            for k in range(1, rep):
                x = x + arrived_ref[r * rep + k]
            sums.append(x)
            residue, column = group_place(lists_ref[pl.ds(r, 1), :])
            place = jnp.broadcast_to(residue * half + column, (groups, LANES))
            hots.append(jnp.where(place == here, 1.0, 0.0).astype(jnp.bfloat16))
        high, low = split_two(jnp.concatenate(sums, axis=1))
        right = jnp.concatenate(hots, axis=1)
        for part in (high, low):
            total = total + lax.dot_general(
                part, right, (((1,), (1,)), ((), ())), preferred_element_type=jnp.float32
            )
        return total

    return repeat_chunks(regions // CHUNK, add_up, jnp.zeros((options, groups), jnp.float32))


def middle_kernel(arrived_ref, lists_ref, shift_ref, picked_ref):
    regions = lists_ref.shape[0]
    rep = arrived_ref.shape[0] // regions
    applied = block_sums(arrived_ref, lists_ref, shift_ref.shape[2])
    dual = jnp.maximum(shift_ref[lax.axis_index("rep")] + DUAL_STEP * applied, 0.0)
    blocks = [dual[:, b * LANES : (b + 1) * LANES] for b in range(SUBLANES // 2)]

    def one(r, carry):
        found = pick_rows(blocks, lists_ref, r)
        for k in range(rep):
            picked_ref[r * rep + k] = found
        return carry

    each_region(regions, one)


def last_kernel(arrived_ref, lists_ref, base_ref, fresh_ref, dual_ref, primal_ref, sem):
    copy = pltpu.make_async_copy(fresh_ref, primal_ref, sem)
    copy.start()
    half = LANES // 2
    dual = jnp.maximum(base_ref[...] + block_sums(arrived_ref, lists_ref, base_ref.shape[1]), 0.0)
    lines = []
    for b in range(SUBLANES // 2):
        block = dual[:, b * LANES : (b + 1) * LANES]
        lines.append(block)
        lines.append(pltpu.roll(block, half, 1))
    dual_ref[...] = jnp.concatenate(lines, axis=0).T[: dual_ref.shape[0], :]
    copy.wait()


def call(kernel, outs, scratch=(), ins=None):
    vmem = pl.BlockSpec(memory_space=pltpu.VMEM)
    hbm = pl.BlockSpec(memory_space=pltpu.HBM)
    params = {} if ins is None else {"in_specs": [hbm if far else vmem for far in ins]}
    return pl.pallas_call(
        kernel,
        out_shape=[jax.ShapeDtypeStruct(shape, kind) for shape, kind, _ in outs],
        out_specs=[hbm if far else vmem for _, _, far in outs],
        scratch_shapes=list(scratch),
        compiler_params=pltpu.CompilerParams(vmem_limit_bytes=48 * 1024 * 1024),
        **params,
    )


def local(unit_cost, start_primal, start_dual, quota_bound, person_slot, cell_lists):
    options, persons = unit_cost.shape
    regions = lax.axis_size("region")
    rep = lax.axis_size("rep")
    quarter = options // rep
    groups = quota_bound.shape[0] // options
    rows = persons // LANES
    halves = options // SUBLANES

    def to_tiles(x):
        x = x.reshape(halves, SUBLANES, rows, LANES).transpose(0, 2, 1, 3)
        return x.reshape(options * rows, LANES)

    def from_tiles(x):
        x = x.reshape(halves, rows, SUBLANES, LANES).transpose(0, 2, 1, 3)
        return x.reshape(options, persons)

    def array(*shape, kind=jnp.float32, far=False):
        return (shape, kind, far)

    flat = (groups * options // LANES, LANES)
    tiles = array(options * rows, LANES)
    scratch = (
        pltpu.VMEM(tiles[0], jnp.float32),
        pltpu.VMEM((2 * options, persons), jnp.bfloat16),
        pltpu.VMEM((LANES, persons), jnp.bfloat16),
    )
    quarters = array(regions * rep, quarter, LANES)

    picked, shift, base, lists, slots, cost, primal = call(
        functools.partial(first_kernel, options),
        (
            array(regions, options + SUBLANES, LANES),
            array(rep, quarter, groups),
            array(options, groups),
            array(regions, LANES, kind=jnp.int32),
            array(rows, LANES, kind=jnp.int32),
            tiles,
            tiles,
        ),
        (pltpu.VMEM(flat, jnp.float32), pltpu.VMEM(flat, jnp.float32), pltpu.SemaphoreType.DMA((6,))),
        (True,) * 6,
    )(
        start_dual.reshape(flat),
        quota_bound.reshape(flat),
        cell_lists[0],
        person_slot.reshape(rows, LANES),
        to_tiles(unit_cost),
        to_tiles(start_primal),
    )
    first_prices = lax.all_to_all(picked, "region", split_axis=0, concat_axis=0, tiled=True)
    both = ("region", "rep")

    primal, sums = call(functools.partial(person_kernel, options, rep, False), (tiles, quarters), scratch)(
        first_prices, slots, cost, primal
    )
    arrived = lax.all_to_all(sums, both, split_axis=0, concat_axis=0, tiled=True)
    (picked,) = call(middle_kernel, (quarters,))(arrived, lists, shift)
    prices = lax.all_to_all(picked, both, split_axis=0, concat_axis=0, tiled=True)
    primal, sums = call(
        functools.partial(person_kernel, options, rep, True), (tiles, array(regions * rep, options, LANES)), scratch
    )(prices, first_prices, slots, cost, primal)
    arrived = lax.all_to_all(sums, both, split_axis=0, concat_axis=0, tiled=True)
    dual, primal = call(
        last_kernel,
        (array(*flat), array(options * rows, LANES, far=True)),
        (pltpu.SemaphoreType.DMA,),
    )(arrived, lists, base, primal)
    return (from_tiles(primal), dual.reshape(-1))


def solution(mesh):
    placed = (
        P(None, ("region", "rep")),
        P(None, ("region", "rep")),
        P("region"),
        P("region"),
        P(("region", "rep")),
        P("region", None, None),
    )
    return jax.shard_map(
        local,
        mesh=mesh,
        in_specs=placed,
        out_specs=(P(None, ("region", "rep")), P("region")),
        check_vma=False,
    )
```

time: 59.5 us -> 57 us (0.958)
  blocking collectives: 48.4 us -> 45.1 us
  local copies, waits for them, and re-layouts: 4.1 us -> 4.81 us
    all_to_all x2 -> x1, blocking collectives: 23.6 us -> 14.2 us  [local(): lax.all_to_all(picked, 'region', split_axis=0, concat_axis=0, tiled=True)]
    all_to_all x2 -> x3, blocking collectives: 24.8 us -> 30.9 us  [the longest x2 21.8 us: local(): lax.all_to_all(sums, both, split_axis=0, concat_axis=0, tiled=True)]
    unnamed x14 -> x12, local copies, waits for them, and re-layouts: 4.1 us -> 4.81 us
where the time goes in v2:
time: 57 us; the launch traced here: 56.5 us
  blocking collectives  45.1 us (79%)
  Pallas kernels  5.99 us (11%)
  local copies, waits for them, and re-layouts  4.81 us (8%)
  between operations  0.66 us (1%)
    all_to_all x2, blocking collectives, local(): lax.all_to_all(sums, both, split_axis=0, concat_axis=0, tiled=True)  21.8 us
    all_to_all x1, blocking collectives, local(): lax.all_to_all(picked, 'region', split_axis=0, concat_axis=0, tiled=True)  14.2 us
    all_to_all x1, blocking collectives, local(): lax.all_to_all(picked, both, split_axis=0, concat_axis=0, tiled=True)  9.1 us
    unnamed x12, local copies, waits for them, and re-layouts  4.81 us
    pallas_call x1, Pallas kernels, local(): call(functools.partial(person_kernel, options, rep, False), (tiles, quart...  1.58 us
    pallas_call x1, Pallas kernels, local(): call(functools.partial(person_kernel, options, rep, True), (tiles, array(...  1.58 us
    pallas_call x1, Pallas kernels, local(): call(last_kernel, (array(*flat), array(options * rows, LANES, far=True)),...  1.44 us

profile of v2, /device:TPU:0, one launch (start us, length us, event | category | flops | bytes accessed | tf_op | source)
XLA Modules:
  0.0 56.5 jit_solution(15320859560334600207)
XLA Ops:
  0.6 0.0 copy-start.5
  0.6 0.7 %copy-done.5 = s32[1,8,128]{2,1,0:T(8,128)S(1)} copy-done((s32[1,8,128]{2,1,0:T(8,128)S(1)}, s32[1,8,128]{2,1,0:T(8,128)}, u32[]{:S(2)}) %copy-start.5) | copy-done | bytes 4120
  1.3 0.0 copy-start
  1.3 0.9 %copy-done = f32[16,4096]{1,0:T(8,128)S(1)} copy-done((f32[16,4096]{1,0:T(8,128)S(1)}, f32[16,4096]{1,0:T(8,128)}, u32[]{:S(2)}) %copy-start) | copy-done | bytes 262168
  2.3 0.0 copy-start.1
  2.3 0.9 %copy-done.1 = f32[16,4096]{1,0:T(8,128)S(1)} copy-done((f32[16,4096]{1,0:T(8,128)S(1)}, f32[16,4096]{1,0:T(8,128)}, u32[]{:S(2)}) %copy-start.1) | copy-done | bytes 262168
  3.2 0.0 copy-start.2
  3.2 0.8 %copy-done.2 = f32[8192]{0:T(1024)S(1)} copy-done((f32[8192]{0:T(1024)S(1)}, f32[8192]{0:T(1024)}, u32[]{:S(2)}) %copy-start.2) | copy-done | bytes 32792
  4.0 0.0 copy-start.3
  4.0 0.8 %copy-done.3 = f32[8192]{0:T(1024)S(1)} copy-done((f32[8192]{0:T(1024)S(1)}, f32[8192]{0:T(1024)}, u32[]{:S(2)}) %copy-start.3) | copy-done | bytes 32792
  4.7 0.0 copy-start.4
  4.7 0.7 %copy-done.4 = s32[4096]{0:T(1024)S(1)} copy-done((s32[4096]{0:T(1024)S(1)}, s32[4096]{0:T(1024)}, u32[]{:S(2)}) %copy-start.4) | copy-done | bytes 16408
  5.5 0.6 %shard_map.77 = (f32[8,24,128]{2,1,0:T(8,128)S(1)}, f32[4,4,512]{2,1,0:T(4,128)S(1)}, f32[16,512]{1,0:T(8,128)S(1)}, s32[8,128]{1,0:T(8,128)S(1)}, s32[32,128]{1...) custom-call(f32[64,128]{1,0:T(8,128)S(1)} %bitcast.22, f32[64,128]{1,0:T(8,128)S(1)} %bitcast.23, ...), custom_call_target="tpu_custom_call" | custom-call | tf_op jit(solution)/shard_map/pallas_call | solution.py:347
  6.0 14.2 %all_to_all.20.refs_0_.refs_1_ = f32[8,24,128]{2,1,0:T(8,128)S(1)} all-to-all(f32[8,24,128]{2,1,0:T(8,128)S(1)} %get-tuple-element.15), channel_id=1, replica_groups=mesh['region'=8,'rep'=4] {'region'}, dimensions={0} | all-to-all | bytes 196608 | tf_op jit(solution)/shard_map/all_to_all | solution.py:368
  20.2 1.6 %shard_map.78 = (f32[512,128]{1,0:T(8,128)S(1)}, f32[32,4,128]{2,1,0:T(4,128)S(1)}) custom-call(f32[8,24,128]{2,1,0:T(8,128)S(1)} %all_to_all.20.refs_0_.refs_1_, s32[32,128]{1,0:T(8,128)S(1)} %get-tuple-element.16.refs_1_.refs_2_, f32[512,128]{1,0:T(8,128)S(1)} %get-tuple-element.17.refs_2_.refs_3_, f32[512,128]{1,0:T(8,128)S(1)} %get-tuple-element.18.refs_3_), custom_call_target="tpu_custom_call" | custom-call | tf_op jit(solution)/shard_map/pallas_call | solution.py:371
  21.8 9.5 %all_to_all.21.arrived_ref = f32[32,4,128]{2,1,0:T(4,128)S(1)} all-to-all(f32[32,4,128]{2,1,0:T(4,128)S(1)} %get-tuple-element.19), channel_id=1, replica_groups=mesh['region'=8,'rep'=4] {'region','rep'}, dimensions={0} | all-to-all | bytes 131072 | tf_op jit(solution)/shard_map/all_to_all | solution.py:374
  31.3 0.8 %shard_map.79 = f32[32,4,128]{2,1,0:T(4,128)S(1)} custom-call(f32[32,4,128]{2,1,0:T(4,128)S(1)} %all_to_all.21.arrived_ref, s32[8,128]{1,0:T(8,128)S(1)} %get-tuple-element.20.lists_ref, f32[4,4,512]{2,1,0:T(4,128)S(1)} %get-tuple-element.21.shift_ref), custom_call_target="tpu_custom_call" | custom-call | tf_op jit(solution)/shard_map/pallas_call | solution.py:375
  32.1 9.1 %all_to_all.22.refs_0_ = f32[32,4,128]{2,1,0:T(4,128)S(1)} all-to-all(f32[32,4,128]{2,1,0:T(4,128)S(1)} %shard_map.79), channel_id=1, replica_groups=mesh['region'=8,'rep'=4] {'region','rep'}, dimensions={0} | all-to-all | bytes 131072 | tf_op jit(solution)/shard_map/all_to_all | solution.py:376
  41.2 1.6 %shard_map.80 = (f32[512,128]{1,0:T(8,128)S(1)}, f32[32,16,128]{2,1,0:T(8,128)S(1)}) custom-call(f32[32,4,128]{2,1,0:T(4,128)S(1)} %all_to_all.22.refs_0_, f32[8,24,128]{2,1,0:T(8,128)S(1)} %all_to_all.20.refs_0_.refs_1_, s32[32,128]{1,0:T(8,128)S(1)} %get-tuple-element.16.refs_1_.refs_2_, f32[512,128]{1,0:T(8,128)S(1)} %get-tuple-element.17.refs_2_.refs_3_, ...), custom_call_target="tpu_custom_call" | custom-call | tf_op jit(solution)/shard_map/pallas_call | solution.py:377
  42.8 12.3 %all_to_all.23.arrived_ref = f32[32,16,128]{2,1,0:T(8,128)S(1)} all-to-all(f32[32,16,128]{2,1,0:T(8,128)S(1)} %get-tuple-element.23), channel_id=1, replica_groups=mesh['region'=8,'rep'=4] {'region','rep'}, dimensions={0} | all-to-all | bytes 524288 | tf_op jit(solution)/shard_map/all_to_all | solution.py:380
  55.1 1.4 %shard_map.81 = (f32[64,128]{1,0:T(8,128)}, f32[512,128]{1,0:T(8,128)}) custom-call(f32[32,16,128]{2,1,0:T(8,128)S(1)} %all_to_all.23.arrived_ref, s32[8,128]{1,0:T(8,128)S(1)} %get-tuple-element.20.lists_ref, f32[16,512]{1,0:T(8,128)S(1)} %get-tuple-element.24.base_ref, f32[512,128]{1,0:T(8,128)S(1)} %get-tuple-element.25.fresh_ref), custom_call_target="tpu_custom_call" | custom-call | tf_op jit(solution)/shard_map/pallas_call | solution.py:381
Async XLA Ops:
  0.6 0.7 %copy-start.5 = (s32[1,8,128]{2,1,0:T(8,128)S(1)}, s32[1,8,128]{2,1,0:T(8,128)}, u32[]{:S(2)}) copy-start(s32[1,8,128]{2,1,0:T(8,128)} %param.11) | copy-start | bytes 12292
  1.3 0.9 %copy-start = (f32[16,4096]{1,0:T(8,128)S(1)}, f32[16,4096]{1,0:T(8,128)}, u32[]{:S(2)}) copy-start(f32[16,4096]{1,0:T(8,128)} %param.6) | copy-start | bytes 786436
  2.3 0.9 %copy-start.1 = (f32[16,4096]{1,0:T(8,128)S(1)}, f32[16,4096]{1,0:T(8,128)}, u32[]{:S(2)}) copy-start(f32[16,4096]{1,0:T(8,128)} %param.7) | copy-start | bytes 786436
  3.2 0.8 %copy-start.2 = (f32[8192]{0:T(1024)S(1)}, f32[8192]{0:T(1024)}, u32[]{:S(2)}) copy-start(f32[8192]{0:T(1024)} %param.8) | copy-start | bytes 98308
  4.0 0.8 %copy-start.3 = (f32[8192]{0:T(1024)S(1)}, f32[8192]{0:T(1024)}, u32[]{:S(2)}) copy-start(f32[8192]{0:T(1024)} %param.9) | copy-start | bytes 98308
  4.7 0.7 %copy-start.4 = (s32[4096]{0:T(1024)S(1)}, s32[4096]{0:T(1024)}, u32[]{:S(2)}) copy-start(s32[4096]{0:T(1024)} %param.10) | copy-start | bytes 49156

commit v3 on v2

--- a/solution.py
+++ b/solution.py
@@ -287,9 +287,9 @@
     each_region(regions, one)
 
 
-def last_kernel(arrived_ref, lists_ref, base_ref, fresh_ref, dual_ref, primal_ref, sem):
-    copy = pltpu.make_async_copy(fresh_ref, primal_ref, sem)
-    copy.start()
+def last_kernel(arrived_ref, lists_ref, base_ref, fresh_ref, dual_ref, primal_ref, flat_ref, sems):
+    copy_primal = pltpu.make_async_copy(fresh_ref, primal_ref, sems.at[0])
+    copy_primal.start()
     half = LANES // 2
     dual = jnp.maximum(base_ref[...] + block_sums(arrived_ref, lists_ref, base_ref.shape[1]), 0.0)
     lines = []
@@ -297,8 +297,11 @@
         block = dual[:, b * LANES : (b + 1) * LANES]
         lines.append(block)
         lines.append(pltpu.roll(block, half, 1))
-    dual_ref[...] = jnp.concatenate(lines, axis=0).T[: dual_ref.shape[0], :]
-    copy.wait()
+    flat_ref[...] = jnp.concatenate(lines, axis=0).T[: flat_ref.shape[0], :]
+    copy_dual = pltpu.make_async_copy(flat_ref, dual_ref, sems.at[1])
+    copy_dual.start()
+    copy_primal.wait()
+    copy_dual.wait()
 
 
 def call(kernel, outs, scratch=(), ins=None):
@@ -358,12 +361,17 @@
         (pltpu.VMEM(flat, jnp.float32), pltpu.VMEM(flat, jnp.float32), pltpu.SemaphoreType.DMA((6,))),
         (True,) * 6,
     )(
-        start_dual.reshape(flat),
-        quota_bound.reshape(flat),
-        cell_lists[0],
-        person_slot.reshape(rows, LANES),
-        to_tiles(unit_cost),
-        to_tiles(start_primal),
+        *(
+            pltpu.with_memory_space_constraint(x, pltpu.HBM)
+            for x in (
+                start_dual.reshape(flat),
+                quota_bound.reshape(flat),
+                cell_lists[0],
+                person_slot.reshape(rows, LANES),
+                to_tiles(unit_cost),
+                to_tiles(start_primal),
+            )
+        )
     )
     first_prices = lax.all_to_all(picked, "region", split_axis=0, concat_axis=0, tiled=True)
     both = ("region", "rep")
@@ -380,8 +388,8 @@
     arrived = lax.all_to_all(sums, both, split_axis=0, concat_axis=0, tiled=True)
     dual, primal = call(
         last_kernel,
-        (array(*flat), array(options * rows, LANES, far=True)),
-        (pltpu.SemaphoreType.DMA,),
+        (array(*flat, far=True), array(options * rows, LANES, far=True)),
+        (pltpu.VMEM(flat, jnp.float32), pltpu.SemaphoreType.DMA((2,))),
     )(arrived, lists, base, primal)
     return (from_tiles(primal), dual.reshape(-1))
 

time: 57 us -> 52.6 us (0.923)
  local copies, waits for them, and re-layouts: 4.81 us -> 0 us
  Pallas kernels: 5.99 us -> 6.67 us
    unnamed x12 -> x0, local copies, waits for them, and re-layouts: 4.81 us -> none
    pallas_call x1, Pallas kernels: 0.58 us -> 1.24 us  [local(): call(functools.partial(first_kernel, options), (array(regions, options +...]
where the time goes in v3:
time: 52.6 us; the launch traced here: 52.4 us
  blocking collectives  45.1 us (86%)
  Pallas kernels  6.67 us (13%)
  between operations  0.65 us (1%)
    all_to_all x2, blocking collectives, local(): lax.all_to_all(sums, both, split_axis=0, concat_axis=0, tiled=True)  21.8 us
    all_to_all x1, blocking collectives, local(): lax.all_to_all(picked, 'region', split_axis=0, concat_axis=0, tiled=True)  14.2 us
    all_to_all x1, blocking collectives, local(): lax.all_to_all(picked, both, split_axis=0, concat_axis=0, tiled=True)  9.1 us
    pallas_call x1, Pallas kernels, local(): call(functools.partial(person_kernel, options, rep, False), (tiles, quart...  1.59 us
    pallas_call x1, Pallas kernels, local(): call(functools.partial(person_kernel, options, rep, True), (tiles, array(...  1.58 us
    pallas_call x1, Pallas kernels, local(): call(last_kernel, (array(*flat, far=True), array(options * rows, LANES, f...  1.45 us
    pallas_call x1, Pallas kernels, local(): call(functools.partial(first_kernel, options), (array(regions, options +...  1.24 us

profile of v3, /device:TPU:0, one launch (start us, length us, event | category | flops | bytes accessed | tf_op | source)
XLA Modules:
  0.0 52.4 jit_solution(12751119286473234599)
XLA Ops:
  0.6 1.2 %shard_map.77 = (f32[8,24,128]{2,1,0:T(8,128)S(1)}, f32[4,4,512]{2,1,0:T(4,128)S(1)}, f32[16,512]{1,0:T(8,128)S(1)}, s32[8,128]{1,0:T(8,128)S(1)}, s32[32,128]{1...) custom-call(f32[64,128]{1,0:T(8,128)} %bitcast.22, f32[64,128]{1,0:T(8,128)} %bitcast.23, ...), custom_call_target="tpu_custom_call" | custom-call | tf_op jit(solution)/shard_map/pallas_call | solution.py:350
  1.9 14.2 %all_to_all.20.refs_0_.refs_1_ = f32[8,24,128]{2,1,0:T(8,128)S(1)} all-to-all(f32[8,24,128]{2,1,0:T(8,128)S(1)} %get-tuple-element.15), channel_id=1, replica_groups=mesh['region'=8,'rep'=4] {'region'}, dimensions={0} | all-to-all | bytes 196608 | tf_op jit(solution)/shard_map/all_to_all | solution.py:376
  16.1 1.6 %shard_map.78 = (f32[512,128]{1,0:T(8,128)S(1)}, f32[32,4,128]{2,1,0:T(4,128)S(1)}) custom-call(f32[8,24,128]{2,1,0:T(8,128)S(1)} %all_to_all.20.refs_0_.refs_1_, s32[32,128]{1,0:T(8,128)S(1)} %get-tuple-element.16.refs_1_.refs_2_, f32[512,128]{1,0:T(8,128)S(1)} %get-tuple-element.17.refs_2_.refs_3_, f32[512,128]{1,0:T(8,128)S(1)} %get-tuple-element.18.refs_3_), custom_call_target="tpu_custom_call" | custom-call | tf_op jit(solution)/shard_map/pallas_call | solution.py:379
  17.7 9.5 %all_to_all.21.arrived_ref = f32[32,4,128]{2,1,0:T(4,128)S(1)} all-to-all(f32[32,4,128]{2,1,0:T(4,128)S(1)} %get-tuple-element.19), channel_id=1, replica_groups=mesh['region'=8,'rep'=4] {'region','rep'}, dimensions={0} | all-to-all | bytes 131072 | tf_op jit(solution)/shard_map/all_to_all | solution.py:382
  27.1 0.8 %shard_map.79 = f32[32,4,128]{2,1,0:T(4,128)S(1)} custom-call(f32[32,4,128]{2,1,0:T(4,128)S(1)} %all_to_all.21.arrived_ref, s32[8,128]{1,0:T(8,128)S(1)} %get-tuple-element.20.lists_ref, f32[4,4,512]{2,1,0:T(4,128)S(1)} %get-tuple-element.21.shift_ref), custom_call_target="tpu_custom_call" | custom-call | tf_op jit(solution)/shard_map/pallas_call | solution.py:383
  28.0 9.1 %all_to_all.22.refs_0_ = f32[32,4,128]{2,1,0:T(4,128)S(1)} all-to-all(f32[32,4,128]{2,1,0:T(4,128)S(1)} %shard_map.79), channel_id=1, replica_groups=mesh['region'=8,'rep'=4] {'region','rep'}, dimensions={0} | all-to-all | bytes 131072 | tf_op jit(solution)/shard_map/all_to_all | solution.py:384
  37.1 1.6 %shard_map.80 = (f32[512,128]{1,0:T(8,128)S(1)}, f32[32,16,128]{2,1,0:T(8,128)S(1)}) custom-call(f32[32,4,128]{2,1,0:T(4,128)S(1)} %all_to_all.22.refs_0_, f32[8,24,128]{2,1,0:T(8,128)S(1)} %all_to_all.20.refs_0_.refs_1_, s32[32,128]{1,0:T(8,128)S(1)} %get-tuple-element.16.refs_1_.refs_2_, f32[512,128]{1,0:T(8,128)S(1)} %get-tuple-element.17.refs_2_.refs_3_, ...), custom_call_target="tpu_custom_call" | custom-call | tf_op jit(solution)/shard_map/pallas_call | solution.py:385
  38.6 12.3 %all_to_all.23.arrived_ref = f32[32,16,128]{2,1,0:T(8,128)S(1)} all-to-all(f32[32,16,128]{2,1,0:T(8,128)S(1)} %get-tuple-element.23), channel_id=1, replica_groups=mesh['region'=8,'rep'=4] {'region','rep'}, dimensions={0} | all-to-all | bytes 524288 | tf_op jit(solution)/shard_map/all_to_all | solution.py:388
  50.9 1.4 %shard_map.81 = (f32[64,128]{1,0:T(8,128)}, f32[512,128]{1,0:T(8,128)}) custom-call(f32[32,16,128]{2,1,0:T(8,128)S(1)} %all_to_all.23.arrived_ref, s32[8,128]{1,0:T(8,128)S(1)} %get-tuple-element.20.lists_ref, f32[16,512]{1,0:T(8,128)S(1)} %get-tuple-element.24.base_ref, f32[512,128]{1,0:T(8,128)S(1)} %get-tuple-element.25.fresh_ref), custom_call_target="tpu_custom_call" | custom-call | tf_op jit(solution)/shard_map/pallas_call | solution.py:389

commit v4 on v1

v4 whole, which is shorter than its diff:
```python
import functools

import jax
import jax.numpy as jnp
from jax import lax
from jax.experimental import pallas as pl
from jax.experimental.pallas import tpu as pltpu
from jax.sharding import PartitionSpec as P

ITERS = 2
BISECT = 30
PRIMAL_STEP = 0.5
DUAL_STEP = 0.25
LANES = 128
SUBLANES = 8
CHUNK = 8
PACKED = 16
WIDE = 256
BLOCKS = 4
VMEM_LIMIT = 48 * 1024 * 1024


def sorting_network(count):
    pairs = []
    p = 1
    while p < count:
        k = p
        while k >= 1:
            for j in range(k % p, count - k, 2 * k):
                for i in range(min(k, count - j - k)):
                    if (i + j) // (2 * p) == (i + j + k) // (2 * p):
                        pairs.append((i + j, i + j + k))
            k //= 2
        p *= 2
    return pairs


def repeat_chunks(total, body, init):
    if total == 1:
        return body(0, init)
    return lax.fori_loop(0, total, body, init)


def simplex_theta(values):
    ranked = list(values)
    for a, b in sorting_network(len(values)):
        ranked[a], ranked[b] = jnp.maximum(ranked[a], ranked[b]), jnp.minimum(ranked[a], ranked[b])
    largest = ranked[0]
    total = jnp.zeros_like(largest)
    best = jnp.full_like(largest, -1.0)
    for k in range(1, len(values)):
        total = total + (ranked[k] - largest)
        best = jnp.maximum(best, (total - 1.0) * (1.0 / (k + 1)))
    cells = float(2**BISECT)
    step = jnp.maximum(jnp.ceil((best + 1.0) * cells), 1.0) - 0.5
    return (largest - 1.0) + step * (1.0 / cells)


def split_two(x):
    high = x.astype(jnp.bfloat16)
    low = (x - high.astype(jnp.float32)).astype(jnp.bfloat16)
    return high, low


def one_hot(index, count):
    wide = jnp.broadcast_to(index.astype(jnp.float32), (PACKED, index.shape[1])).astype(jnp.bfloat16)
    lines = []
    for first in range(0, count, PACKED):
        here = lax.broadcasted_iota(jnp.int32, wide.shape, 0) + first
        hit = wide == here.astype(jnp.float32).astype(jnp.bfloat16)
        lines.append(jnp.where(hit, jnp.bfloat16(1), jnp.bfloat16(0)))
    return jnp.concatenate(lines, axis=0)


def product(left, right):
    return lax.dot_general(left, right, (((1,), (1,)), ((), ())), preferred_element_type=jnp.float32)


def group_place(lists):
    return (lists & (SUBLANES - 1)) >> 1, (lists & 1) * (LANES // 2) + (lists >> 3)


def each_region(regions, body):
    if regions <= CHUNK:
        for r in range(regions):
            body(r, 0)
    else:
        lax.fori_loop(0, regions, body, 0)


def first_kernel(options, dual_far, lists_far, picked_ref, rows_ref, counts_ref, lists_ref, dual_ref, sems):
    copies = [
        pltpu.make_async_copy(dual_far, dual_ref, sems.at[0]),
        pltpu.make_async_copy(lists_far, lists_ref, sems.at[1]),
    ]
    for copy in copies:
        copy.start()
    for copy in copies:
        copy.wait()
    half = LANES // 2
    regions = lists_ref.shape[0]
    there = lax.broadcasted_iota(jnp.int32, (LANES, LANES), 0)
    which = lax.broadcasted_iota(jnp.int32, (SUBLANES, LANES), 0)

    def count_up(chunk, total):
        lefts, rights = [], []
        for i in range(CHUNK):
            block, lane = group_place(lists_ref[pl.ds(chunk * CHUNK + i, 1), :])
            lefts.append(jnp.where(block == which, 1.0, 0.0).astype(jnp.bfloat16))
            rights.append(jnp.where(lane == there, 1.0, 0.0).astype(jnp.bfloat16))
        return total + product(jnp.concatenate(lefts, axis=1), jnp.concatenate(rights, axis=1))

    counts = repeat_chunks(regions // CHUNK, count_up, jnp.zeros((SUBLANES, LANES), jnp.float32))
    counts_ref[...] = counts
    shares = 1.0 / jnp.maximum(counts, 1.0)

    flat = dual_ref[...]
    turned = jnp.concatenate([flat, flat], axis=0).T
    left = lax.broadcasted_iota(jnp.int32, (options, LANES), 1) < half
    duals = []
    for b in range(BLOCKS):
        even = turned[2 * b * options : (2 * b + 1) * options, :]
        odd = turned[(2 * b + 1) * options : (2 * b + 2) * options, :]
        dual = jnp.where(left, even, odd)
        rows_ref[b] = dual
        duals.append(dual)

    def one(r, carry):
        block, lane = group_place(lists_ref[pl.ds(r, 1), :])
        wide_block = jnp.broadcast_to(block, (options, LANES))
        wide_lane = jnp.broadcast_to(lane, (options, LANES))
        found = jnp.take_along_axis(duals[0], wide_lane, axis=1)
        for b in range(1, BLOCKS):
            found = jnp.where(wide_block == b, jnp.take_along_axis(duals[b], wide_lane, axis=1), found)
        picked_ref[r, 0:options, :] = found
        share = jnp.take_along_axis(shares, wide_lane[:SUBLANES], axis=1)
        share = jnp.sum(jnp.where(block == which, share, 0.0), axis=0, keepdims=True)
        picked_ref[r, options : options + SUBLANES, :] = jnp.broadcast_to(share, (SUBLANES, LANES))
        return carry

    each_region(regions, one)


def prepare_kernel(options, *refs):
    far, (rows_ref, counts_ref, lists_ref), outs, (quota_ref, sems) = refs[:4], refs[4:7], refs[7:16], refs[16:]
    slot_ref, cost_ref, primal_ref, shift_ref, base_ref, hot_ref, owner_ref, place_ref, block_ref = outs
    copies = [
        pltpu.make_async_copy(source, target, sems.at[i])
        for i, (source, target) in enumerate(zip(far, (slot_ref, quota_ref, cost_ref, primal_ref)))
    ]
    for copy in copies:
        copy.start()
    half = LANES // 2
    regions = lists_ref.shape[0]
    rows = slot_ref.shape[0]
    quarter = shift_ref.shape[1] // BLOCKS

    def lists_row(r, carry):
        block, lane = group_place(lists_ref[pl.ds(r, 1), :])
        place_ref[r] = one_hot(lane, LANES)
        block_ref[r] = jnp.broadcast_to(block, (SUBLANES, LANES))
        return carry

    each_region(regions, lists_row)
    copies[0].wait()
    for c in range(rows):
        span = slice(c * LANES, (c + 1) * LANES)
        slot = slot_ref[c : c + 1, :]
        hot_ref[:, span] = one_hot(slot & (WIDE - 1), WIDE)
        owner = jnp.broadcast_to((slot // WIDE).astype(jnp.float32), (PACKED, LANES))
        owner_ref[:, span] = owner.astype(jnp.bfloat16)
    copies[1].wait()
    flat = quota_ref[...]
    turned = jnp.concatenate([flat, flat], axis=0).T
    left = lax.broadcasted_iota(jnp.int32, (options, LANES), 1) < half
    for b in range(BLOCKS):
        even = turned[2 * b * options : (2 * b + 1) * options, :]
        odd = turned[(2 * b + 1) * options : (2 * b + 2) * options, :]
        pull = DUAL_STEP * jnp.where(left, even, odd)
        dual = rows_ref[b]
        shift = dual - pull
        for k in range(options // quarter):
            shift_ref[k, b * quarter : (b + 1) * quarter, :] = shift[k * quarter : (k + 1) * quarter, :]
        alone = dual
        for _ in range(ITERS - 1):
            alone = jnp.maximum(alone - pull, 0.0)
        named = jnp.broadcast_to(counts_ref[b : b + 1, :], alone.shape) > 0.0
        base_ref[b] = jnp.where(named, 0.0, alone) - pull
    for copy in copies[2:]:
        copy.wait()


def person_kernel(options, rep, last, *refs):
    if last:
        prices_ref, share_ref = refs[:2]
        regions = share_ref.shape[0]
    else:
        (prices_ref,) = refs[:1]
        regions = prices_ref.shape[0]
    slot_ref, cost_ref, primal_ref, hot_ref, owner_ref, fresh_ref, sums_ref, x_ref, parts_ref = refs[-9:]
    quarter = options // rep
    rows = slot_ref.shape[0]
    halves = options // SUBLANES
    chunks = regions // CHUNK
    blocks = CHUNK * LANES // WIDE
    groups = rows // SUBLANES
    stretch = SUBLANES * LANES

    def price(d, o):
        if last:
            return prices_ref[d * rep + o // quarter, o % quarter : o % quarter + 1, :]
        return prices_ref[d, o : o + 1, :]

    def partial_sums(chunk, g):
        span = slice(g * stretch, (g + 1) * stretch)
        owner = owner_ref[:, span]
        lines = []
        for part in range(2):
            x = parts_ref[part * options : (part + 1) * options, span]
            for e in range(blocks):
                number = jnp.asarray(chunk * blocks + e, jnp.float32).astype(jnp.bfloat16)
                lines.append(jnp.where(owner == number, x, jnp.bfloat16(0)))
        return product(jnp.concatenate(lines, axis=0), hot_ref[:, span])

    def hand_on(chunk, total):
        total = total[: blocks * options] + total[blocks * options :]
        for i in range(CHUNK):
            d = chunk * CHUNK + i
            e, h = divmod(i, WIDE // LANES)
            block = total[e * options : (e + 1) * options, h * LANES : (h + 1) * LANES]
            if last:
                share = jnp.where(lax.axis_index("rep") == 0, share_ref[d, options : options + SUBLANES, :], 0.0)
                held = jnp.concatenate([price(d, o) for o in range(options)], axis=0)
                block = DUAL_STEP * block + held * jnp.concatenate([share] * halves, axis=0)
            for k in range(rep):
                sums_ref[d * rep + k] = block if last else block[k * quarter : (k + 1) * quarter, :]

    total = None
    for g in range(groups):
        slot = slot_ref[g * SUBLANES : (g + 1) * SUBLANES, :]
        owner = slot // LANES
        within = slot - owner * LANES

        def pick(chunk, found):
            found = list(found)
            for d in range(CHUNK):
                mine = owner == chunk * CHUNK + d
                for o in range(options):
                    table = jnp.broadcast_to(price(chunk * CHUNK + d, o), (SUBLANES, LANES))
                    value = jnp.take_along_axis(table, within, axis=1)
                    found[o] = jnp.where(mine, value, found[o])
            return tuple(found)

        zero = jnp.zeros((SUBLANES, LANES), jnp.float32)
        adjoint = repeat_chunks(chunks, pick, (zero,) * options)
        places = []
        values = []
        for o in range(options):
            first = ((o // SUBLANES) * rows + g * SUBLANES) * SUBLANES + o % SUBLANES
            at = pl.ds(first, SUBLANES, stride=SUBLANES)
            places.append(at)
            values.append(primal_ref[at, :] - PRIMAL_STEP * (cost_ref[at, :] + adjoint[o]))
        theta = simplex_theta(values)
        for o in range(options):
            fresh = jnp.maximum(values[o] - theta, 0.0)
            fresh_ref[places[o], :] = fresh
            x_ref[places[o], :] = 2.0 * fresh - primal_ref[places[o], :]
        for c in range(g * SUBLANES, (g + 1) * SUBLANES):
            span = slice(c * LANES, (c + 1) * LANES)
            x = jnp.concatenate(
                [x_ref[(h * rows + c) * SUBLANES : (h * rows + c + 1) * SUBLANES, :] for h in range(halves)], axis=0
            )
            high, low = split_two(x)
            parts_ref[0:options, span] = high
            parts_ref[options : 2 * options, span] = low
        if chunks == 1:
            found = partial_sums(0, g)
            total = found if total is None else total + found

    if chunks == 1:
        hand_on(0, total)
    else:

        def add_up(chunk, carry):
            total = partial_sums(chunk, 0)
            for g in range(1, groups):
                total = total + partial_sums(chunk, g)
            hand_on(chunk, total)
            return carry

        lax.fori_loop(0, chunks, add_up, 0)


def block_sums(arrived_ref, place_ref, block_ref):
    regions = place_ref.shape[0]
    rep = arrived_ref.shape[0] // regions
    options = arrived_ref.shape[1]
    lines = BLOCKS * options
    copies = max(1, SUBLANES // options)
    tall = copies * options
    row = lax.broadcasted_iota(jnp.int32, (tall, CHUNK * LANES), 0) // options

    def add_up(chunk, total):
        sums, hots, numbers = [], [], []
        for i in range(CHUNK):
            r = chunk * CHUNK + i
            x = arrived_ref[r * rep]
            for k in range(1, rep):
                x = x + arrived_ref[r * rep + k]
            sums.append(jnp.concatenate([x] * copies, axis=0))
            hots.append(place_ref[r])
            numbers.append(jnp.concatenate([block_ref[r]] * (tall // SUBLANES), axis=0))
        x = jnp.concatenate(sums, axis=1)
        number = jnp.concatenate(numbers, axis=1) - row
        high = x.astype(jnp.bfloat16).astype(jnp.float32)
        left = [
            jnp.where(number == first, part, 0.0) for part in (high, x - high) for first in range(0, BLOCKS, copies)
        ]
        found = product(jnp.concatenate(left, axis=0).astype(jnp.bfloat16), jnp.concatenate(hots, axis=1))
        return total + found[:lines] + found[lines:]

    return repeat_chunks(regions // CHUNK, add_up, jnp.zeros((lines, LANES), jnp.float32))


def middle_kernel(arrived_ref, lists_ref, place_ref, block_ref, shift_ref, picked_ref):
    regions = lists_ref.shape[0]
    rep = arrived_ref.shape[0] // regions
    options = arrived_ref.shape[1]
    applied = block_sums(arrived_ref, place_ref, block_ref)
    dual = jnp.maximum(shift_ref[lax.axis_index("rep")] + DUAL_STEP * applied, 0.0)
    blocks = [dual[b * options : (b + 1) * options, :] for b in range(BLOCKS)]

    def one(r, carry):
        block, lane = group_place(lists_ref[pl.ds(r, 1), :])
        block = jnp.broadcast_to(block, (options, LANES))
        lane = jnp.broadcast_to(lane, (options, LANES))
        found = jnp.take_along_axis(blocks[0], lane, axis=1)
        for b in range(1, BLOCKS):
            found = jnp.where(block == b, jnp.take_along_axis(blocks[b], lane, axis=1), found)
        for k in range(rep):
            picked_ref[r * rep + k] = found
        return carry

    each_region(regions, one)


def last_kernel(arrived_ref, place_ref, block_ref, base_ref, dual_ref):
    options = base_ref.shape[1]
    sums = block_sums(arrived_ref, place_ref, block_ref)
    lines = []
    for b in range(BLOCKS):
        block = jnp.maximum(base_ref[b] + sums[b * options : (b + 1) * options, :], 0.0)
        lines.append(block)
        lines.append(pltpu.roll(block, LANES // 2, 1))
    dual_ref[...] = jnp.concatenate(lines, axis=0).T[: dual_ref.shape[0], :]


def write_kernel(fresh_ref, primal_far, sem):
    copy = pltpu.make_async_copy(fresh_ref, primal_far, sem)
    copy.start()
    copy.wait()


def call(kernel, outs, scratch=(), ins=None):
    vmem = pl.BlockSpec(memory_space=pltpu.VMEM)
    hbm = pl.BlockSpec(memory_space=pltpu.HBM)
    params = {} if ins is None else {"in_specs": [hbm if far else vmem for far in ins]}
    return pl.pallas_call(
        kernel,
        out_shape=[jax.ShapeDtypeStruct(shape, kind) for shape, kind, _ in outs],
        out_specs=[hbm if far else vmem for _, _, far in outs],
        scratch_shapes=list(scratch),
        compiler_params=pltpu.CompilerParams(vmem_limit_bytes=VMEM_LIMIT),
        **params,
    )


def far(x):
    return pltpu.with_memory_space_constraint(x, pltpu.HBM)


def local(unit_cost, start_primal, start_dual, quota_bound, person_slot, cell_lists):
    options, persons = unit_cost.shape
    regions = lax.axis_size("region")
    rep = lax.axis_size("rep")
    quarter = options // rep
    groups = quota_bound.shape[0] // options
    rows = persons // LANES
    halves = options // SUBLANES

    def to_tiles(x):
        x = x.reshape(halves, SUBLANES, rows, LANES).transpose(0, 2, 1, 3)
        return x.reshape(options * rows, LANES)

    def from_tiles(x):
        x = x.reshape(halves, rows, SUBLANES, LANES).transpose(0, 2, 1, 3)
        return x.reshape(options, persons)

    def array(*shape, kind=jnp.float32, far=False):
        return (shape, kind, far)

    flat = (groups * options // LANES, LANES)
    tiles = array(options * rows, LANES)
    block_rows = array(BLOCKS, options, LANES)
    quarters = array(regions * rep, quarter, LANES)
    wholes = array(regions * rep, options, LANES)
    both = ("region", "rep")
    exchange = functools.partial(lax.all_to_all, split_axis=0, concat_axis=0, tiled=True)

    picked, dual_rows, counts, lists = call(
        functools.partial(first_kernel, options),
        (
            array(regions, options + SUBLANES, LANES),
            block_rows,
            array(SUBLANES, LANES),
            array(regions, LANES, kind=jnp.int32),
        ),
        (pltpu.VMEM(flat, jnp.float32), pltpu.SemaphoreType.DMA((2,))),
        (True, True),
    )(far(start_dual.reshape(flat)), far(cell_lists[0]))
    first_prices = exchange(picked, "region")
    slots, cost, primal, shift, base, hot, owner, place, block = call(
        functools.partial(prepare_kernel, options),
        (
            array(rows, LANES, kind=jnp.int32),
            tiles,
            tiles,
            array(rep, BLOCKS * quarter, LANES),
            block_rows,
            array(WIDE, persons, kind=jnp.bfloat16),
            array(PACKED, persons, kind=jnp.bfloat16),
            array(regions, LANES, LANES, kind=jnp.bfloat16),
            array(regions, SUBLANES, LANES, kind=jnp.int32),
        ),
        (pltpu.VMEM(flat, jnp.float32), pltpu.SemaphoreType.DMA((4,))),
        (True,) * 4 + (False,) * 3,
    )(
        far(person_slot.reshape(rows, LANES)),
        far(quota_bound.reshape(flat)),
        far(to_tiles(unit_cost)),
        far(to_tiles(start_primal)),
        dual_rows,
        counts,
        lists,
    )
    scratch = (pltpu.VMEM(tiles[0], jnp.float32), pltpu.VMEM((2 * options, persons), jnp.bfloat16))

    primal, sums = call(functools.partial(person_kernel, options, rep, False), (tiles, quarters), scratch)(
        first_prices, slots, cost, primal, hot, owner
    )
    arrived = exchange(sums, both)
    (picked,) = call(middle_kernel, (quarters,))(arrived, lists, place, block, shift)
    prices = exchange(picked, both)
    primal, sums = call(functools.partial(person_kernel, options, rep, True), (tiles, wholes), scratch)(
        prices, first_prices, slots, cost, primal, hot, owner
    )
    arrived = exchange(sums, both)
    (primal,) = call(write_kernel, (array(*tiles[0], far=True),), (pltpu.SemaphoreType.DMA,))(primal)
    (dual,) = call(last_kernel, (array(*flat),))(arrived, place, block, base)
    return (from_tiles(primal), dual.reshape(-1))


def solution(mesh):
    placed = (
        P(None, ("region", "rep")),
        P(None, ("region", "rep")),
        P("region"),
        P("region"),
        P(("region", "rep")),
        P("region", None, None),
    )
    return jax.shard_map(
        local,
        mesh=mesh,
        in_specs=placed,
        out_specs=(P(None, ("region", "rep")), P("region")),
        check_vma=False,
    )
```

time: 59.5 us -> 53.9 us (0.906)
  blocking collectives: 48.4 us -> 18.6 us
  waiting for transfers between devices: 0 us -> 15.5 us
  starting transfers between devices: 0 us -> 9.88 us
  local copies, waits for them, and re-layouts: 4.1 us -> 0 us
  Pallas kernels: 5.79 us -> 8.85 us
    all_to_all x4 -> x2, blocking collectives: 48.4 us -> 18.6 us  [the longest x1 9.46 us: local(): arrived = exchange(sums, both)]
    all_to_all x0 -> x2, waiting for transfers between devices: none -> 15.5 us  [the longest x1 9.88 us: local(): arrived = exchange(sums, both)]
    all_to_all x0 -> x2, starting transfers between devices: none -> 9.88 us  [the longest x1 7.29 us: local(): first_prices = exchange(picked, 'region')]
    unnamed x14 -> x0, local copies, waits for them, and re-layouts: 4.1 us -> none
    pallas_call x5 -> x7, Pallas kernels: 5.79 us -> 8.85 us  [the longest x1 2.14 us: local(): call(functools.partial(person_kernel, options, rep, True), (tiles, wholes...]
  transfers between devices with their start and end apart: 0 -> 2, of which waited for: 0 -> 2; matrix products, arithmetic and copies ran while one was open for 0% -> 0% of each run, Pallas kernels for 0% -> 4%
where the time goes in v4:
time: 53.9 us; the launch traced here: 53.5 us
  blocking collectives  18.6 us (35%)
  waiting for transfers between devices  15.5 us (29%)
  starting transfers between devices  9.88 us (18%)
  Pallas kernels  8.85 us (16%)
  between operations  0.68 us (1%)
    all_to_all x1, waiting for transfers between devices, local(): arrived = exchange(sums, both)  9.88 us
    all_to_all x1, blocking collectives, local(): arrived = exchange(sums, both)  9.46 us
    all_to_all x1, blocking collectives, local(): prices = exchange(picked, both)  9.1 us
    all_to_all x1, starting transfers between devices, local(): first_prices = exchange(picked, 'region')  7.29 us
    all_to_all x1, waiting for transfers between devices, local(): first_prices = exchange(picked, 'region')  5.65 us
    all_to_all x1, starting transfers between devices, local(): arrived = exchange(sums, both)  2.58 us
    pallas_call x1, Pallas kernels, local(): call(functools.partial(person_kernel, options, rep, True), (tiles, wholes...  2.14 us
    pallas_call x1, Pallas kernels, local(): call(functools.partial(first_kernel, options), (array(regions, options +...  1.78 us
  transfers between devices with their start and end apart: 2, of which 2 were waited for; matrix products, arithmetic and copies ran while one was open for 0% of the time, Pallas kernels for 4%

profile of v4, /device:TPU:0, one launch (start us, length us, event | category | flops | bytes accessed | tf_op | source)
XLA Modules:
  0.0 53.5 jit_solution(9017617906844542152)
XLA Ops:
  0.6 1.8 %shard_map.77 = (f32[8,24,128]{2,1,0:T(8,128)}, f32[4,16,128]{2,1,0:T(8,128)S(1)}, f32[8,128]{1,0:T(8,128)S(1)}, s32[8,128]{1,0:T(8,128)S(1)}) custom-call(f32[64,128]{1,0:T(8,128)} %bitcast.25, s32[8,128]{1,0:T(8,128)} %bitcast.27), custom_call_target="tpu_custom_call" | custom-call | tf_op jit(solution)/shard_map/pallas_call | solution.py:410
  2.4 7.3 %all-to-all-start = ((f32[8,24,128]{2,1,0:T(8,128)}), f32[8,24,128]{2,1,0:T(8,128)S(1)}, u32[]{:S(2)}, u32[]{:S(2)}) async-start(f32[8,24,128]{2,1,0:T(8,128)} %get-tuple-element.19), calls=%async_computation | async-start | bytes 196608 | tf_op jit(solution)/shard_map/all_to_all | solution.py:421
  9.7 1.5 %shard_map.78 = (s32[32,128]{1,0:T(8,128)S(1)}, f32[512,128]{1,0:T(8,128)S(1)}, f32[512,128]{1,0:T(8,128)S(1)}, f32[4,16,128]{2,1,0:T(8,128)S(1)}, f32[4,16,128]...) custom-call(s32[32,128]{1,0:T(8,128)} %bitcast.26, ...), custom_call_target="tpu_custom_call" | custom-call | tf_op jit(solution)/shard_map/pallas_call | solution.py:422
  11.2 5.7 %all-to-all-done.refs_0_.refs_1_ = f32[8,24,128]{2,1,0:T(8,128)S(1)} async-done(((f32[8,24,128]{2,1,0:T(8,128)}), f32[8,24,128]{2,1,0:T(8,128)S(1)}, u32[]{:S(2)}, u32[]{:S(2)}) %all-to-all-start) | async-done | bytes 98336 | tf_op jit(solution)/shard_map/all_to_all | solution.py:421
  16.8 1.4 %shard_map.79 = (f32[512,128]{1,0:T(8,128)S(1)}, f32[32,4,128]{2,1,0:T(4,128)S(1)}) custom-call(f32[8,24,128]{2,1,0:T(8,128)S(1)} %all-to-all-done.refs_0_.refs_1_, s32[32,128]{1,0:T(8,128)S(1)} %get-tuple-element.23.refs_1_.refs_2_, f32[512,128]{1,0:T(8,128)S(1)} %get-tuple-element.24.refs_2_.refs_3_, f32[512,128]{1,0:T(8,128)S(1)} %get-tuple-element.25.refs_3_, ...), custom_call_target="tpu_custom_call" | custom-call | tf_op jit(solution)/shard_map/pallas_call | solution.py:448
  18.3 9.5 %all_to_all.20.arrived_ref = f32[32,4,128]{2,1,0:T(4,128)S(1)} all-to-all(f32[32,4,128]{2,1,0:T(4,128)S(1)} %get-tuple-element.28), channel_id=1, replica_groups=mesh['region'=8,'rep'=4] {'region','rep'}, dimensions={0} | all-to-all | bytes 131072 | tf_op jit(solution)/shard_map/all_to_all | solution.py:451
  27.7 0.3 shard_map.80
  28.1 9.1 %all_to_all.21.refs_0_ = f32[32,4,128]{2,1,0:T(4,128)S(1)} all-to-all(f32[32,4,128]{2,1,0:T(4,128)S(1)} %shard_map.80), channel_id=1, replica_groups=mesh['region'=8,'rep'=4] {'region','rep'}, dimensions={0} | all-to-all | bytes 131072 | tf_op jit(solution)/shard_map/all_to_all | solution.py:453
  37.2 2.1 %shard_map.81 = (f32[512,128]{1,0:T(8,128)S(1)}, f32[32,16,128]{2,1,0:T(8,128)}) custom-call(f32[32,4,128]{2,1,0:T(4,128)S(1)} %all_to_all.21.refs_0_, f32[8,24,128]{2,1,0:T(8,128)S(1)} %all-to-all-done.refs_0_.refs_1_, s32[32,128]{1,0:T(8,128)S(1)} %get-tuple-element.23.refs_1_.refs_2_, f32[512,128]{1,0:T(8,128)S(1)} %get-tuple-element.24.refs_2_.refs_3_, ...), custom_call_target="tpu_custom_call" | custom-call | tf_op jit(solution)/shard_map/pallas_call | solution.py:454
  39.3 2.6 %all-to-all-start.3 = ((f32[32,16,128]{2,1,0:T(8,128)}), f32[32,16,128]{2,1,0:T(8,128)S(1)}, u32[]{:S(2)}, u32[]{:S(2)}) async-start(f32[32,16,128]{2,1,0:T(8,128)} %get-tuple-element.34), calls=%async_computation.3 | async-start | bytes 524288 | tf_op jit(solution)/shard_map/all_to_all | solution.py:457
  41.9 0.7 %shard_map.82 = f32[512,128]{1,0:T(8,128)} custom-call(f32[512,128]{1,0:T(8,128)S(1)} %get-tuple-element.33.fresh_ref), custom_call_target="tpu_custom_call" | custom-call | tf_op jit(solution)/shard_map/pallas_call | solution.py:458
  42.6 9.9 %all-to-all-done.3.arrived_ref = f32[32,16,128]{2,1,0:T(8,128)S(1)} async-done(((f32[32,16,128]{2,1,0:T(8,128)}), f32[32,16,128]{2,1,0:T(8,128)S(1)}, u32[]{:S(2)}, u32[]{:S(2)}) %all-to-all-start.3) | async-done | bytes 262176 | tf_op jit(solution)/shard_map/all_to_all | solution.py:457
  52.5 1.0 %shard_map.83 = f32[64,128]{1,0:T(8,128)} custom-call(f32[32,16,128]{2,1,0:T(8,128)S(1)} %all-to-all-done.3.arrived_ref, bf16[8,128,128]{2,1,0:T(8,128)(2,1)S(1)} %get-tuple-element.29.place_ref, s32[8,8,128]{2,1,0:T(8,128)S(1)} %get-tuple-element.30.block_ref, f32[4,16,128]{2,1,0:T(8,128)S(1)} %get-tuple-element.35.base_ref), custom_call_target="tpu_custom_call" | custom-call | tf_op jit(solution)/shard_map/pallas_call | solution.py:459
Async XLA Ops:
  2.4 14.4 %all-to-all-start = ((f32[8,24,128]{2,1,0:T(8,128)}), f32[8,24,128]{2,1,0:T(8,128)S(1)}, u32[]{:S(2)}, u32[]{:S(2)}) async-start(f32[8,24,128]{2,1,0:T(8,128)} %get-tuple-element.19), calls=%async_computation | async-start | bytes 196608 | tf_op jit(solution)/shard_map/all_to_all | solution.py:421
  39.3 13.2 %all-to-all-start.3 = ((f32[32,16,128]{2,1,0:T(8,128)}), f32[32,16,128]{2,1,0:T(8,128)S(1)}, u32[]{:S(2)}, u32[]{:S(2)}) async-start(f32[32,16,128]{2,1,0:T(8,128)} %get-tuple-element.34), calls=%async_computation.3 | async-start | bytes 524288 | tf_op jit(solution)/shard_map/all_to_all | solution.py:457

commit v5 on v4

--- a/solution.py
+++ b/solution.py
@@ -88,17 +88,24 @@
         lax.fori_loop(0, regions, body, 0)
 
 
-def first_kernel(options, dual_far, lists_far, picked_ref, rows_ref, counts_ref, lists_ref, dual_ref, sems):
+def turn_rows(flat, options):
+    turned = jnp.concatenate([flat, flat], axis=0).T
+    left = lax.broadcasted_iota(jnp.int32, (options, LANES), 1) < LANES // 2
+    pairs = [turned[i * options : (i + 1) * options, :] for i in range(2 * BLOCKS)]
+    return [jnp.where(left, pairs[2 * b], pairs[2 * b + 1]) for b in range(BLOCKS)]
+
+
+def first_kernel(options, *refs):
+    far, outs, (dual_ref, quota_ref, sems) = refs[:6], refs[6:13], refs[13:]
+    picked_ref, shift_ref, base_ref, lists_ref, slot_ref, cost_ref, primal_ref = outs
+    targets = (lists_ref, dual_ref, quota_ref, slot_ref, cost_ref, primal_ref)
     copies = [
-        pltpu.make_async_copy(dual_far, dual_ref, sems.at[0]),
-        pltpu.make_async_copy(lists_far, lists_ref, sems.at[1]),
+        pltpu.make_async_copy(source, target, sems.at[i]) for i, (source, target) in enumerate(zip(far, targets))
     ]
     for copy in copies:
         copy.start()
-    for copy in copies:
-        copy.wait()
-    half = LANES // 2
     regions = lists_ref.shape[0]
+    quarter = shift_ref.shape[1] // BLOCKS
     there = lax.broadcasted_iota(jnp.int32, (LANES, LANES), 0)
     which = lax.broadcasted_iota(jnp.int32, (SUBLANES, LANES), 0)
 
@@ -107,23 +114,14 @@
         for i in range(CHUNK):
             block, lane = group_place(lists_ref[pl.ds(chunk * CHUNK + i, 1), :])
             lefts.append(jnp.where(block == which, 1.0, 0.0).astype(jnp.bfloat16))
-            rights.append(jnp.where(lane == there, 1.0, 0.0).astype(jnp.bfloat16))
+            rights.append(one_hot(lane, LANES))
         return total + product(jnp.concatenate(lefts, axis=1), jnp.concatenate(rights, axis=1))
 
+    copies[0].wait()
     counts = repeat_chunks(regions // CHUNK, count_up, jnp.zeros((SUBLANES, LANES), jnp.float32))
-    counts_ref[...] = counts
     shares = 1.0 / jnp.maximum(counts, 1.0)
-
-    flat = dual_ref[...]
-    turned = jnp.concatenate([flat, flat], axis=0).T
-    left = lax.broadcasted_iota(jnp.int32, (options, LANES), 1) < half
-    duals = []
-    for b in range(BLOCKS):
-        even = turned[2 * b * options : (2 * b + 1) * options, :]
-        odd = turned[(2 * b + 1) * options : (2 * b + 2) * options, :]
-        dual = jnp.where(left, even, odd)
-        rows_ref[b] = dual
-        duals.append(dual)
+    copies[1].wait()
+    duals = turn_rows(dual_ref[...], options)
 
     def one(r, carry):
         block, lane = group_place(lists_ref[pl.ds(r, 1), :])
@@ -139,54 +137,18 @@
         return carry
 
     each_region(regions, one)
-
-
-def prepare_kernel(options, *refs):
-    far, (rows_ref, counts_ref, lists_ref), outs, (quota_ref, sems) = refs[:4], refs[4:7], refs[7:16], refs[16:]
-    slot_ref, cost_ref, primal_ref, shift_ref, base_ref, hot_ref, owner_ref, place_ref, block_ref = outs
-    copies = [
-        pltpu.make_async_copy(source, target, sems.at[i])
-        for i, (source, target) in enumerate(zip(far, (slot_ref, quota_ref, cost_ref, primal_ref)))
-    ]
-    for copy in copies:
-        copy.start()
-    half = LANES // 2
-    regions = lists_ref.shape[0]
-    rows = slot_ref.shape[0]
-    quarter = shift_ref.shape[1] // BLOCKS
-
-    def lists_row(r, carry):
-        block, lane = group_place(lists_ref[pl.ds(r, 1), :])
-        place_ref[r] = one_hot(lane, LANES)
-        block_ref[r] = jnp.broadcast_to(block, (SUBLANES, LANES))
-        return carry
-
-    each_region(regions, lists_row)
-    copies[0].wait()
-    for c in range(rows):
-        span = slice(c * LANES, (c + 1) * LANES)
-        slot = slot_ref[c : c + 1, :]
-        hot_ref[:, span] = one_hot(slot & (WIDE - 1), WIDE)
-        owner = jnp.broadcast_to((slot // WIDE).astype(jnp.float32), (PACKED, LANES))
-        owner_ref[:, span] = owner.astype(jnp.bfloat16)
-    copies[1].wait()
-    flat = quota_ref[...]
-    turned = jnp.concatenate([flat, flat], axis=0).T
-    left = lax.broadcasted_iota(jnp.int32, (options, LANES), 1) < half
-    for b in range(BLOCKS):
-        even = turned[2 * b * options : (2 * b + 1) * options, :]
-        odd = turned[(2 * b + 1) * options : (2 * b + 2) * options, :]
-        pull = DUAL_STEP * jnp.where(left, even, odd)
-        dual = rows_ref[b]
-        shift = dual - pull
+    copies[2].wait()
+    for b, quota in enumerate(turn_rows(quota_ref[...], options)):
+        pull = DUAL_STEP * quota
+        shift = duals[b] - pull
         for k in range(options // quarter):
             shift_ref[k, b * quarter : (b + 1) * quarter, :] = shift[k * quarter : (k + 1) * quarter, :]
-        alone = dual
+        alone = duals[b]
         for _ in range(ITERS - 1):
             alone = jnp.maximum(alone - pull, 0.0)
-        named = jnp.broadcast_to(counts_ref[b : b + 1, :], alone.shape) > 0.0
+        named = jnp.broadcast_to(counts[b : b + 1, :], alone.shape) > 0.0
         base_ref[b] = jnp.where(named, 0.0, alone) - pull
-    for copy in copies[2:]:
+    for copy in copies[3:]:
         copy.wait()
 
 
@@ -197,7 +159,7 @@
     else:
         (prices_ref,) = refs[:1]
         regions = prices_ref.shape[0]
-    slot_ref, cost_ref, primal_ref, hot_ref, owner_ref, fresh_ref, sums_ref, x_ref, parts_ref = refs[-9:]
+    slot_ref, cost_ref, primal_ref, fresh_ref, sums_ref, x_ref, parts_ref, hot_ref, owner_ref = refs[-9:]
     quarter = options // rep
     rows = slot_ref.shape[0]
     halves = options // SUBLANES
@@ -273,6 +235,10 @@
             high, low = split_two(x)
             parts_ref[0:options, span] = high
             parts_ref[options : 2 * options, span] = low
+            line = slot_ref[c : c + 1, :]
+            hot_ref[:, span] = one_hot(line & (WIDE - 1), WIDE)
+            number = jnp.broadcast_to((line // WIDE).astype(jnp.float32), (PACKED, LANES))
+            owner_ref[:, span] = number.astype(jnp.bfloat16)
         if chunks == 1:
             found = partial_sums(0, g)
             total = found if total is None else total + found
@@ -291,8 +257,8 @@
         lax.fori_loop(0, chunks, add_up, 0)
 
 
-def block_sums(arrived_ref, place_ref, block_ref):
-    regions = place_ref.shape[0]
+def block_sums(arrived_ref, lists_ref):
+    regions = lists_ref.shape[0]
     rep = arrived_ref.shape[0] // regions
     options = arrived_ref.shape[1]
     lines = BLOCKS * options
@@ -308,8 +274,9 @@
             for k in range(1, rep):
                 x = x + arrived_ref[r * rep + k]
             sums.append(jnp.concatenate([x] * copies, axis=0))
-            hots.append(place_ref[r])
-            numbers.append(jnp.concatenate([block_ref[r]] * (tall // SUBLANES), axis=0))
+            block, lane = group_place(lists_ref[pl.ds(r, 1), :])
+            hots.append(one_hot(lane, LANES))
+            numbers.append(jnp.broadcast_to(block, (tall, LANES)))
         x = jnp.concatenate(sums, axis=1)
         number = jnp.concatenate(numbers, axis=1) - row
         high = x.astype(jnp.bfloat16).astype(jnp.float32)
@@ -322,11 +289,11 @@
     return repeat_chunks(regions // CHUNK, add_up, jnp.zeros((lines, LANES), jnp.float32))
 
 
-def middle_kernel(arrived_ref, lists_ref, place_ref, block_ref, shift_ref, picked_ref):
+def middle_kernel(arrived_ref, lists_ref, shift_ref, picked_ref):
     regions = lists_ref.shape[0]
     rep = arrived_ref.shape[0] // regions
     options = arrived_ref.shape[1]
-    applied = block_sums(arrived_ref, place_ref, block_ref)
+    applied = block_sums(arrived_ref, lists_ref)
     dual = jnp.maximum(shift_ref[lax.axis_index("rep")] + DUAL_STEP * applied, 0.0)
     blocks = [dual[b * options : (b + 1) * options, :] for b in range(BLOCKS)]
 
@@ -344,20 +311,17 @@
     each_region(regions, one)
 
 
-def last_kernel(arrived_ref, place_ref, block_ref, base_ref, dual_ref):
+def last_kernel(arrived_ref, lists_ref, base_ref, fresh_ref, dual_ref, primal_far, sem):
+    copy = pltpu.make_async_copy(fresh_ref, primal_far, sem)
+    copy.start()
     options = base_ref.shape[1]
-    sums = block_sums(arrived_ref, place_ref, block_ref)
+    sums = block_sums(arrived_ref, lists_ref)
     lines = []
     for b in range(BLOCKS):
         block = jnp.maximum(base_ref[b] + sums[b * options : (b + 1) * options, :], 0.0)
         lines.append(block)
         lines.append(pltpu.roll(block, LANES // 2, 1))
     dual_ref[...] = jnp.concatenate(lines, axis=0).T[: dual_ref.shape[0], :]
-
-
-def write_kernel(fresh_ref, primal_far, sem):
-    copy = pltpu.make_async_copy(fresh_ref, primal_far, sem)
-    copy.start()
     copy.wait()
 
 
@@ -407,56 +371,47 @@
     both = ("region", "rep")
     exchange = functools.partial(lax.all_to_all, split_axis=0, concat_axis=0, tiled=True)
 
-    picked, dual_rows, counts, lists = call(
+    picked, shift, base, lists, slots, cost, primal = call(
         functools.partial(first_kernel, options),
         (
             array(regions, options + SUBLANES, LANES),
+            array(rep, BLOCKS * quarter, LANES),
             block_rows,
-            array(SUBLANES, LANES),
             array(regions, LANES, kind=jnp.int32),
-        ),
-        (pltpu.VMEM(flat, jnp.float32), pltpu.SemaphoreType.DMA((2,))),
-        (True, True),
-    )(far(start_dual.reshape(flat)), far(cell_lists[0]))
-    first_prices = exchange(picked, "region")
-    slots, cost, primal, shift, base, hot, owner, place, block = call(
-        functools.partial(prepare_kernel, options),
-        (
             array(rows, LANES, kind=jnp.int32),
             tiles,
             tiles,
-            array(rep, BLOCKS * quarter, LANES),
-            block_rows,
-            array(WIDE, persons, kind=jnp.bfloat16),
-            array(PACKED, persons, kind=jnp.bfloat16),
-            array(regions, LANES, LANES, kind=jnp.bfloat16),
-            array(regions, SUBLANES, LANES, kind=jnp.int32),
         ),
-        (pltpu.VMEM(flat, jnp.float32), pltpu.SemaphoreType.DMA((4,))),
-        (True,) * 4 + (False,) * 3,
+        (pltpu.VMEM(flat, jnp.float32), pltpu.VMEM(flat, jnp.float32), pltpu.SemaphoreType.DMA((6,))),
+        (True,) * 6,
     )(
+        far(cell_lists[0]),
+        far(start_dual.reshape(flat)),
+        far(quota_bound.reshape(flat)),
         far(person_slot.reshape(rows, LANES)),
-        far(quota_bound.reshape(flat)),
         far(to_tiles(unit_cost)),
         far(to_tiles(start_primal)),
-        dual_rows,
-        counts,
-        lists,
-    )
-    scratch = (pltpu.VMEM(tiles[0], jnp.float32), pltpu.VMEM((2 * options, persons), jnp.bfloat16))
-
+    )
+    first_prices = exchange(picked, "region")
+    scratch = (
+        pltpu.VMEM(tiles[0], jnp.float32),
+        pltpu.VMEM((2 * options, persons), jnp.bfloat16),
+        pltpu.VMEM((WIDE, persons), jnp.bfloat16),
+        pltpu.VMEM((PACKED, persons), jnp.bfloat16),
+    )
     primal, sums = call(functools.partial(person_kernel, options, rep, False), (tiles, quarters), scratch)(
-        first_prices, slots, cost, primal, hot, owner
+        first_prices, slots, cost, primal
     )
     arrived = exchange(sums, both)
-    (picked,) = call(middle_kernel, (quarters,))(arrived, lists, place, block, shift)
+    (picked,) = call(middle_kernel, (quarters,))(arrived, lists, shift)
     prices = exchange(picked, both)
     primal, sums = call(functools.partial(person_kernel, options, rep, True), (tiles, wholes), scratch)(
-        prices, first_prices, slots, cost, primal, hot, owner
+        prices, first_prices, slots, cost, primal
     )
     arrived = exchange(sums, both)
-    (primal,) = call(write_kernel, (array(*tiles[0], far=True),), (pltpu.SemaphoreType.DMA,))(primal)
-    (dual,) = call(last_kernel, (array(*flat),))(arrived, place, block, base)
+    dual, primal = call(
+        last_kernel, (array(*flat), array(*tiles[0], far=True)), (pltpu.SemaphoreType.DMA,)
+    )(arrived, lists, base, primal)
     return (from_tiles(primal), dual.reshape(-1))
 
 

time: 53.9 us -> 52.6 us (0.976)
  blocking collectives: 18.6 us -> 45.1 us
  waiting for transfers between devices: 15.5 us -> 0 us
  starting transfers between devices: 9.88 us -> 0 us
  Pallas kernels: 8.85 us -> 6.61 us
    all_to_all x2 -> x0, waiting for transfers between devices: 15.5 us -> none  [the longest x1 9.88 us: local(): arrived = exchange(sums, both)]
    all_to_all x0 -> x1, blocking collectives: none -> 14.2 us  [local(): first_prices = exchange(picked, 'region')]
    all_to_all x1 -> x2, blocking collectives: 9.46 us -> 21.8 us  [local(): arrived = exchange(sums, both)]
    all_to_all x2 -> x0, starting transfers between devices: 9.88 us -> none  [the longest x1 7.29 us: local(): first_prices = exchange(picked, 'region')]
    pallas_call x4 -> x2, Pallas kernels: 3.51 us -> 1.69 us  [the longest x1 1.34 us: local(): call(last_kernel, (array(*flat), array(*tiles[0], far=True)), (pltpu.Sema...]
  transfers between devices with their start and end apart: 2 -> 0, of which waited for: 2 -> 0; matrix products, arithmetic and copies ran while one was open for 0% -> 0% of each run, Pallas kernels for 4% -> 0%
where the time goes in v5:
time: 52.6 us; the launch traced here: 52.4 us
  blocking collectives  45.1 us (86%)
  Pallas kernels  6.61 us (13%)
  between operations  0.66 us (1%)
    all_to_all x2, blocking collectives, local(): arrived = exchange(sums, both)  21.8 us
    all_to_all x1, blocking collectives, local(): first_prices = exchange(picked, 'region')  14.2 us
    all_to_all x1, blocking collectives, local(): prices = exchange(picked, both)  9.1 us
    pallas_call x1, Pallas kernels, local(): call(functools.partial(person_kernel, options, rep, False), (tiles, quart...  1.75 us
    pallas_call x1, Pallas kernels, local(): call(functools.partial(person_kernel, options, rep, True), (tiles, wholes...  1.75 us
    pallas_call x1, Pallas kernels, local(): call(functools.partial(first_kernel, options), (array(regions, options +...  1.42 us
    pallas_call x1, Pallas kernels, local(): call(last_kernel, (array(*flat), array(*tiles[0], far=True)), (pltpu.Sema...  1.34 us

profile of v5, /device:TPU:0, one launch (start us, length us, event | category | flops | bytes accessed | tf_op | source)
XLA Modules:
  0.0 52.4 jit_solution(13964170453225608235)
XLA Ops:
  0.6 1.4 %shard_map.77 = (f32[8,24,128]{2,1,0:T(8,128)S(1)}, f32[4,16,128]{2,1,0:T(8,128)S(1)}, f32[4,16,128]{2,1,0:T(8,128)S(1)}, s32[8,128]{1,0:T(8,128)S(1)}, s32[32,1...) custom-call(s32[8,128]{1,0:T(8,128)} %bitcast.25, f32[64,128]{1,0:T(8,128)} %bitcast.22, ...), custom_call_target="tpu_custom_call" | custom-call | tf_op jit(solution)/shard_map/pallas_call | solution.py:374
  2.1 14.2 %all_to_all.20.refs_0_.refs_1_ = f32[8,24,128]{2,1,0:T(8,128)S(1)} all-to-all(f32[8,24,128]{2,1,0:T(8,128)S(1)} %get-tuple-element.15), channel_id=1, replica_groups=mesh['region'=8,'rep'=4] {'region'}, dimensions={0} | all-to-all | bytes 196608 | tf_op jit(solution)/shard_map/all_to_all | solution.py:395
  16.3 1.8 %shard_map.78 = (f32[512,128]{1,0:T(8,128)S(1)}, f32[32,4,128]{2,1,0:T(4,128)S(1)}) custom-call(f32[8,24,128]{2,1,0:T(8,128)S(1)} %all_to_all.20.refs_0_.refs_1_, s32[32,128]{1,0:T(8,128)S(1)} %get-tuple-element.16.refs_1_.refs_2_, f32[512,128]{1,0:T(8,128)S(1)} %get-tuple-element.17.refs_2_.refs_3_, f32[512,128]{1,0:T(8,128)S(1)} %get-tuple-element.18.refs_3_), custom_call_target="tpu_custom_call" | custom-call | tf_op jit(solution)/shard_map/pallas_call | solution.py:402
  18.0 9.5 %all_to_all.21.arrived_ref = f32[32,4,128]{2,1,0:T(4,128)S(1)} all-to-all(f32[32,4,128]{2,1,0:T(4,128)S(1)} %get-tuple-element.19), channel_id=1, replica_groups=mesh['region'=8,'rep'=4] {'region','rep'}, dimensions={0} | all-to-all | bytes 131072 | tf_op jit(solution)/shard_map/all_to_all | solution.py:405
  27.5 0.3 shard_map.79
  27.8 9.1 %all_to_all.22.refs_0_ = f32[32,4,128]{2,1,0:T(4,128)S(1)} all-to-all(f32[32,4,128]{2,1,0:T(4,128)S(1)} %shard_map.79), channel_id=1, replica_groups=mesh['region'=8,'rep'=4] {'region','rep'}, dimensions={0} | all-to-all | bytes 131072 | tf_op jit(solution)/shard_map/all_to_all | solution.py:407
  36.9 1.7 %shard_map.80 = (f32[512,128]{1,0:T(8,128)S(1)}, f32[32,16,128]{2,1,0:T(8,128)S(1)}) custom-call(f32[32,4,128]{2,1,0:T(4,128)S(1)} %all_to_all.22.refs_0_, f32[8,24,128]{2,1,0:T(8,128)S(1)} %all_to_all.20.refs_0_.refs_1_, s32[32,128]{1,0:T(8,128)S(1)} %get-tuple-element.16.refs_1_.refs_2_, f32[512,128]{1,0:T(8,128)S(1)} %get-tuple-element.17.refs_2_.refs_3_, ...), custom_call_target="tpu_custom_call" | custom-call | tf_op jit(solution)/shard_map/pallas_call | solution.py:408
  38.7 12.3 %all_to_all.23.arrived_ref = f32[32,16,128]{2,1,0:T(8,128)S(1)} all-to-all(f32[32,16,128]{2,1,0:T(8,128)S(1)} %get-tuple-element.23), channel_id=1, replica_groups=mesh['region'=8,'rep'=4] {'region','rep'}, dimensions={0} | all-to-all | bytes 524288 | tf_op jit(solution)/shard_map/all_to_all | solution.py:411
  51.0 1.3 %shard_map.81 = (f32[64,128]{1,0:T(8,128)}, f32[512,128]{1,0:T(8,128)}) custom-call(f32[32,16,128]{2,1,0:T(8,128)S(1)} %all_to_all.23.arrived_ref, s32[8,128]{1,0:T(8,128)S(1)} %get-tuple-element.20.lists_ref, f32[4,16,128]{2,1,0:T(8,128)S(1)} %get-tuple-element.24.base_ref, f32[512,128]{1,0:T(8,128)S(1)} %get-tuple-element.25.fresh_ref), custom_call_target="tpu_custom_call" | custom-call | tf_op jit(solution)/shard_map/pallas_call | solution.py:412

commit v6 on v5

--- a/solution.py
+++ b/solution.py
@@ -147,42 +147,49 @@
         for _ in range(ITERS - 1):
             alone = jnp.maximum(alone - pull, 0.0)
         named = jnp.broadcast_to(counts[b : b + 1, :], alone.shape) > 0.0
-        base_ref[b] = jnp.where(named, 0.0, alone) - pull
+        base = jnp.where(named, 0.0, alone) - pull
+        for h in range(base_ref.shape[0]):
+            base_ref[h, b] = base[h * base_ref.shape[2] : (h + 1) * base_ref.shape[2], :]
     for copy in copies[3:]:
         copy.wait()
 
 
 def person_kernel(options, rep, last, *refs):
     if last:
-        prices_ref, share_ref = refs[:2]
+        prices_ref, share_ref, slot_ref, cost_ref, primal_ref, fresh_ref, sums_ref, x_ref, *kept_refs = refs
         regions = share_ref.shape[0]
     else:
-        (prices_ref,) = refs[:1]
+        prices_ref, slot_ref, cost_ref, primal_ref, fresh_ref, sums_ref, x_ref, *kept_refs = refs
         regions = prices_ref.shape[0]
-    slot_ref, cost_ref, primal_ref, fresh_ref, sums_ref, x_ref, parts_ref, hot_ref, owner_ref = refs[-9:]
     quarter = options // rep
     rows = slot_ref.shape[0]
     halves = options // SUBLANES
     chunks = regions // CHUNK
     blocks = CHUNK * LANES // WIDE
     groups = rows // SUBLANES
-    stretch = SUBLANES * LANES
+    sent = sums_ref.shape[1]
 
     def price(d, o):
         if last:
             return prices_ref[d * rep + o // quarter, o % quarter : o % quarter + 1, :]
         return prices_ref[d, o : o + 1, :]
 
-    def partial_sums(chunk, g):
-        span = slice(g * stretch, (g + 1) * stretch)
-        owner = owner_ref[:, span]
+    def operands(c):
+        x = [x_ref[(h * rows + c) * SUBLANES : (h * rows + c + 1) * SUBLANES, :] for h in range(halves)]
+        high, low = split_two(jnp.concatenate(x, axis=0))
+        line = slot_ref[c : c + 1, :]
+        number = jnp.broadcast_to((line // WIDE).astype(jnp.float32), (PACKED, LANES)).astype(jnp.bfloat16)
+        return high, low, one_hot(line & (WIDE - 1), WIDE), number
+
+    def partial_sums(chunk, pieces):
         lines = []
         for part in range(2):
-            x = parts_ref[part * options : (part + 1) * options, span]
             for e in range(blocks):
-                number = jnp.asarray(chunk * blocks + e, jnp.float32).astype(jnp.bfloat16)
-                lines.append(jnp.where(owner == number, x, jnp.bfloat16(0)))
-        return product(jnp.concatenate(lines, axis=0), hot_ref[:, span])
+                mine = jnp.asarray(chunk * blocks + e, jnp.float32).astype(jnp.bfloat16)
+                kept = [jnp.where(piece[3] == mine, piece[part], jnp.bfloat16(0)) for piece in pieces]
+                lines.append(jnp.concatenate(kept, axis=1))
+        hot = jnp.concatenate([piece[2] for piece in pieces], axis=1)
+        return product(jnp.concatenate(lines, axis=0), hot)
 
     def hand_on(chunk, total):
         total = total[: blocks * options] + total[blocks * options :]
@@ -195,7 +202,8 @@
                 held = jnp.concatenate([price(d, o) for o in range(options)], axis=0)
                 block = DUAL_STEP * block + held * jnp.concatenate([share] * halves, axis=0)
             for k in range(rep):
-                sums_ref[d * rep + k] = block if last else block[k * quarter : (k + 1) * quarter, :]
+                first = k * sent % options
+                sums_ref[d * rep + k] = block[first : first + sent, :]
 
     total = None
     for g in range(groups):
@@ -227,31 +235,21 @@
             fresh = jnp.maximum(values[o] - theta, 0.0)
             fresh_ref[places[o], :] = fresh
             x_ref[places[o], :] = 2.0 * fresh - primal_ref[places[o], :]
-        for c in range(g * SUBLANES, (g + 1) * SUBLANES):
-            span = slice(c * LANES, (c + 1) * LANES)
-            x = jnp.concatenate(
-                [x_ref[(h * rows + c) * SUBLANES : (h * rows + c + 1) * SUBLANES, :] for h in range(halves)], axis=0
-            )
-            high, low = split_two(x)
-            parts_ref[0:options, span] = high
-            parts_ref[options : 2 * options, span] = low
-            line = slot_ref[c : c + 1, :]
-            hot_ref[:, span] = one_hot(line & (WIDE - 1), WIDE)
-            number = jnp.broadcast_to((line // WIDE).astype(jnp.float32), (PACKED, LANES))
-            owner_ref[:, span] = number.astype(jnp.bfloat16)
+        pieces = [operands(c) for c in range(g * SUBLANES, (g + 1) * SUBLANES)]
         if chunks == 1:
-            found = partial_sums(0, g)
+            found = partial_sums(0, pieces)
             total = found if total is None else total + found
+        else:
+            for c, piece in zip(range(g * SUBLANES, (g + 1) * SUBLANES), pieces):
+                for ref, value in zip(kept_refs, piece):
+                    ref[:, c * LANES : (c + 1) * LANES] = value
 
     if chunks == 1:
         hand_on(0, total)
     else:
 
         def add_up(chunk, carry):
-            total = partial_sums(chunk, 0)
-            for g in range(1, groups):
-                total = total + partial_sums(chunk, g)
-            hand_on(chunk, total)
+            hand_on(chunk, partial_sums(chunk, [[ref[...] for ref in kept_refs]]))
             return carry
 
         lax.fori_loop(0, chunks, add_up, 0)
@@ -311,18 +309,28 @@
     each_region(regions, one)
 
 
-def last_kernel(arrived_ref, lists_ref, base_ref, fresh_ref, dual_ref, primal_far, sem):
-    copy = pltpu.make_async_copy(fresh_ref, primal_far, sem)
-    copy.start()
-    options = base_ref.shape[1]
+def half_kernel(arrived_ref, lists_ref, base_ref, part_ref):
+    sent = arrived_ref.shape[1]
+    shares = base_ref.shape[0]
+    mine = lax.axis_index("rep") % shares
     sums = block_sums(arrived_ref, lists_ref)
     lines = []
     for b in range(BLOCKS):
-        block = jnp.maximum(base_ref[b] + sums[b * options : (b + 1) * options, :], 0.0)
-        lines.append(block)
-        lines.append(pltpu.roll(block, LANES // 2, 1))
-    dual_ref[...] = jnp.concatenate(lines, axis=0).T[: dual_ref.shape[0], :]
-    copy.wait()
+        block = jnp.maximum(base_ref[mine, b] + sums[b * sent : (b + 1) * sent, :], 0.0)
+        whole = jnp.concatenate([jnp.where(mine == h, block, 0.0) for h in range(shares)], axis=0)
+        lines.append(whole)
+        lines.append(pltpu.roll(whole, LANES // 2, 1))
+    part_ref[...] = jnp.concatenate(lines, axis=0).T[: part_ref.shape[0], :]
+
+
+def last_kernel(mine_ref, other_ref, fresh_ref, dual_far, primal_far, sum_ref, sems):
+    copy_primal = pltpu.make_async_copy(fresh_ref, primal_far, sems.at[0])
+    copy_primal.start()
+    sum_ref[...] = mine_ref[...] + other_ref[...]
+    copy_dual = pltpu.make_async_copy(sum_ref, dual_far, sems.at[1])
+    copy_dual.start()
+    copy_primal.wait()
+    copy_dual.wait()
 
 
 def call(kernel, outs, scratch=(), ins=None):
@@ -365,9 +373,10 @@
 
     flat = (groups * options // LANES, LANES)
     tiles = array(options * rows, LANES)
-    block_rows = array(BLOCKS, options, LANES)
+    half = options // 2
+    base_rows = array(2, BLOCKS, half, LANES)
     quarters = array(regions * rep, quarter, LANES)
-    wholes = array(regions * rep, options, LANES)
+    half_rows = array(regions * rep, half, LANES)
     both = ("region", "rep")
     exchange = functools.partial(lax.all_to_all, split_axis=0, concat_axis=0, tiled=True)
 
@@ -376,7 +385,7 @@
         (
             array(regions, options + SUBLANES, LANES),
             array(rep, BLOCKS * quarter, LANES),
-            block_rows,
+            base_rows,
             array(regions, LANES, kind=jnp.int32),
             array(rows, LANES, kind=jnp.int32),
             tiles,
@@ -393,25 +402,26 @@
         far(to_tiles(start_primal)),
     )
     first_prices = exchange(picked, "region")
-    scratch = (
-        pltpu.VMEM(tiles[0], jnp.float32),
-        pltpu.VMEM((2 * options, persons), jnp.bfloat16),
-        pltpu.VMEM((WIDE, persons), jnp.bfloat16),
-        pltpu.VMEM((PACKED, persons), jnp.bfloat16),
-    )
+    scratch = (pltpu.VMEM(tiles[0], jnp.float32),)
+    if regions > CHUNK:
+        scratch += tuple(pltpu.VMEM((tall, persons), jnp.bfloat16) for tall in (options, options, WIDE, PACKED))
     primal, sums = call(functools.partial(person_kernel, options, rep, False), (tiles, quarters), scratch)(
         first_prices, slots, cost, primal
     )
     arrived = exchange(sums, both)
     (picked,) = call(middle_kernel, (quarters,))(arrived, lists, shift)
     prices = exchange(picked, both)
-    primal, sums = call(functools.partial(person_kernel, options, rep, True), (tiles, wholes), scratch)(
+    primal, sums = call(functools.partial(person_kernel, options, rep, True), (tiles, half_rows), scratch)(
         prices, first_prices, slots, cost, primal
     )
     arrived = exchange(sums, both)
+    (part,) = call(half_kernel, (array(*flat),))(arrived, lists, base)
+    other = lax.ppermute(part, "rep", [(k, k ^ 1) for k in range(rep)])
     dual, primal = call(
-        last_kernel, (array(*flat), array(*tiles[0], far=True)), (pltpu.SemaphoreType.DMA,)
-    )(arrived, lists, base, primal)
+        last_kernel,
+        (array(*flat, far=True), array(*tiles[0], far=True)),
+        (pltpu.VMEM(flat, jnp.float32), pltpu.SemaphoreType.DMA((2,))),
+    )(part, other, primal)
     return (from_tiles(primal), dual.reshape(-1))
 
 

time: 52.6 us -> 50.5 us (0.960)
  blocking collectives: 45.1 us -> 42.7 us
  Pallas kernels: 6.61 us -> 5.61 us
  waiting for transfers between devices: 0 us -> 0.99 us
    all_to_all x2, blocking collectives: 21.8 us -> 19.4 us  [local(): arrived = exchange(sums, both)]
    ppermute x0 -> x1, waiting for transfers between devices: none -> 0.99 us  [local(): other = lax.ppermute(part, 'rep', [(k, k ^ 1) for k in range(rep)])]
    pallas_call x2 -> x3, Pallas kernels: 3.09 us -> 2.45 us  [the longest x1 1.39 us: local(): call(functools.partial(person_kernel, options, rep, True), (tiles, half_r...]
  transfers between devices with their start and end apart: 0 -> 1, of which waited for: 0 -> 1; matrix products, arithmetic and copies ran while one was open for 0% -> 0% of each run, Pallas kernels for 0% -> 0%
where the time goes in v6:
time: 50.5 us; the launch traced here: 50.2 us
  blocking collectives  42.7 us (85%)
  Pallas kernels  5.61 us (11%)
  waiting for transfers between devices  0.99 us (2%)
  between operations  0.66 us (1%)
    all_to_all x2, blocking collectives, local(): arrived = exchange(sums, both)  19.4 us
    all_to_all x1, blocking collectives, local(): first_prices = exchange(picked, 'region')  14.2 us
    all_to_all x1, blocking collectives, local(): prices = exchange(picked, both)  9.1 us
    pallas_call x1, Pallas kernels, local(): call(functools.partial(first_kernel, options), (array(regions, options +...  1.42 us
    pallas_call x1, Pallas kernels, local(): call(functools.partial(person_kernel, options, rep, False), (tiles, quart...  1.4 us
    pallas_call x1, Pallas kernels, local(): call(functools.partial(person_kernel, options, rep, True), (tiles, half_r...  1.39 us
  transfers between devices with their start and end apart: 1, of which 1 were waited for; matrix products, arithmetic and copies ran while one was open for 0% of the time, Pallas kernels for 0%

profile of v6, /device:TPU:0, one launch (start us, length us, event | category | flops | bytes accessed | tf_op | source)
XLA Modules:
  0.0 50.2 jit_solution(13263876889207881532)
XLA Ops:
  0.6 1.4 %shard_map.77 = (f32[8,24,128]{2,1,0:T(8,128)S(1)}, f32[4,16,128]{2,1,0:T(8,128)S(1)}, f32[2,4,8,128]{3,2,1,0:T(8,128)S(1)}, s32[8,128]{1,0:T(8,128)S(1)}, s32[3...) custom-call(s32[8,128]{1,0:T(8,128)} %bitcast.25, f32[64,128]{1,0:T(8,128)} %bitcast.22, ...), custom_call_target="tpu_custom_call" | custom-call | tf_op jit(solution)/shard_map/pallas_call | solution.py:383
  2.1 14.2 %all_to_all.20.refs_0_.refs_1_ = f32[8,24,128]{2,1,0:T(8,128)S(1)} all-to-all(f32[8,24,128]{2,1,0:T(8,128)S(1)} %get-tuple-element.15), channel_id=1, replica_groups=mesh['region'=8,'rep'=4] {'region'}, dimensions={0} | all-to-all | bytes 196608 | tf_op jit(solution)/shard_map/all_to_all | solution.py:404
  16.3 1.4 %shard_map.78 = (f32[512,128]{1,0:T(8,128)S(1)}, f32[32,4,128]{2,1,0:T(4,128)S(1)}) custom-call(f32[8,24,128]{2,1,0:T(8,128)S(1)} %all_to_all.20.refs_0_.refs_1_, s32[32,128]{1,0:T(8,128)S(1)} %get-tuple-element.16.refs_1_.refs_2_, f32[512,128]{1,0:T(8,128)S(1)} %get-tuple-element.17.refs_2_.refs_3_, f32[512,128]{1,0:T(8,128)S(1)} %get-tuple-element.18.refs_3_), custom_call_target="tpu_custom_call" | custom-call | tf_op jit(solution)/shard_map/pallas_call | solution.py:408
  17.7 9.5 %all_to_all.21.arrived_ref = f32[32,4,128]{2,1,0:T(4,128)S(1)} all-to-all(f32[32,4,128]{2,1,0:T(4,128)S(1)} %get-tuple-element.19), channel_id=1, replica_groups=mesh['region'=8,'rep'=4] {'region','rep'}, dimensions={0} | all-to-all | bytes 131072 | tf_op jit(solution)/shard_map/all_to_all | solution.py:411
  27.1 0.3 shard_map.79
  27.5 9.1 %all_to_all.22.refs_0_ = f32[32,4,128]{2,1,0:T(4,128)S(1)} all-to-all(f32[32,4,128]{2,1,0:T(4,128)S(1)} %shard_map.79), channel_id=1, replica_groups=mesh['region'=8,'rep'=4] {'region','rep'}, dimensions={0} | all-to-all | bytes 131072 | tf_op jit(solution)/shard_map/all_to_all | solution.py:413
  36.6 1.4 %shard_map.80 = (f32[512,128]{1,0:T(8,128)S(1)}, f32[32,8,128]{2,1,0:T(8,128)S(1)}) custom-call(f32[32,4,128]{2,1,0:T(4,128)S(1)} %all_to_all.22.refs_0_, f32[8,24,128]{2,1,0:T(8,128)S(1)} %all_to_all.20.refs_0_.refs_1_, s32[32,128]{1,0:T(8,128)S(1)} %get-tuple-element.16.refs_1_.refs_2_, f32[512,128]{1,0:T(8,128)S(1)} %get-tuple-element.17.refs_2_.refs_3_, ...), custom_call_target="tpu_custom_call" | custom-call | tf_op jit(solution)/shard_map/pallas_call | solution.py:414
  38.0 9.9 %all_to_all.23.arrived_ref = f32[32,8,128]{2,1,0:T(8,128)S(1)} all-to-all(f32[32,8,128]{2,1,0:T(8,128)S(1)} %get-tuple-element.23), channel_id=1, replica_groups=mesh['region'=8,'rep'=4] {'region','rep'}, dimensions={0} | all-to-all | bytes 262144 | tf_op jit(solution)/shard_map/all_to_all | solution.py:417
  47.9 0.3 shard_map.81.mine_ref
  48.3 0.3 collective-permute-start
  48.5 1.0 %collective-permute-done.other_ref = f32[64,128]{1,0:T(8,128)S(1)} collective-permute-done((f32[64,128]{1,0:T(8,128)S(1)}, f32[64,128]{1,0:T(8,128)S(1)}, u32[]{:S(2)}, u32[]{:S(2)}) %collective-permute-start) | collective-permute-done | bytes 32800 | tf_op jit(solution)/shard_map/ppermute | solution.py:419
  49.5 0.7 %shard_map.82 = (f32[64,128]{1,0:T(8,128)}, f32[512,128]{1,0:T(8,128)}) custom-call(f32[64,128]{1,0:T(8,128)S(1)} %shard_map.81.mine_ref, f32[64,128]{1,0:T(8,128)S(1)} %collective-permute-done.other_ref, f32[512,128]{1,0:T(8,128)S(1)} %get-tuple-element.25.fresh_ref), custom_call_target="tpu_custom_call" | custom-call | tf_op jit(solution)/shard_map/pallas_call | solution.py:420
Async XLA Ops:
  48.3 1.3 %collective-permute-start = (f32[64,128]{1,0:T(8,128)S(1)}, f32[64,128]{1,0:T(8,128)S(1)}, u32[]{:S(2)}, u32[]{:S(2)}) collective-permute-start(f32[64,128]{1,0:T(8,128)S(1)} %shard_map.81.mine_ref), channel_id=1, source_target_pairs={{0,1},{1,0},{2,3},{3,2},{4,5},{5,4},{6,7},{7,6},{8,9},{9,8},{10,11... | collective-permute-start | bytes 98312 | tf_op jit(solution)/shard_map/ppermute | solution.py:419

commit v7 on v6

--- a/solution.py
+++ b/solution.py
@@ -16,6 +16,8 @@
 CHUNK = 8
 PACKED = 16
 WIDE = 256
+LANE_BITS = LANES.bit_length() - 1
+WIDE_BITS = WIDE.bit_length() - 1
 BLOCKS = 4
 VMEM_LIMIT = 48 * 1024 * 1024
 
@@ -117,10 +119,10 @@
             rights.append(one_hot(lane, LANES))
         return total + product(jnp.concatenate(lefts, axis=1), jnp.concatenate(rights, axis=1))
 
-    copies[0].wait()
+    for copy in copies[:3]:
+        copy.wait()
     counts = repeat_chunks(regions // CHUNK, count_up, jnp.zeros((SUBLANES, LANES), jnp.float32))
     shares = 1.0 / jnp.maximum(counts, 1.0)
-    copies[1].wait()
     duals = turn_rows(dual_ref[...], options)
 
     def one(r, carry):
@@ -137,7 +139,6 @@
         return carry
 
     each_region(regions, one)
-    copies[2].wait()
     for b, quota in enumerate(turn_rows(quota_ref[...], options)):
         pull = DUAL_STEP * quota
         shift = duals[b] - pull
@@ -156,10 +157,10 @@
 
 def person_kernel(options, rep, last, *refs):
     if last:
-        prices_ref, share_ref, slot_ref, cost_ref, primal_ref, fresh_ref, sums_ref, x_ref, *kept_refs = refs
+        prices_ref, share_ref, turned_ref, slot_ref, cost_ref, primal_ref, fresh_ref, sums_ref, *kept_refs = refs
         regions = share_ref.shape[0]
     else:
-        prices_ref, slot_ref, cost_ref, primal_ref, fresh_ref, sums_ref, x_ref, *kept_refs = refs
+        prices_ref, slot_ref, cost_ref, primal_ref, fresh_ref, sums_ref, turned_ref, *kept_refs = refs
         regions = prices_ref.shape[0]
     quarter = options // rep
     rows = slot_ref.shape[0]
@@ -175,21 +176,35 @@
         return prices_ref[d, o : o + 1, :]
 
     def operands(c):
-        x = [x_ref[(h * rows + c) * SUBLANES : (h * rows + c + 1) * SUBLANES, :] for h in range(halves)]
-        high, low = split_two(jnp.concatenate(x, axis=0))
+        tiles = [slice((h * rows + c) * SUBLANES, (h * rows + c + 1) * SUBLANES) for h in range(halves)]
+        x = jnp.concatenate([2.0 * fresh_ref[tile, :] - primal_ref[tile, :] for tile in tiles], axis=0)
+        high, low = split_two(x)
+        span = slice(c * LANES, (c + 1) * LANES)
         line = slot_ref[c : c + 1, :]
-        number = jnp.broadcast_to((line // WIDE).astype(jnp.float32), (PACKED, LANES)).astype(jnp.bfloat16)
-        return high, low, one_hot(line & (WIDE - 1), WIDE), number
+        if last:
+            turned = turned_ref[span, :]
+        else:
+            within = jnp.broadcast_to((line & (WIDE - 1)).astype(jnp.float32), (LANES, LANES))
+            turned = within.astype(jnp.bfloat16).T
+            turned_ref[span, :] = turned
+        turned = jnp.concatenate([turned] * (WIDE // LANES), axis=1)
+        here = lax.broadcasted_iota(jnp.int32, (PACKED, WIDE), 1).astype(jnp.float32).astype(jnp.bfloat16)
+        hot = [
+            jnp.where(turned[first : first + PACKED] == here, jnp.bfloat16(1), jnp.bfloat16(0))
+            for first in range(0, LANES, PACKED)
+        ]
+        number = jnp.broadcast_to((line >> WIDE_BITS).astype(jnp.float32), (PACKED, LANES)).astype(jnp.bfloat16)
+        return high, low, number, jnp.concatenate(hot, axis=0)
 
     def partial_sums(chunk, pieces):
         lines = []
         for part in range(2):
             for e in range(blocks):
                 mine = jnp.asarray(chunk * blocks + e, jnp.float32).astype(jnp.bfloat16)
-                kept = [jnp.where(piece[3] == mine, piece[part], jnp.bfloat16(0)) for piece in pieces]
+                kept = [jnp.where(piece[2] == mine, piece[part], jnp.bfloat16(0)) for piece in pieces]
                 lines.append(jnp.concatenate(kept, axis=1))
-        hot = jnp.concatenate([piece[2] for piece in pieces], axis=1)
-        return product(jnp.concatenate(lines, axis=0), hot)
+        hot = jnp.concatenate([piece[3] for piece in pieces], axis=0)
+        return jnp.dot(jnp.concatenate(lines, axis=0), hot, preferred_element_type=jnp.float32)
 
     def hand_on(chunk, total):
         total = total[: blocks * options] + total[blocks * options :]
@@ -205,11 +220,10 @@
                 first = k * sent % options
                 sums_ref[d * rep + k] = block[first : first + sent, :]
 
-    total = None
     for g in range(groups):
         slot = slot_ref[g * SUBLANES : (g + 1) * SUBLANES, :]
-        owner = slot // LANES
-        within = slot - owner * LANES
+        owner = slot >> LANE_BITS
+        within = slot & (LANES - 1)
 
         def pick(chunk, found):
             found = list(found)
@@ -232,21 +246,17 @@
             values.append(primal_ref[at, :] - PRIMAL_STEP * (cost_ref[at, :] + adjoint[o]))
         theta = simplex_theta(values)
         for o in range(options):
-            fresh = jnp.maximum(values[o] - theta, 0.0)
-            fresh_ref[places[o], :] = fresh
-            x_ref[places[o], :] = 2.0 * fresh - primal_ref[places[o], :]
-        pieces = [operands(c) for c in range(g * SUBLANES, (g + 1) * SUBLANES)]
-        if chunks == 1:
-            found = partial_sums(0, pieces)
-            total = found if total is None else total + found
-        else:
-            for c, piece in zip(range(g * SUBLANES, (g + 1) * SUBLANES), pieces):
-                for ref, value in zip(kept_refs, piece):
-                    ref[:, c * LANES : (c + 1) * LANES] = value
-
+            fresh_ref[places[o], :] = jnp.maximum(values[o] - theta, 0.0)
+
+    pieces = [operands(c) for c in range(rows)]
     if chunks == 1:
-        hand_on(0, total)
+        hand_on(0, partial_sums(0, pieces))
     else:
+        for c, piece in enumerate(pieces):
+            span = slice(c * LANES, (c + 1) * LANES)
+            for ref, value in zip(kept_refs[:3], piece):
+                ref[:, span] = value
+            kept_refs[3][span, :] = piece[3]
 
         def add_up(chunk, carry):
             hand_on(chunk, partial_sums(chunk, [[ref[...] for ref in kept_refs]]))
@@ -402,17 +412,19 @@
         far(to_tiles(start_primal)),
     )
     first_prices = exchange(picked, "region")
-    scratch = (pltpu.VMEM(tiles[0], jnp.float32),)
+    scratch = ()
     if regions > CHUNK:
-        scratch += tuple(pltpu.VMEM((tall, persons), jnp.bfloat16) for tall in (options, options, WIDE, PACKED))
-    primal, sums = call(functools.partial(person_kernel, options, rep, False), (tiles, quarters), scratch)(
-        first_prices, slots, cost, primal
-    )
+        kept = ((options, persons), (options, persons), (PACKED, persons), (persons, WIDE))
+        scratch = tuple(pltpu.VMEM(shape, jnp.bfloat16) for shape in kept)
+    turned = array(persons, LANES, kind=jnp.bfloat16)
+    primal, sums, turned = call(
+        functools.partial(person_kernel, options, rep, False), (tiles, quarters, turned), scratch
+    )(first_prices, slots, cost, primal)
     arrived = exchange(sums, both)
     (picked,) = call(middle_kernel, (quarters,))(arrived, lists, shift)
     prices = exchange(picked, both)
     primal, sums = call(functools.partial(person_kernel, options, rep, True), (tiles, half_rows), scratch)(
-        prices, first_prices, slots, cost, primal
+        prices, first_prices, turned, slots, cost, primal
     )
     arrived = exchange(sums, both)
     (part,) = call(half_kernel, (array(*flat),))(arrived, lists, base)

time: 50.5 us -> 49.8 us (0.986)
  Pallas kernels: 5.61 us -> 4.92 us
where the time goes in v7:
time: 49.8 us; the launch traced here: 49.6 us
  blocking collectives  42.7 us (86%)
  Pallas kernels  4.92 us (10%)
  waiting for transfers between devices  0.99 us (2%)
  between operations  0.66 us (1%)
    all_to_all x2, blocking collectives, local(): arrived = exchange(sums, both)  19.4 us
    all_to_all x1, blocking collectives, local(): first_prices = exchange(picked, 'region')  14.2 us
    all_to_all x1, blocking collectives, local(): prices = exchange(picked, both)  9.1 us
    pallas_call x1, Pallas kernels, local(): call(functools.partial(first_kernel, options), (array(regions, options +...  1.25 us
    pallas_call x1, Pallas kernels, local(): call(functools.partial(person_kernel, options, rep, False), (tiles, quart...  1.2 us
    pallas_call x1, Pallas kernels, local(): call(functools.partial(person_kernel, options, rep, True), (tiles, half_r...  1.07 us
  transfers between devices with their start and end apart: 1, of which 1 were waited for; matrix products, arithmetic and copies ran while one was open for 0% of the time, Pallas kernels for 0%

profile of v7, /device:TPU:0, one launch (start us, length us, event | category | flops | bytes accessed | tf_op | source)
XLA Modules:
  0.0 49.6 jit_solution(12845375847264837201)
XLA Ops:
  0.6 1.2 %shard_map.77 = (f32[8,24,128]{2,1,0:T(8,128)S(1)}, f32[4,16,128]{2,1,0:T(8,128)S(1)}, f32[2,4,8,128]{3,2,1,0:T(8,128)S(1)}, s32[8,128]{1,0:T(8,128)S(1)}, s32[3...) custom-call(s32[8,128]{1,0:T(8,128)} %bitcast.25, f32[64,128]{1,0:T(8,128)} %bitcast.22, ...), custom_call_target="tpu_custom_call" | custom-call | tf_op jit(solution)/shard_map/pallas_call | solution.py:393
  1.9 14.2 %all_to_all.20.refs_0_.refs_1_ = f32[8,24,128]{2,1,0:T(8,128)S(1)} all-to-all(f32[8,24,128]{2,1,0:T(8,128)S(1)} %get-tuple-element.16), channel_id=1, replica_groups=mesh['region'=8,'rep'=4] {'region'}, dimensions={0} | all-to-all | bytes 196608 | tf_op jit(solution)/shard_map/all_to_all | solution.py:414
  16.1 1.2 %shard_map.78 = (f32[512,128]{1,0:T(8,128)S(1)}, f32[32,4,128]{2,1,0:T(4,128)S(1)}, bf16[4096,128]{1,0:T(8,128)(2,1)S(1)}) custom-call(f32[8,24,128]{2,1,0:T(8,128)S(1)} %all_to_all.20.refs_0_.refs_1_, s32[32,128]{1,0:T(8,128)S(1)} %get-tuple-element.17.refs_1_.refs_3_, f32[512,128]{1,0:T(8,128)S(1)} %get-tuple-element.18.refs_2_.refs_4_, ...), custom_call_target="tpu_custom_call" | custom-call | tf_op jit(solution)/shard_map/pallas_call | solution.py:420
  17.3 9.5 %all_to_all.21.arrived_ref = f32[32,4,128]{2,1,0:T(4,128)S(1)} all-to-all(f32[32,4,128]{2,1,0:T(4,128)S(1)} %get-tuple-element.20), channel_id=1, replica_groups=mesh['region'=8,'rep'=4] {'region','rep'}, dimensions={0} | all-to-all | bytes 131072 | tf_op jit(solution)/shard_map/all_to_all | solution.py:423
  26.8 0.3 shard_map.79
  27.1 9.1 %all_to_all.22.refs_0_ = f32[32,4,128]{2,1,0:T(4,128)S(1)} all-to-all(f32[32,4,128]{2,1,0:T(4,128)S(1)} %shard_map.79), channel_id=1, replica_groups=mesh['region'=8,'rep'=4] {'region','rep'}, dimensions={0} | all-to-all | bytes 131072 | tf_op jit(solution)/shard_map/all_to_all | solution.py:425
  36.2 1.1 %shard_map.80 = (f32[512,128]{1,0:T(8,128)S(1)}, f32[32,8,128]{2,1,0:T(8,128)S(1)}) custom-call(f32[32,4,128]{2,1,0:T(4,128)S(1)} %all_to_all.22.refs_0_, f32[8,24,128]{2,1,0:T(8,128)S(1)} %all_to_all.20.refs_0_.refs_1_, bf16[4096,128]{1,0:T(8,128)(2,1)S(1)} %get-tuple-element.23.refs_2_, s32[32,128]{1,0:T(8,128)S(1)} %get-tuple-element.17.refs_1_.refs_3_, ...), custom_call_target="tpu_custom_call" | custom-call | tf_op jit(solution)/shard_map/pallas_call | solution.py:426
  37.3 9.9 %all_to_all.23.arrived_ref = f32[32,8,128]{2,1,0:T(8,128)S(1)} all-to-all(f32[32,8,128]{2,1,0:T(8,128)S(1)} %get-tuple-element.25), channel_id=1, replica_groups=mesh['region'=8,'rep'=4] {'region','rep'}, dimensions={0} | all-to-all | bytes 262144 | tf_op jit(solution)/shard_map/all_to_all | solution.py:429
  47.2 0.3 shard_map.81.mine_ref
  47.6 0.3 collective-permute-start
  47.8 1.0 %collective-permute-done.other_ref = f32[64,128]{1,0:T(8,128)S(1)} collective-permute-done((f32[64,128]{1,0:T(8,128)S(1)}, f32[64,128]{1,0:T(8,128)S(1)}, u32[]{:S(2)}, u32[]{:S(2)}) %collective-permute-start) | collective-permute-done | bytes 32800 | tf_op jit(solution)/shard_map/ppermute | solution.py:431
  48.8 0.7 %shard_map.82 = (f32[64,128]{1,0:T(8,128)}, f32[512,128]{1,0:T(8,128)}) custom-call(f32[64,128]{1,0:T(8,128)S(1)} %shard_map.81.mine_ref, f32[64,128]{1,0:T(8,128)S(1)} %collective-permute-done.other_ref, f32[512,128]{1,0:T(8,128)S(1)} %get-tuple-element.27.fresh_ref), custom_call_target="tpu_custom_call" | custom-call | tf_op jit(solution)/shard_map/pallas_call | solution.py:432
Async XLA Ops:
  47.6 1.3 %collective-permute-start = (f32[64,128]{1,0:T(8,128)S(1)}, f32[64,128]{1,0:T(8,128)S(1)}, u32[]{:S(2)}, u32[]{:S(2)}) collective-permute-start(f32[64,128]{1,0:T(8,128)S(1)} %shard_map.81.mine_ref), channel_id=1, source_target_pairs={{0,1},{1,0},{2,3},{3,2},{4,5},{5,4},{6,7},{7,6},{8,9},{9,8},{10,11... | collective-permute-start | bytes 98312 | tf_op jit(solution)/shard_map/ppermute | solution.py:431

commit v8 on v7

--- a/solution.py
+++ b/solution.py
@@ -226,14 +226,19 @@
         within = slot & (LANES - 1)
 
         def pick(chunk, found):
-            found = list(found)
-            for d in range(CHUNK):
-                mine = owner == chunk * CHUNK + d
-                for o in range(options):
+            near = owner - chunk * CHUNK
+            here = (near >= 0) & (near < CHUNK)
+            bits = [(near & (1 << i)) == 0 for i in range(CHUNK.bit_length() - 1)]
+            picked = []
+            for o in range(options):
+                level = []
+                for d in range(CHUNK):
                     table = jnp.broadcast_to(price(chunk * CHUNK + d, o), (SUBLANES, LANES))
-                    value = jnp.take_along_axis(table, within, axis=1)
-                    found[o] = jnp.where(mine, value, found[o])
-            return tuple(found)
+                    level.append(jnp.take_along_axis(table, within, axis=1))
+                for low in bits:
+                    level = [jnp.where(low, a, b) for a, b in zip(level[::2], level[1::2])]
+                picked.append(level[0] if chunks == 1 else jnp.where(here, level[0], found[o]))
+            return tuple(picked)
 
         zero = jnp.zeros((SUBLANES, LANES), jnp.float32)
         adjoint = repeat_chunks(chunks, pick, (zero,) * options)
@@ -333,14 +338,10 @@
     part_ref[...] = jnp.concatenate(lines, axis=0).T[: part_ref.shape[0], :]
 
 
-def last_kernel(mine_ref, other_ref, fresh_ref, dual_far, primal_far, sum_ref, sems):
-    copy_primal = pltpu.make_async_copy(fresh_ref, primal_far, sems.at[0])
-    copy_primal.start()
-    sum_ref[...] = mine_ref[...] + other_ref[...]
-    copy_dual = pltpu.make_async_copy(sum_ref, dual_far, sems.at[1])
-    copy_dual.start()
-    copy_primal.wait()
-    copy_dual.wait()
+def write_kernel(fresh_ref, primal_far, sem):
+    copy = pltpu.make_async_copy(fresh_ref, primal_far, sem)
+    copy.start()
+    copy.wait()
 
 
 def call(kernel, outs, scratch=(), ins=None):
@@ -429,11 +430,8 @@
     arrived = exchange(sums, both)
     (part,) = call(half_kernel, (array(*flat),))(arrived, lists, base)
     other = lax.ppermute(part, "rep", [(k, k ^ 1) for k in range(rep)])
-    dual, primal = call(
-        last_kernel,
-        (array(*flat, far=True), array(*tiles[0], far=True)),
-        (pltpu.VMEM(flat, jnp.float32), pltpu.SemaphoreType.DMA((2,))),
-    )(part, other, primal)
+    (primal,) = call(write_kernel, (array(*tiles[0], far=True),), (pltpu.SemaphoreType.DMA,))(primal)
+    dual = part + other
     return (from_tiles(primal), dual.reshape(-1))
 
 

time: 49.8 us -> 49.7 us (level)
  waiting for transfers between devices: 0.99 us -> 0.27 us
  other arithmetic: 0 us -> 0.62 us
    ppermute x1, waiting for transfers between devices: 0.99 us -> 0.27 us  [local(): other = lax.ppermute(part, 'rep', [(k, k ^ 1) for k in range(rep)])]
    reshape x0 -> x1, other arithmetic: none -> 0.62 us  [local(): return (from_tiles(primal), dual.reshape(-1))]
  transfers between devices with their start and end apart: 1 -> 1, of which waited for: 1 -> 1; matrix products, arithmetic and copies ran while one was open for 0% -> 0% of each run, Pallas kernels for 0% -> 1%
where the time goes in v8:
time: 49.7 us; the launch traced here: 49.4 us
  blocking collectives  42.7 us (86%)
  Pallas kernels  4.87 us (10%)
  between operations  0.67 us (1%)
  other arithmetic  0.62 us (1%)
    all_to_all x2, blocking collectives, local(): arrived = exchange(sums, both)  19.4 us
    all_to_all x1, blocking collectives, local(): first_prices = exchange(picked, 'region')  14.2 us
    all_to_all x1, blocking collectives, local(): prices = exchange(picked, both)  9.1 us
    pallas_call x1, Pallas kernels, local(): call(functools.partial(first_kernel, options), (array(regions, options +...  1.25 us
    pallas_call x1, Pallas kernels, local(): call(functools.partial(person_kernel, options, rep, False), (tiles, quart...  1.22 us
    pallas_call x1, Pallas kernels, local(): call(functools.partial(person_kernel, options, rep, True), (tiles, half_r...  1.01 us
  transfers between devices with their start and end apart: 1, of which 1 were waited for; matrix products, arithmetic and copies ran while one was open for 0% of the time, Pallas kernels for 1%

profile of v8, /device:TPU:0, one launch (start us, length us, event | category | flops | bytes accessed | tf_op | source)
XLA Modules:
  0.0 49.4 jit_solution(10673707856724759845)
XLA Ops:
  0.6 1.2 %shard_map.77 = (f32[8,24,128]{2,1,0:T(8,128)S(1)}, f32[4,16,128]{2,1,0:T(8,128)S(1)}, f32[2,4,8,128]{3,2,1,0:T(8,128)S(1)}, s32[8,128]{1,0:T(8,128)S(1)}, s32[3...) custom-call(s32[8,128]{1,0:T(8,128)} %bitcast.27, f32[64,128]{1,0:T(8,128)} %bitcast.24, ...), custom_call_target="tpu_custom_call" | custom-call | tf_op jit(solution)/shard_map/pallas_call | solution.py:394
  1.9 14.2 %all_to_all.20.refs_0_.refs_1_ = f32[8,24,128]{2,1,0:T(8,128)S(1)} all-to-all(f32[8,24,128]{2,1,0:T(8,128)S(1)} %get-tuple-element.14), channel_id=1, replica_groups=mesh['region'=8,'rep'=4] {'region'}, dimensions={0} | all-to-all | bytes 196608 | tf_op jit(solution)/shard_map/all_to_all | solution.py:415
  16.1 1.2 %shard_map.78 = (f32[512,128]{1,0:T(8,128)S(1)}, f32[32,4,128]{2,1,0:T(4,128)S(1)}, bf16[4096,128]{1,0:T(8,128)(2,1)S(1)}) custom-call(f32[8,24,128]{2,1,0:T(8,128)S(1)} %all_to_all.20.refs_0_.refs_1_, s32[32,128]{1,0:T(8,128)S(1)} %get-tuple-element.15.refs_1_.refs_3_, f32[512,128]{1,0:T(8,128)S(1)} %get-tuple-element.16.refs_2_.refs_4_, ...), custom_call_target="tpu_custom_call" | custom-call | tf_op jit(solution)/shard_map/pallas_call | solution.py:421
  17.3 9.5 %all_to_all.21.arrived_ref = f32[32,4,128]{2,1,0:T(4,128)S(1)} all-to-all(f32[32,4,128]{2,1,0:T(4,128)S(1)} %get-tuple-element.18), channel_id=1, replica_groups=mesh['region'=8,'rep'=4] {'region','rep'}, dimensions={0} | all-to-all | bytes 131072 | tf_op jit(solution)/shard_map/all_to_all | solution.py:424
  26.8 0.3 shard_map.79
  27.1 9.1 %all_to_all.22.refs_0_ = f32[32,4,128]{2,1,0:T(4,128)S(1)} all-to-all(f32[32,4,128]{2,1,0:T(4,128)S(1)} %shard_map.79), channel_id=1, replica_groups=mesh['region'=8,'rep'=4] {'region','rep'}, dimensions={0} | all-to-all | bytes 131072 | tf_op jit(solution)/shard_map/all_to_all | solution.py:426
  36.2 1.0 %shard_map.80 = (f32[512,128]{1,0:T(8,128)S(1)}, f32[32,8,128]{2,1,0:T(8,128)S(1)}) custom-call(f32[32,4,128]{2,1,0:T(4,128)S(1)} %all_to_all.22.refs_0_, f32[8,24,128]{2,1,0:T(8,128)S(1)} %all_to_all.20.refs_0_.refs_1_, bf16[4096,128]{1,0:T(8,128)(2,1)S(1)} %get-tuple-element.21.refs_2_, s32[32,128]{1,0:T(8,128)S(1)} %get-tuple-element.15.refs_1_.refs_3_, ...), custom_call_target="tpu_custom_call" | custom-call | tf_op jit(solution)/shard_map/pallas_call | solution.py:427
  37.3 9.9 %all_to_all.23.arrived_ref = f32[32,8,128]{2,1,0:T(8,128)S(1)} all-to-all(f32[32,8,128]{2,1,0:T(8,128)S(1)} %get-tuple-element.24), channel_id=1, replica_groups=mesh['region'=8,'rep'=4] {'region','rep'}, dimensions={0} | all-to-all | bytes 262144 | tf_op jit(solution)/shard_map/all_to_all | solution.py:430
  47.2 0.3 shard_map.82
  47.5 0.3 collective-permute-start
  47.8 0.7 %shard_map.81 = f32[512,128]{1,0:T(8,128)} custom-call(f32[512,128]{1,0:T(8,128)S(1)} %get-tuple-element.23.fresh_ref), custom_call_target="tpu_custom_call" | custom-call | tf_op jit(solution)/shard_map/pallas_call | solution.py:433
  48.5 0.3 collective-permute-done
  48.8 0.6 %add_bitcast_fusion = f32[8192]{0:T(1024)} fusion(f32[64,128]{1,0:T(8,128)S(1)} %shard_map.82, f32[64,128]{1,0:T(8,128)S(1)} %collective-permute-done), kind=kLoop, calls=%fused_computation | loop fusion | flops 8192 | bytes 98304 | tf_op jit(solution)/shard_map/reshape | solution.py:435
Async XLA Ops:
  47.5 1.3 %collective-permute-start = (f32[64,128]{1,0:T(8,128)S(1)}, f32[64,128]{1,0:T(8,128)S(1)}, u32[]{:S(2)}, u32[]{:S(2)}) collective-permute-start(f32[64,128]{1,0:T(8,128)S(1)} %shard_map.82), channel_id=1, source_target_pairs={{0,1},{1,0},{2,3},{3,2},{4,5},{5,4},{6,7},{7,6},{8,9},{9,8},{10,11... | collective-permute-start | bytes 98312 | tf_op jit(solution)/shard_map/ppermute | solution.py:432

commit v9 on v8

--- a/solution.py
+++ b/solution.py
@@ -172,7 +172,7 @@
 
     def price(d, o):
         if last:
-            return prices_ref[d * rep + o // quarter, o % quarter : o % quarter + 1, :]
+            return prices_ref[o // quarter * regions + d, o % quarter : o % quarter + 1, :]
         return prices_ref[d, o : o + 1, :]
 
     def operands(c):
@@ -218,7 +218,7 @@
                 block = DUAL_STEP * block + held * jnp.concatenate([share] * halves, axis=0)
             for k in range(rep):
                 first = k * sent % options
-                sums_ref[d * rep + k] = block[first : first + sent, :]
+                sums_ref[k * regions + d] = block[first : first + sent, :]
 
     for g in range(groups):
         slot = slot_ref[g * SUBLANES : (g + 1) * SUBLANES, :]
@@ -283,9 +283,9 @@
         sums, hots, numbers = [], [], []
         for i in range(CHUNK):
             r = chunk * CHUNK + i
-            x = arrived_ref[r * rep]
+            x = arrived_ref[r]
             for k in range(1, rep):
-                x = x + arrived_ref[r * rep + k]
+                x = x + arrived_ref[k * regions + r]
             sums.append(jnp.concatenate([x] * copies, axis=0))
             block, lane = group_place(lists_ref[pl.ds(r, 1), :])
             hots.append(one_hot(lane, LANES))
@@ -318,7 +318,7 @@
         for b in range(1, BLOCKS):
             found = jnp.where(block == b, jnp.take_along_axis(blocks[b], lane, axis=1), found)
         for k in range(rep):
-            picked_ref[r * rep + k] = found
+            picked_ref[k * regions + r] = found
         return carry
 
     each_region(regions, one)
@@ -388,7 +388,7 @@
     base_rows = array(2, BLOCKS, half, LANES)
     quarters = array(regions * rep, quarter, LANES)
     half_rows = array(regions * rep, half, LANES)
-    both = ("region", "rep")
+    both = ("rep", "region")
     exchange = functools.partial(lax.all_to_all, split_axis=0, concat_axis=0, tiled=True)
 
     picked, shift, base, lists, slots, cost, primal = call(

time: 49.7 us -> 48.9 us (0.984)
  blocking collectives: 42.7 us -> 42 us
    all_to_all x2, blocking collectives: 19.4 us -> 18.8 us  [local(): arrived = exchange(sums, both)]
where the time goes in v9:
time: 48.9 us; the launch traced here: 48.7 us
  blocking collectives  42 us (86%)
  Pallas kernels  4.87 us (10%)
  between operations  0.67 us (1%)
  other arithmetic  0.62 us (1%)
    all_to_all x2, blocking collectives, local(): arrived = exchange(sums, both)  18.8 us
    all_to_all x1, blocking collectives, local(): first_prices = exchange(picked, 'region')  14.2 us
    all_to_all x1, blocking collectives, local(): prices = exchange(picked, both)  8.97 us
    pallas_call x1, Pallas kernels, local(): call(functools.partial(first_kernel, options), (array(regions, options +...  1.25 us
    pallas_call x1, Pallas kernels, local(): call(functools.partial(person_kernel, options, rep, False), (tiles, quart...  1.22 us
    pallas_call x1, Pallas kernels, local(): call(functools.partial(person_kernel, options, rep, True), (tiles, half_r...  1.01 us
  transfers between devices with their start and end apart: 1, of which 1 were waited for; matrix products, arithmetic and copies ran while one was open for 0% of the time, Pallas kernels for 1%

profile of v9, /device:TPU:0, one launch (start us, length us, event | category | flops | bytes accessed | tf_op | source)
XLA Modules:
  0.0 48.7 jit_solution(2567506508260692)
XLA Ops:
  0.6 1.2 %shard_map.77 = (f32[8,24,128]{2,1,0:T(8,128)S(1)}, f32[4,16,128]{2,1,0:T(8,128)S(1)}, f32[2,4,8,128]{3,2,1,0:T(8,128)S(1)}, s32[8,128]{1,0:T(8,128)S(1)}, s32[3...) custom-call(s32[8,128]{1,0:T(8,128)} %bitcast.27, f32[64,128]{1,0:T(8,128)} %bitcast.24, ...), custom_call_target="tpu_custom_call" | custom-call | tf_op jit(solution)/shard_map/pallas_call | solution.py:394
  1.9 14.2 %all_to_all.20.refs_0_.refs_1_ = f32[8,24,128]{2,1,0:T(8,128)S(1)} all-to-all(f32[8,24,128]{2,1,0:T(8,128)S(1)} %get-tuple-element.14), channel_id=1, replica_groups=mesh['region'=8,'rep'=4] {'region'}, dimensions={0} | all-to-all | bytes 196608 | tf_op jit(solution)/shard_map/all_to_all | solution.py:415
  16.1 1.2 %shard_map.78 = (f32[512,128]{1,0:T(8,128)S(1)}, f32[32,4,128]{2,1,0:T(4,128)S(1)}, bf16[4096,128]{1,0:T(8,128)(2,1)S(1)}) custom-call(f32[8,24,128]{2,1,0:T(8,128)S(1)} %all_to_all.20.refs_0_.refs_1_, s32[32,128]{1,0:T(8,128)S(1)} %get-tuple-element.15.refs_1_.refs_3_, f32[512,128]{1,0:T(8,128)S(1)} %get-tuple-element.16.refs_2_.refs_4_, ...), custom_call_target="tpu_custom_call" | custom-call | tf_op jit(solution)/shard_map/pallas_call | solution.py:421
  17.3 9.3 %all_to_all.21.arrived_ref = f32[32,4,128]{2,1,0:T(4,128)S(1)} all-to-all(f32[32,4,128]{2,1,0:T(4,128)S(1)} %get-tuple-element.18), channel_id=1, replica_groups=mesh['region'=8,'rep'=4] {'rep','region'}, dimensions={0} | all-to-all | bytes 131072 | tf_op jit(solution)/shard_map/all_to_all | solution.py:424
  26.7 0.3 shard_map.79
  27.0 9.0 %all_to_all.22.refs_0_ = f32[32,4,128]{2,1,0:T(4,128)S(1)} all-to-all(f32[32,4,128]{2,1,0:T(4,128)S(1)} %shard_map.79), channel_id=1, replica_groups=mesh['region'=8,'rep'=4] {'rep','region'}, dimensions={0} | all-to-all | bytes 131072 | tf_op jit(solution)/shard_map/all_to_all | solution.py:426
  36.0 1.0 %shard_map.80 = (f32[512,128]{1,0:T(8,128)S(1)}, f32[32,8,128]{2,1,0:T(8,128)S(1)}) custom-call(f32[32,4,128]{2,1,0:T(4,128)S(1)} %all_to_all.22.refs_0_, f32[8,24,128]{2,1,0:T(8,128)S(1)} %all_to_all.20.refs_0_.refs_1_, bf16[4096,128]{1,0:T(8,128)(2,1)S(1)} %get-tuple-element.21.refs_2_, s32[32,128]{1,0:T(8,128)S(1)} %get-tuple-element.15.refs_1_.refs_3_, ...), custom_call_target="tpu_custom_call" | custom-call | tf_op jit(solution)/shard_map/pallas_call | solution.py:427
  37.0 9.4 %all_to_all.23.arrived_ref = f32[32,8,128]{2,1,0:T(8,128)S(1)} all-to-all(f32[32,8,128]{2,1,0:T(8,128)S(1)} %get-tuple-element.24), channel_id=1, replica_groups=mesh['region'=8,'rep'=4] {'rep','region'}, dimensions={0} | all-to-all | bytes 262144 | tf_op jit(solution)/shard_map/all_to_all | solution.py:430
  46.4 0.3 shard_map.82
  46.8 0.2 collective-permute-start
  46.9 0.7 %shard_map.81 = f32[512,128]{1,0:T(8,128)} custom-call(f32[512,128]{1,0:T(8,128)S(1)} %get-tuple-element.23.fresh_ref), custom_call_target="tpu_custom_call" | custom-call | tf_op jit(solution)/shard_map/pallas_call | solution.py:433
  47.7 0.4 collective-permute-done
  48.0 0.6 %add_bitcast_fusion = f32[8192]{0:T(1024)} fusion(f32[64,128]{1,0:T(8,128)S(1)} %shard_map.82, f32[64,128]{1,0:T(8,128)S(1)} %collective-permute-done), kind=kLoop, calls=%fused_computation | loop fusion | flops 8192 | bytes 98304 | tf_op jit(solution)/shard_map/reshape | solution.py:435
Async XLA Ops:
  46.8 1.3 %collective-permute-start = (f32[64,128]{1,0:T(8,128)S(1)}, f32[64,128]{1,0:T(8,128)S(1)}, u32[]{:S(2)}, u32[]{:S(2)}) collective-permute-start(f32[64,128]{1,0:T(8,128)S(1)} %shard_map.82), channel_id=1, source_target_pairs={{0,1},{1,0},{2,3},{3,2},{4,5},{5,4},{6,7},{7,6},{8,9},{9,8},{10,11... | collective-permute-start | bytes 98312 | tf_op jit(solution)/shard_map/ppermute | solution.py:432

commit v10 on v9

--- a/solution.py
+++ b/solution.py
@@ -98,8 +98,8 @@
 
 
 def first_kernel(options, *refs):
-    far, outs, (dual_ref, quota_ref, sems) = refs[:6], refs[6:13], refs[13:]
-    picked_ref, shift_ref, base_ref, lists_ref, slot_ref, cost_ref, primal_ref = outs
+    far, outs, (dual_ref, quota_ref, sems) = refs[:6], refs[6:14], refs[14:]
+    picked_ref, shift_ref, base_ref, lists_ref, slot_ref, cost_ref, primal_ref, turned_ref = outs
     targets = (lists_ref, dual_ref, quota_ref, slot_ref, cost_ref, primal_ref)
     copies = [
         pltpu.make_async_copy(source, target, sems.at[i]) for i, (source, target) in enumerate(zip(far, targets))
@@ -119,7 +119,7 @@
             rights.append(one_hot(lane, LANES))
         return total + product(jnp.concatenate(lefts, axis=1), jnp.concatenate(rights, axis=1))
 
-    for copy in copies[:3]:
+    for copy in copies[:4]:
         copy.wait()
     counts = repeat_chunks(regions // CHUNK, count_up, jnp.zeros((SUBLANES, LANES), jnp.float32))
     shares = 1.0 / jnp.maximum(counts, 1.0)
@@ -151,7 +151,10 @@
         base = jnp.where(named, 0.0, alone) - pull
         for h in range(base_ref.shape[0]):
             base_ref[h, b] = base[h * base_ref.shape[2] : (h + 1) * base_ref.shape[2], :]
-    for copy in copies[3:]:
+    for c in range(slot_ref.shape[0]):
+        within = jnp.broadcast_to((slot_ref[c : c + 1, :] & (WIDE - 1)).astype(jnp.float32), (LANES, LANES))
+        turned_ref[c * LANES : (c + 1) * LANES, :] = within.astype(jnp.bfloat16).T
+    for copy in copies[4:]:
         copy.wait()
 
 
@@ -160,7 +163,7 @@
         prices_ref, share_ref, turned_ref, slot_ref, cost_ref, primal_ref, fresh_ref, sums_ref, *kept_refs = refs
         regions = share_ref.shape[0]
     else:
-        prices_ref, slot_ref, cost_ref, primal_ref, fresh_ref, sums_ref, turned_ref, *kept_refs = refs
+        prices_ref, turned_ref, slot_ref, cost_ref, primal_ref, fresh_ref, sums_ref, *kept_refs = refs
         regions = prices_ref.shape[0]
     quarter = options // rep
     rows = slot_ref.shape[0]
@@ -181,12 +184,7 @@
         high, low = split_two(x)
         span = slice(c * LANES, (c + 1) * LANES)
         line = slot_ref[c : c + 1, :]
-        if last:
-            turned = turned_ref[span, :]
-        else:
-            within = jnp.broadcast_to((line & (WIDE - 1)).astype(jnp.float32), (LANES, LANES))
-            turned = within.astype(jnp.bfloat16).T
-            turned_ref[span, :] = turned
+        turned = turned_ref[span, :]
         turned = jnp.concatenate([turned] * (WIDE // LANES), axis=1)
         here = lax.broadcasted_iota(jnp.int32, (PACKED, WIDE), 1).astype(jnp.float32).astype(jnp.bfloat16)
         hot = [
@@ -391,7 +389,7 @@
     both = ("rep", "region")
     exchange = functools.partial(lax.all_to_all, split_axis=0, concat_axis=0, tiled=True)
 
-    picked, shift, base, lists, slots, cost, primal = call(
+    picked, shift, base, lists, slots, cost, primal, turned = call(
         functools.partial(first_kernel, options),
         (
             array(regions, options + SUBLANES, LANES),
@@ -401,6 +399,7 @@
             array(rows, LANES, kind=jnp.int32),
             tiles,
             tiles,
+            array(persons, LANES, kind=jnp.bfloat16),
         ),
         (pltpu.VMEM(flat, jnp.float32), pltpu.VMEM(flat, jnp.float32), pltpu.SemaphoreType.DMA((6,))),
         (True,) * 6,
@@ -417,10 +416,9 @@
     if regions > CHUNK:
         kept = ((options, persons), (options, persons), (PACKED, persons), (persons, WIDE))
         scratch = tuple(pltpu.VMEM(shape, jnp.bfloat16) for shape in kept)
-    turned = array(persons, LANES, kind=jnp.bfloat16)
-    primal, sums, turned = call(
-        functools.partial(person_kernel, options, rep, False), (tiles, quarters, turned), scratch
-    )(first_prices, slots, cost, primal)
+    primal, sums = call(functools.partial(person_kernel, options, rep, False), (tiles, quarters), scratch)(
+        first_prices, turned, slots, cost, primal
+    )
     arrived = exchange(sums, both)
     (picked,) = call(middle_kernel, (quarters,))(arrived, lists, shift)
     prices = exchange(picked, both)

time: 48.9 us -> 48.8 us (level)
  no operation moved by 1% of the time
where the time goes in v10:
time: 48.8 us; the launch traced here: 48.6 us
  blocking collectives  42 us (86%)
  Pallas kernels  4.81 us (10%)
  between operations  0.67 us (1%)
  other arithmetic  0.62 us (1%)
    all_to_all x2, blocking collectives, local(): arrived = exchange(sums, both)  18.8 us
    all_to_all x1, blocking collectives, local(): first_prices = exchange(picked, 'region')  14.2 us
    all_to_all x1, blocking collectives, local(): prices = exchange(picked, both)  8.97 us
    pallas_call x1, Pallas kernels, local(): call(functools.partial(first_kernel, options), (array(regions, options +...  1.37 us
    pallas_call x1, Pallas kernels, local(): call(functools.partial(person_kernel, options, rep, False), (tiles, quart...  1.04 us
    pallas_call x1, Pallas kernels, local(): call(functools.partial(person_kernel, options, rep, True), (tiles, half_r...  1.01 us
  transfers between devices with their start and end apart: 1, of which 1 were waited for; matrix products, arithmetic and copies ran while one was open for 0% of the time, Pallas kernels for 1%

profile of v10, /device:TPU:0, one launch (start us, length us, event | category | flops | bytes accessed | tf_op | source)
XLA Modules:
  0.0 48.6 jit_solution(3202323881140685089)
XLA Ops:
  0.6 1.4 %shard_map.77 = (f32[8,24,128]{2,1,0:T(8,128)S(1)}, f32[4,16,128]{2,1,0:T(8,128)S(1)}, f32[2,4,8,128]{3,2,1,0:T(8,128)S(1)}, s32[8,128]{1,0:T(8,128)S(1)}, s32[3...) custom-call(s32[8,128]{1,0:T(8,128)} %bitcast.27, ...), custom_call_target="tpu_custom_call" | custom-call | tf_op jit(solution)/shard_map/pallas_call | solution.py:392
  2.0 14.2 %all_to_all.20.refs_0_.refs_1_ = f32[8,24,128]{2,1,0:T(8,128)S(1)} all-to-all(f32[8,24,128]{2,1,0:T(8,128)S(1)} %get-tuple-element.14), channel_id=1, replica_groups=mesh['region'=8,'rep'=4] {'region'}, dimensions={0} | all-to-all | bytes 196608 | tf_op jit(solution)/shard_map/all_to_all | solution.py:414
  16.2 1.0 %shard_map.78 = (f32[512,128]{1,0:T(8,128)S(1)}, f32[32,4,128]{2,1,0:T(4,128)S(1)}) custom-call(f32[8,24,128]{2,1,0:T(8,128)S(1)} %all_to_all.20.refs_0_.refs_1_, bf16[4096,128]{1,0:T(8,128)(2,1)S(1)} %get-tuple-element.15.refs_1_.refs_2_, s32[32,128]{1,0:T(8,128)S(1)} %get-tuple-element.16.refs_2_.refs_3_, ...), custom_call_target="tpu_custom_call" | custom-call | tf_op jit(solution)/shard_map/pallas_call | solution.py:419
  17.3 9.3 %all_to_all.21.arrived_ref = f32[32,4,128]{2,1,0:T(4,128)S(1)} all-to-all(f32[32,4,128]{2,1,0:T(4,128)S(1)} %get-tuple-element.19), channel_id=1, replica_groups=mesh['region'=8,'rep'=4] {'rep','region'}, dimensions={0} | all-to-all | bytes 131072 | tf_op jit(solution)/shard_map/all_to_all | solution.py:422
  26.6 0.3 shard_map.79
  26.9 9.0 %all_to_all.22.refs_0_ = f32[32,4,128]{2,1,0:T(4,128)S(1)} all-to-all(f32[32,4,128]{2,1,0:T(4,128)S(1)} %shard_map.79), channel_id=1, replica_groups=mesh['region'=8,'rep'=4] {'rep','region'}, dimensions={0} | all-to-all | bytes 131072 | tf_op jit(solution)/shard_map/all_to_all | solution.py:424
  35.9 1.0 %shard_map.80 = (f32[512,128]{1,0:T(8,128)S(1)}, f32[32,8,128]{2,1,0:T(8,128)S(1)}) custom-call(f32[32,4,128]{2,1,0:T(4,128)S(1)} %all_to_all.22.refs_0_, f32[8,24,128]{2,1,0:T(8,128)S(1)} %all_to_all.20.refs_0_.refs_1_, bf16[4096,128]{1,0:T(8,128)(2,1)S(1)} %get-tuple-element.15.refs_1_.refs_2_, s32[32,128]{1,0:T(8,128)S(1)} %get-tuple-element.16.refs_2_.refs_3_, ...), custom_call_target="tpu_custom_call" | custom-call | tf_op jit(solution)/shard_map/pallas_call | solution.py:425
  36.9 9.4 %all_to_all.23.arrived_ref = f32[32,8,128]{2,1,0:T(8,128)S(1)} all-to-all(f32[32,8,128]{2,1,0:T(8,128)S(1)} %get-tuple-element.24), channel_id=1, replica_groups=mesh['region'=8,'rep'=4] {'rep','region'}, dimensions={0} | all-to-all | bytes 262144 | tf_op jit(solution)/shard_map/all_to_all | solution.py:428
  46.4 0.3 shard_map.82
  46.7 0.2 collective-permute-start
  46.9 0.7 %shard_map.81 = f32[512,128]{1,0:T(8,128)} custom-call(f32[512,128]{1,0:T(8,128)S(1)} %get-tuple-element.23.fresh_ref), custom_call_target="tpu_custom_call" | custom-call | tf_op jit(solution)/shard_map/pallas_call | solution.py:431
  47.6 0.4 collective-permute-done
  48.0 0.6 %add_bitcast_fusion = f32[8192]{0:T(1024)} fusion(f32[64,128]{1,0:T(8,128)S(1)} %shard_map.82, f32[64,128]{1,0:T(8,128)S(1)} %collective-permute-done), kind=kLoop, calls=%fused_computation | loop fusion | flops 8192 | bytes 98304 | tf_op jit(solution)/shard_map/reshape | solution.py:433
Async XLA Ops:
  46.7 1.3 %collective-permute-start = (f32[64,128]{1,0:T(8,128)S(1)}, f32[64,128]{1,0:T(8,128)S(1)}, u32[]{:S(2)}, u32[]{:S(2)}) collective-permute-start(f32[64,128]{1,0:T(8,128)S(1)} %shard_map.82), channel_id=1, source_target_pairs={{0,1},{1,0},{2,3},{3,2},{4,5},{5,4},{6,7},{7,6},{8,9},{9,8},{10,11... | collective-permute-start | bytes 98312 | tf_op jit(solution)/shard_map/ppermute | solution.py:430

commit v11 on v10

--- a/solution.py
+++ b/solution.py
@@ -98,8 +98,8 @@
 
 
 def first_kernel(options, *refs):
-    far, outs, (dual_ref, quota_ref, sems) = refs[:6], refs[6:14], refs[14:]
-    picked_ref, shift_ref, base_ref, lists_ref, slot_ref, cost_ref, primal_ref, turned_ref = outs
+    far, outs, (dual_ref, quota_ref, sems) = refs[:6], refs[6:15], refs[15:]
+    picked_ref, shift_ref, base_ref, lists_ref, slot_ref, cost_ref, primal_ref, turned_ref, lanes_ref = outs
     targets = (lists_ref, dual_ref, quota_ref, slot_ref, cost_ref, primal_ref)
     copies = [
         pltpu.make_async_copy(source, target, sems.at[i]) for i, (source, target) in enumerate(zip(far, targets))
@@ -136,6 +136,7 @@
         share = jnp.take_along_axis(shares, wide_lane[:SUBLANES], axis=1)
         share = jnp.sum(jnp.where(block == which, share, 0.0), axis=0, keepdims=True)
         picked_ref[r, options : options + SUBLANES, :] = jnp.broadcast_to(share, (SUBLANES, LANES))
+        lanes_ref[r] = jnp.broadcast_to(lane.astype(jnp.float32), (LANES, LANES)).astype(jnp.bfloat16).T
         return carry
 
     each_region(regions, one)
@@ -268,7 +269,7 @@
         lax.fori_loop(0, chunks, add_up, 0)
 
 
-def block_sums(arrived_ref, lists_ref):
+def block_sums(arrived_ref, lists_ref, lanes_ref):
     regions = lists_ref.shape[0]
     rep = arrived_ref.shape[0] // regions
     options = arrived_ref.shape[1]
@@ -276,6 +277,8 @@
     copies = max(1, SUBLANES // options)
     tall = copies * options
     row = lax.broadcasted_iota(jnp.int32, (tall, CHUNK * LANES), 0) // options
+
+    here = lax.broadcasted_iota(jnp.int32, (PACKED, LANES), 1).astype(jnp.float32).astype(jnp.bfloat16)
 
     def add_up(chunk, total):
         sums, hots, numbers = [], [], []
@@ -285,8 +288,11 @@
             for k in range(1, rep):
                 x = x + arrived_ref[k * regions + r]
             sums.append(jnp.concatenate([x] * copies, axis=0))
-            block, lane = group_place(lists_ref[pl.ds(r, 1), :])
-            hots.append(one_hot(lane, LANES))
+            block, _ = group_place(lists_ref[pl.ds(r, 1), :])
+            turned = lanes_ref[r]
+            for first in range(0, LANES, PACKED):
+                hit = turned[first : first + PACKED] == here
+                hots.append(jnp.where(hit, jnp.bfloat16(1), jnp.bfloat16(0)))
             numbers.append(jnp.broadcast_to(block, (tall, LANES)))
         x = jnp.concatenate(sums, axis=1)
         number = jnp.concatenate(numbers, axis=1) - row
@@ -294,17 +300,18 @@
         left = [
             jnp.where(number == first, part, 0.0) for part in (high, x - high) for first in range(0, BLOCKS, copies)
         ]
-        found = product(jnp.concatenate(left, axis=0).astype(jnp.bfloat16), jnp.concatenate(hots, axis=1))
+        left = jnp.concatenate(left, axis=0).astype(jnp.bfloat16)
+        found = jnp.dot(left, jnp.concatenate(hots, axis=0), preferred_element_type=jnp.float32)
         return total + found[:lines] + found[lines:]
 
     return repeat_chunks(regions // CHUNK, add_up, jnp.zeros((lines, LANES), jnp.float32))
 
 
-def middle_kernel(arrived_ref, lists_ref, shift_ref, picked_ref):
+def middle_kernel(arrived_ref, lists_ref, lanes_ref, shift_ref, picked_ref):
     regions = lists_ref.shape[0]
     rep = arrived_ref.shape[0] // regions
     options = arrived_ref.shape[1]
-    applied = block_sums(arrived_ref, lists_ref)
+    applied = block_sums(arrived_ref, lists_ref, lanes_ref)
     dual = jnp.maximum(shift_ref[lax.axis_index("rep")] + DUAL_STEP * applied, 0.0)
     blocks = [dual[b * options : (b + 1) * options, :] for b in range(BLOCKS)]
 
@@ -322,11 +329,11 @@
     each_region(regions, one)
 
 
-def half_kernel(arrived_ref, lists_ref, base_ref, part_ref):
+def half_kernel(arrived_ref, lists_ref, lanes_ref, base_ref, part_ref):
     sent = arrived_ref.shape[1]
     shares = base_ref.shape[0]
     mine = lax.axis_index("rep") % shares
-    sums = block_sums(arrived_ref, lists_ref)
+    sums = block_sums(arrived_ref, lists_ref, lanes_ref)
     lines = []
     for b in range(BLOCKS):
         block = jnp.maximum(base_ref[mine, b] + sums[b * sent : (b + 1) * sent, :], 0.0)
@@ -389,7 +396,7 @@
     both = ("rep", "region")
     exchange = functools.partial(lax.all_to_all, split_axis=0, concat_axis=0, tiled=True)
 
-    picked, shift, base, lists, slots, cost, primal, turned = call(
+    picked, shift, base, lists, slots, cost, primal, turned, lanes = call(
         functools.partial(first_kernel, options),
         (
             array(regions, options + SUBLANES, LANES),
@@ -400,6 +407,7 @@
             tiles,
             tiles,
             array(persons, LANES, kind=jnp.bfloat16),
+            array(regions, LANES, LANES, kind=jnp.bfloat16),
         ),
         (pltpu.VMEM(flat, jnp.float32), pltpu.VMEM(flat, jnp.float32), pltpu.SemaphoreType.DMA((6,))),
         (True,) * 6,
@@ -420,13 +428,13 @@
         first_prices, turned, slots, cost, primal
     )
     arrived = exchange(sums, both)
-    (picked,) = call(middle_kernel, (quarters,))(arrived, lists, shift)
+    (picked,) = call(middle_kernel, (quarters,))(arrived, lists, lanes, shift)
     prices = exchange(picked, both)
     primal, sums = call(functools.partial(person_kernel, options, rep, True), (tiles, half_rows), scratch)(
         prices, first_prices, turned, slots, cost, primal
     )
     arrived = exchange(sums, both)
-    (part,) = call(half_kernel, (array(*flat),))(arrived, lists, base)
+    (part,) = call(half_kernel, (array(*flat),))(arrived, lists, lanes, base)
     other = lax.ppermute(part, "rep", [(k, k ^ 1) for k in range(rep)])
     (primal,) = call(write_kernel, (array(*tiles[0], far=True),), (pltpu.SemaphoreType.DMA,))(primal)
     dual = part + other

time: 48.8 us -> 48.9 us (level)
  no operation moved by 1% of the time
where the time goes in v11:
time: 48.9 us; the launch traced here: 48.6 us
  blocking collectives  42 us (86%)
  Pallas kernels  4.85 us (10%)
  between operations  0.67 us (1%)
  other arithmetic  0.62 us (1%)
    all_to_all x2, blocking collectives, local(): arrived = exchange(sums, both)  18.8 us
    all_to_all x1, blocking collectives, local(): first_prices = exchange(picked, 'region')  14.2 us
    all_to_all x1, blocking collectives, local(): prices = exchange(picked, both)  8.97 us
    pallas_call x1, Pallas kernels, local(): call(functools.partial(first_kernel, options), (array(regions, options +...  1.46 us
    pallas_call x1, Pallas kernels, local(): call(functools.partial(person_kernel, options, rep, False), (tiles, quart...  1.02 us
    pallas_call x1, Pallas kernels, local(): call(functools.partial(person_kernel, options, rep, True), (tiles, half_r...  1.01 us
  transfers between devices with their start and end apart: 1, of which 1 were waited for; matrix products, arithmetic and copies ran while one was open for 0% of the time, Pallas kernels for 1%

profile of v11, /device:TPU:0, one launch (start us, length us, event | category | flops | bytes accessed | tf_op | source)
XLA Modules:
  0.0 48.6 jit_solution(3180740682754371092)
XLA Ops:
  0.6 1.5 %shard_map.77 = (f32[8,24,128]{2,1,0:T(8,128)S(1)}, f32[4,16,128]{2,1,0:T(8,128)S(1)}, f32[2,4,8,128]{3,2,1,0:T(8,128)S(1)}, s32[8,128]{1,0:T(8,128)S(1)}, s32[3...) custom-call(s32[8,128]{1,0:T(8,128)} %bitcast.27, ...), custom_call_target="tpu_custom_call" | custom-call | tf_op jit(solution)/shard_map/pallas_call | solution.py:399
  2.1 14.2 %all_to_all.20.refs_0_.refs_1_ = f32[8,24,128]{2,1,0:T(8,128)S(1)} all-to-all(f32[8,24,128]{2,1,0:T(8,128)S(1)} %get-tuple-element.15), channel_id=1, replica_groups=mesh['region'=8,'rep'=4] {'region'}, dimensions={0} | all-to-all | bytes 196608 | tf_op jit(solution)/shard_map/all_to_all | solution.py:422
  16.3 1.0 %shard_map.78 = (f32[512,128]{1,0:T(8,128)S(1)}, f32[32,4,128]{2,1,0:T(4,128)S(1)}) custom-call(f32[8,24,128]{2,1,0:T(8,128)S(1)} %all_to_all.20.refs_0_.refs_1_, bf16[4096,128]{1,0:T(8,128)(2,1)S(1)} %get-tuple-element.16.refs_1_.refs_2_, s32[32,128]{1,0:T(8,128)S(1)} %get-tuple-element.17.refs_2_.refs_3_, ...), custom_call_target="tpu_custom_call" | custom-call | tf_op jit(solution)/shard_map/pallas_call | solution.py:427
  17.3 9.3 %all_to_all.21.arrived_ref = f32[32,4,128]{2,1,0:T(4,128)S(1)} all-to-all(f32[32,4,128]{2,1,0:T(4,128)S(1)} %get-tuple-element.20), channel_id=1, replica_groups=mesh['region'=8,'rep'=4] {'rep','region'}, dimensions={0} | all-to-all | bytes 131072 | tf_op jit(solution)/shard_map/all_to_all | solution.py:430
  26.7 0.3 shard_map.79
  27.0 9.0 %all_to_all.22.refs_0_ = f32[32,4,128]{2,1,0:T(4,128)S(1)} all-to-all(f32[32,4,128]{2,1,0:T(4,128)S(1)} %shard_map.79), channel_id=1, replica_groups=mesh['region'=8,'rep'=4] {'rep','region'}, dimensions={0} | all-to-all | bytes 131072 | tf_op jit(solution)/shard_map/all_to_all | solution.py:432
  36.0 1.0 %shard_map.80 = (f32[512,128]{1,0:T(8,128)S(1)}, f32[32,8,128]{2,1,0:T(8,128)S(1)}) custom-call(f32[32,4,128]{2,1,0:T(4,128)S(1)} %all_to_all.22.refs_0_, f32[8,24,128]{2,1,0:T(8,128)S(1)} %all_to_all.20.refs_0_.refs_1_, bf16[4096,128]{1,0:T(8,128)(2,1)S(1)} %get-tuple-element.16.refs_1_.refs_2_, s32[32,128]{1,0:T(8,128)S(1)} %get-tuple-element.17.refs_2_.refs_3_, ...), custom_call_target="tpu_custom_call" | custom-call | tf_op jit(solution)/shard_map/pallas_call | solution.py:433
  37.0 9.4 %all_to_all.23.arrived_ref = f32[32,8,128]{2,1,0:T(8,128)S(1)} all-to-all(f32[32,8,128]{2,1,0:T(8,128)S(1)} %get-tuple-element.26), channel_id=1, replica_groups=mesh['region'=8,'rep'=4] {'rep','region'}, dimensions={0} | all-to-all | bytes 262144 | tf_op jit(solution)/shard_map/all_to_all | solution.py:436
  46.4 0.3 shard_map.82
  46.8 0.2 collective-permute-start
  46.9 0.7 %shard_map.81 = f32[512,128]{1,0:T(8,128)} custom-call(f32[512,128]{1,0:T(8,128)S(1)} %get-tuple-element.25.fresh_ref), custom_call_target="tpu_custom_call" | custom-call | tf_op jit(solution)/shard_map/pallas_call | solution.py:439
  47.6 0.4 collective-permute-done
  48.0 0.6 %add_bitcast_fusion = f32[8192]{0:T(1024)} fusion(f32[64,128]{1,0:T(8,128)S(1)} %shard_map.82, f32[64,128]{1,0:T(8,128)S(1)} %collective-permute-done), kind=kLoop, calls=%fused_computation | loop fusion | flops 8192 | bytes 98304 | tf_op jit(solution)/shard_map/reshape | solution.py:441
Async XLA Ops:
  46.8 1.3 %collective-permute-start = (f32[64,128]{1,0:T(8,128)S(1)}, f32[64,128]{1,0:T(8,128)S(1)}, u32[]{:S(2)}, u32[]{:S(2)}) collective-permute-start(f32[64,128]{1,0:T(8,128)S(1)} %shard_map.82), channel_id=1, source_target_pairs={{0,1},{1,0},{2,3},{3,2},{4,5},{5,4},{6,7},{7,6},{8,9},{9,8},{10,11... | collective-permute-start | bytes 98312 | tf_op jit(solution)/shard_map/ppermute | solution.py:438
